TPU v7x, 512 devices: a whole 4x4x16 slice. The times are simulated.
512 devices in a mesh: dp: 32 (over z, core), shard: 16 (over x, y).
Axes of the slice: x: 4, y: 4, z: 16, core: 2. Of those that a mesh axis runs over, the one named last changes fastest.
Arguments:
- grads: bfloat16 [32, 1024, 7168], P('dp', 'shard'), may hold values from -6 to 6
- errors: float32 [32, 1024, 7168], P('dp', 'shard'), may hold values from -4 to 4
- q_prev: float32 [7168, 32], P('shard'), may hold values from -6 to 6
Outputs:
- new_errors: float32 [32, 1024, 7168], P('dp', 'shard')
- q_new: float32 [7168, 32], P('shard')
All inputs are finite; a program needn't handle non-finite values.
Results may differ from a plain program's by a relative error of at most 0.0003.
Values sent between devices are 32-bit elements; how exact they have to be, the bound alone decides.
No kernel may reach another device: no remote copies, remote signals or barrier semaphores. Data moves between devices by JAX's collectives and lax.ppermute only.
A program may use at most 64 MiB of HBM per device.

v0:
```python
import jax
import jax.numpy as jnp
from jax import lax
from jax.sharding import PartitionSpec as P


def per_device(grads, errors, q_prev):
    high = lax.Precision.HIGHEST
    merged = grads.astype(jnp.float32) + errors
    matrix = merged[0]
    width = matrix.shape[1]
    replicas = lax.axis_size("dp")
    partial_left = jnp.dot(
        matrix, lax.all_gather(q_prev, "shard", axis=0, tiled=True), precision=high
    )
    left = lax.psum(partial_left, "dp") / replicas
    local_gram = jnp.dot(left.T, left, precision=high)
    gram = lax.psum(local_gram, "shard")
    lower = jnp.linalg.cholesky(gram)
    p_hat = jax.scipy.linalg.solve_triangular(lower, left.T, lower=True).T
    own_term = jnp.dot(matrix.T, p_hat, precision=high)
    right_full = lax.psum(own_term, ("dp", "shard")) / replicas
    share = width // lax.axis_size("shard")
    q_mine = lax.dynamic_slice_in_dim(right_full, lax.axis_index("shard") * share, share, 0)
    approx = jnp.dot(p_hat, right_full.T, precision=high)
    return (merged - approx[None], q_mine)


def solution(mesh):
    in_specs = (P("dp", "shard", None), P("dp", "shard", None), P("shard", None))
    out_specs = (P("dp", "shard", None), P("shard", None))
    return jax.shard_map(
        per_device, mesh=mesh, in_specs=in_specs, out_specs=out_specs, check_vma=False
    )
```

profile of v0, /device:TPU:1, one launch (start us, length us, event | category | flops | bytes accessed | tf_op | source)
XLA Modules:
  0.0 685.6 jit_solution(17529824092798190716)
XLA Ops:
  7.2 0.0 all-reduce.2.cloned.1.call-start
  7.2 21.1 %all-gather = f32[16,448,32]{1,2,0:T(8,128)S(1)} all-gather(f32[1,448,32]{1,2,0:T(8,128)} %bitcast.24), channel_id=1, replica_groups=mesh['dp'=32,'shard'=16] {'shard'}, dimensions={0}, use_global_device_ids=true | all-gather | bytes 974848 | tf_op jit(solution)/shard_map/all_gather | solution.py:14
  28.3 0.0 copy-start
  28.3 0.0 copy-start.1
  28.3 1.6 copy.10
  29.9 2.6 reshape.15
  32.5 0.0 copy-done
  32.5 0.0 copy-done.1
  32.5 2.8 fusion.3
  35.3 98.7 %psum.21 = f32[64,32]{0,1:T(8,128)S(1)} all-reduce(f32[64,32]{0,1:T(8,128)S(1)} %fusion.3), channel_id=1, replica_groups=mesh['dp'=32,'shard'=16] {'dp'}, use_global_device_ids=true, to_apply=%region_0.0 | all-reduce | flops 2048 | bytes 16384 | tf_op jit(solution)/shard_map/psum | solution.py:16
  134.0 0.1 fusion.10
  134.1 58.2 %psum.22 = f32[32,32]{0,1:T(8,128)S(1)} all-reduce(f32[32,32]{0,1:T(8,128)S(1)} %fusion.10), channel_id=1, replica_groups=mesh['dp'=32,'shard'=16] {'shard'}, use_global_device_ids=true, to_apply=%region_1.0 | all-reduce | flops 1024 | bytes 8192 | tf_op jit(solution)/shard_map/psum | solution.py:18
  192.3 0.1 copy.12
  192.4 2.9 cholesky.16
  195.3 0.6 compare_reduce_fusion
  196.0 0.7 fusion.5
  196.6 2.4 custom-call.7
  199.1 0.2 fusion.6
  199.3 2.2 fusion.1
  201.5 0.0 all-reduce.2.cloned.1.call-update
  201.5 472.2 %all-reduce.2.cloned.1.call-done = f32[7168,32]{0,1:T(8,128)} async-done(((f32[7168,32]{0,1:T(8,128)}), f32[7168,32]{0,1:T(8,128)}) %all-reduce.2.cloned.1.call-update) | async-done | bytes 917520 | tf_op jit(solution)/shard_map/psum | solution.py:22
  673.7 0.0 copy-start.2
  673.7 1.3 broadcast_multiply_fusion
  675.0 0.7 constant_dynamic-slice_fusion
  675.8 0.0 copy-done.2
  675.8 2.9 fusion
  (2 shorter events, 0.0 us)
Async XLA Ops:
  7.2 666.5 %all-reduce.2.cloned.1.call-start = ((), (), s32[]{:S(2)}) async-start(), calls=%async_computation | async-start | bytes 1835008 | tf_op jit(solution)/shard_map/psum | solution.py:22
  28.3 4.2 copy-start
  28.3 4.2 copy-start.1
  673.7 2.1 copy-start.2
Sparse Core Ops, SparseCore 0:
  201.7 472.0 all-reduce.1
where the time goes:
time: 686 us
  waiting for transfers between devices  472 us (69%)
  blocking collectives  178 us (26%)
  between operations  14.1 us (2%)
  matrix products  8.32 us (1%)
  other arithmetic  8.01 us (1%)
    psum x1, waiting for transfers between devices, per_device(): right_full = lax.psum(own_term, ('dp', 'shard')) / replicas  472 us
    psum x1, blocking collectives, per_device(): left = lax.psum(partial_left, 'dp') / replicas  98.7 us
    psum x1, blocking collectives, per_device(): gram = lax.psum(local_gram, 'shard')  58.2 us
    all_gather x1, blocking collectives, per_device(): lax.all_gather(q_prev, 'shard', axis=0, tiled=True)  21.1 us
  transfers between devices with their start and end apart: 1, of which 1 were waited for; matrix products, arithmetic and copies ran while one was open for 0% of the time, Pallas kernels for 0%

commit v1 on v0

v1 whole, which is shorter than its diff:
```python
import jax
import jax.numpy as jnp
from jax import lax
from jax.sharding import Mesh, PartitionSpec as P

HIGH = lax.Precision.HIGHEST
PLANE = ("x", "y")


def to_all(block, peers, axis):
    return lax.all_to_all(jnp.broadcast_to(block, (peers, *block.shape)), axis, 0, 0)


def per_device(grads, errors, q_prev):
    merged = grads[0].astype(jnp.float32) + errors[0]
    rows, width = merged.shape
    share, rank = q_prev.shape
    planes, chips = lax.axis_size("z"), lax.axis_size(PLANE)
    replicas = 2 * planes
    half = rank // 2
    core = lax.axis_index("core")
    here = lax.axis_index(PLANE)

    other = lax.ppermute(merged, "core", [(0, 1), (1, 0)])
    own_q = lax.dynamic_slice_in_dim(q_prev.T, core * half, half, 0)
    all_q = to_all(own_q, chips, PLANE)
    all_q = all_q.transpose(1, 0, 2).reshape(half, width)
    both = merged + other
    left = jnp.dot(all_q, both.T, precision=HIGH) / replicas
    left = to_all(left, planes, "z").sum(0)

    right = jnp.dot(left, both, precision=HIGH) / replicas
    right = right.reshape(half, chips, share).transpose(1, 0, 2)
    right = lax.all_to_all(right, PLANE, 0, 0).sum(0)
    right = to_all(right, planes, "z").sum(0)

    halves = to_all(jnp.concatenate([right, left], 1), chips, PLANE)
    pair = lax.ppermute(halves, "core", [(0, 1), (1, 0)])
    first, second = jnp.where(core == 0, halves, pair), jnp.where(core == 0, pair, halves)
    whole = jnp.stack([first, second])
    whole = whole.transpose(0, 2, 1, 3).reshape(rank, chips, share + rows)
    left_all = whole[:, :, share:].reshape(rank, chips * rows)
    right_all = whole[:, :, :share].reshape(rank, width)
    gram = jnp.dot(left_all, left_all.T, precision=HIGH)
    lower = jnp.linalg.cholesky(gram)
    own_left = lax.dynamic_slice_in_dim(left_all, here * rows, rows, 1)
    solved = jax.scipy.linalg.solve_triangular(
        lower, jnp.concatenate([right_all, own_left], 1), lower=True
    )
    q_new, p_hat = solved[:, :width], solved[:, width:]
    approx = jnp.dot(p_hat.T, q_new, precision=HIGH)
    q_mine = lax.dynamic_slice_in_dim(q_new, here * share, share, 1).T
    return ((merged - approx)[None], q_mine)


def solution(mesh):
    split = Mesh(mesh.devices.reshape(16, 2, 4, 4), ("z", "core", "x", "y"))
    dp = ("z", "core")
    in_specs = (P(dp, PLANE, None), P(dp, PLANE, None), P(PLANE, None))
    out_specs = (P(dp, PLANE, None), P(PLANE, None))
    return jax.shard_map(
        per_device, mesh=split, in_specs=in_specs, out_specs=out_specs, check_vma=False
    )
```

time: 686 us -> 138 us (0.20)
  waiting for transfers between devices: 472 us -> 1.51 us
  blocking collectives: 178 us -> 86 us
  starting transfers between devices: 0.04 us -> 21.3 us
  between operations: 14.1 us -> 0.86 us
    psum x1 -> x0, waiting for transfers between devices: 472 us -> none  [per_device(): right_full = lax.psum(own_term, ('dp', 'shard')) / replicas]
    psum x2 -> x0, blocking collectives: 157 us -> none  [the longest x1 98.7 us: per_device(): left = lax.psum(partial_left, 'dp') / replicas]
    all_to_all x0 -> x5, blocking collectives: none -> 86 us  [the longest x4 72.9 us: to_all(): lax.all_to_all(jnp.broadcast_to(block, (peers, *block.shape)), axis, 0, 0)]
    ppermute x0 -> x2, starting transfers between devices: none -> 21.3 us  [the longest x1 12.5 us: per_device(): pair = lax.ppermute(halves, 'core', [(0, 1), (1, 0)])]
    all_gather x1 -> x0, blocking collectives: 21.1 us -> none  [per_device(): lax.all_gather(q_prev, 'shard', axis=0, tiled=True)]
  transfers between devices with their start and end apart: 1 -> 2, of which waited for: 1 -> 1; matrix products, arithmetic and copies ran while one was open for 0% -> 0% of each run, Pallas kernels for 0% -> 0%
where the time goes in v1:
time: 138 us; the launch traced here: 137 us
  blocking collectives  86 us (62%)
  starting transfers between devices  21.3 us (15%)
  other arithmetic  11.5 us (8%)
  matrix products  8.27 us (6%)
  local copies, waits for them, and re-layouts  7.82 us (6%)
  waiting for transfers between devices  1.51 us (1%)
    all_to_all x4, blocking collectives, to_all(): lax.all_to_all(jnp.broadcast_to(block, (peers, *block.shape)), axis, 0, 0)  72.9 us
    all_to_all x1, blocking collectives, per_device(): right = lax.all_to_all(right, PLANE, 0, 0).sum(0)  13.1 us
    ppermute x1, starting transfers between devices, per_device(): pair = lax.ppermute(halves, 'core', [(0, 1), (1, 0)])  12.5 us
    ppermute x1, starting transfers between devices, per_device(): other = lax.ppermute(merged, 'core', [(0, 1), (1, 0)])  8.79 us
    another operation x3, other arithmetic, per_device(): lower = jnp.linalg.cholesky(gram)  3.6 us
    another operation x2, other arithmetic, per_device(): jax.scipy.linalg.solve_triangular(lower, jnp.concatenate([right_all, own_...  3.09 us
    dot_general x1, matrix products, per_device(): approx = jnp.dot(p_hat.T, q_new, precision=HIGH)  2.87 us
  transfers between devices with their start and end apart: 2, of which 1 were waited for; matrix products, arithmetic and copies ran while one was open for 0% of the time, Pallas kernels for 0%

profile of v1, /device:TPU:1, one launch (start us, length us, event | category | flops | bytes accessed | tf_op | source)
XLA Modules:
  0.0 137.2 jit_solution(8015145085548455496)
XLA Ops:
  0.6 0.0 copy-start
  0.6 1.9 %add_bitcast_fusion = f32[64,7168]{1,0:T(8,128)S(1)} fusion(f32[1,64,7168]{2,1,0:T(8,128)} %param.4, bf16[1,64,7168]{2,1,0:T(8,128)(2,1)} %param.3), kind=kLoop, calls=%fused_computation.3 | loop fusion | flops 917504 | bytes 4587520 | tf_op jit(solution)/shard_map/add | solution.py:15
  2.6 8.8 %collective-permute-start = (f32[64,7168]{1,0:T(8,128)S(1)}, f32[64,7168]{1,0:T(8,128)}, u32[]{:S(2)}, u32[]{:S(2)}) collective-permute-start(f32[64,7168]{1,0:T(8,128)S(1)} %add_bitcast_fusion), channel_id=1, source_target_pairs={{0,16},{16,0},{1,17},{17,1},{2,18},{18,2},{3,19},{19,3},{4,20},{20... | collective-permute-start | bytes 5505032 | tf_op jit(solution)/shard_map/ppermute | solution.py:24
  11.4 0.0 copy-done
  11.4 0.1 broadcast_in_dim.17
  11.5 13.6 %all_to_all.25 = f32[16,16,448]{2,1,0:T(8,128)S(1)} all-to-all(f32[16,16,448]{2,1,0:T(8,128)S(1)} %broadcast_in_dim.17), channel_id=1, replica_groups=mesh['z'=16,'core'=2,'x'=4,'y'=4] {'x','y'}, dimensions={0} | all-to-all | bytes 917504 | tf_op jit(solution)/shard_map/all_to_all | solution.py:11
  25.1 0.3 copy.17
  25.4 0.2 reshape.31
  25.6 0.0 collective-permute-done
  25.6 1.7 %add.36 = f32[64,7168]{1,0:T(8,128)S(1)} add(f32[64,7168]{1,0:T(8,128)S(1)} %add_bitcast_fusion, f32[64,7168]{1,0:T(8,128)} %collective-permute-done) | non-fusion elementwise | flops 458752 | bytes 5505024 | tf_op jit(solution)/shard_map/add | solution.py:28
  27.3 0.0 copy-start.1
  27.3 1.2 copy-done.1
  28.6 1.5 %convolution_multiply_fusion.1 = f32[16,64]{1,0:T(8,128)S(1)} fusion(f32[16,7168]{1,0:T(8,128)S(1)} %reshape.31, f32[64,7168]{1,0:T(8,128)S(1)} %add.36), kind=kOutput, calls=%fused_computation.5 | convolution fusion | flops 88081408 | bytes 2297856 | tf_op jit(solution)/shard_map/dot_general | solution.py:29
  30.1 0.1 reshape.37
  30.2 24.0 %all_to_all.26 = f32[16,1,1024]{2,1,0:T(1,128)S(1)} all-to-all(f32[16,1,1024]{2,1,0:T(1,128)S(1)} %reshape.37), channel_id=1, replica_groups=mesh['z'=16,'core'=2,'x'=4,'y'=4] {'z'}, dimensions={0} | all-to-all | bytes 131072 | tf_op jit(solution)/shard_map/all_to_all | solution.py:11
  54.2 0.5 broadcast.55
  54.7 0.8 reduce.6
  55.5 0.1 reshape.38
  55.6 2.5 %convolution_multiply_fusion = f32[16,7168]{1,0:T(8,128)S(1)} fusion(f32[16,64]{1,0:T(8,128)S(1)} %reduce_sum.27, f32[64,7168]{1,0:T(8,128)} %copy-done.1), kind=kOutput, calls=%fused_computation.2 | convolution fusion | flops 88195072 | bytes 2297856 | tf_op jit(solution)/shard_map/dot_general | solution.py:32
  58.1 0.3 reshape.32
  58.4 0.3 copy.24
  58.7 13.1 %all_to_all.27 = f32[16,16,448]{2,1,0:T(8,128)S(1)} all-to-all(f32[16,16,448]{2,1,0:T(8,128)S(1)} %bitcast.41), channel_id=1, replica_groups=mesh['z'=16,'core'=2,'x'=4,'y'=4] {'x','y'}, dimensions={0} | all-to-all | bytes 917504 | tf_op jit(solution)/shard_map/all_to_all | solution.py:34
  71.9 0.1 broadcast_in_dim.19
  71.9 23.4 %all_to_all.28 = f32[16,16,448]{2,1,0:T(8,128)S(1)} all-to-all(f32[16,16,448]{2,1,0:T(8,128)S(1)} %broadcast_in_dim.19), channel_id=1, replica_groups=mesh['z'=16,'core'=2,'x'=4,'y'=4] {'z'}, dimensions={0} | all-to-all | bytes 917504 | tf_op jit(solution)/shard_map/all_to_all | solution.py:11
  95.3 0.1 pad_maximum_fusion.1
  95.4 0.1 broadcast_in_dim.20
  95.5 11.9 %all_to_all.29 = f32[16,16,512]{2,1,0:T(8,128)S(1)} all-to-all(f32[16,16,512]{2,1,0:T(8,128)S(1)} %broadcast_in_dim.20), channel_id=1, replica_groups=mesh['z'=16,'core'=2,'x'=4,'y'=4] {'x','y'}, dimensions={0} | all-to-all | bytes 1048576 | tf_op jit(solution)/shard_map/all_to_all | solution.py:11
  107.4 12.5 %collective-permute-start.1 = (f32[16,16,512]{2,1,0:T(8,128)S(1)}, f32[16,16,512]{2,1,0:T(8,128)S(1)}, u32[]{:S(2)}, u32[]{:S(2)}) collective-permute-start(f32[16,16,512]{2,1,0:T(8,128)S(1)} %all_to_all.29), channel_id=1, source_target_pairs={{0,16},{16,0},{1,17},{17,1},{2,18},{18,2},{3,19},{19,3},{4,20},{20... | collective-permute-start | bytes 1572872 | tf_op jit(solution)/shard_map/ppermute | solution.py:38
  119.9 1.5 %collective-permute-done.1 = f32[16,16,512]{2,1,0:T(8,128)S(1)} collective-permute-done((f32[16,16,512]{2,1,0:T(8,128)S(1)}, f32[16,16,512]{2,1,0:T(8,128)S(1)}, u32[]{:S(2)}, u32[]{:S(2)}) %collective-permute-start.1) | collective-permute-done | bytes 524320 | tf_op jit(solution)/shard_map/ppermute | solution.py:38
  121.4 0.1 select_bitcast_fusion.1
  121.5 0.1 pad_maximum_fusion
  121.6 0.5 convolution_bitcast_fusion
  122.1 0.1 slice.28
  122.2 0.1 copy.20
  122.3 2.9 %cholesky.16 = f32[32,32]{1,0:T(8,128)S(1)} custom-call(f32[32,32]{1,0:T(8,128)S(1)} %fusion.8), custom_call_target="Cholesky" | custom-call | tf_op jit(solution)/shard_map/jit(cholesky)/cholesky | solution.py:45
  125.2 0.6 compare_reduce_fusion
  125.9 0.7 fusion.5
  126.6 2.4 %custom-call.7 = f32[1,32,32]{1,2,0:T(8,128)S(1)} custom-call(f32[1,32,32]{2,1,0:T(8,128)S(1)} %fusion.5), custom_call_target="InvertDiagBlocksLowerTriangular" | custom-call | tf_op jit(solution)/shard_map/jit(_solve_triangular)/triangular_solve | solution.py:47
  129.0 1.6 %copy.21 = f32[32,16,448]{2,1,0:T(8,128)} copy(f32[32,16,448]{2,0,1:T(8,128)S(1)} %bitcast.39) | data formatting | bytes 1835008 | tf_op jit(solution)/shard_map/slice | solution.py:43
  130.6 1.6 %reshape.34 = f32[32,7168]{1,0:T(8,128)S(1)} reshape(f32[32,16,448]{2,1,0:T(8,128)} %copy.21) | data formatting | bytes 1835008 | tf_op jit(solution)/shard_map/reshape | solution.py:43
  132.2 0.2 copy.22
  132.4 0.1 reshape.35
  132.5 0.1 constant_dynamic-slice_fusion
  132.6 0.9 fusion.1
  133.6 2.9 %fusion = f32[1,64,7168]{2,1,0:T(8,128)} fusion(f32[64,7168]{1,0:T(8,128)S(1)} %add_bitcast_fusion, f32[32,7232]{1,0:T(8,128)S(1)} %fusion.1), kind=kOutput, calls=%fused_computation.1 | convolution fusion | flops 176619520 | bytes 4595712 | tf_op jit(solution)/shard_map/dot_general | solution.py:51
  136.4 0.1 slice.31
  136.5 0.7 dynamic-slice_bitcast_fusion
  (7 shorter events, 0.2 us)
Async XLA Ops:
  0.6 10.7 %copy-start = (f32[448,32]{0,1:T(8,128)S(1)}, f32[448,32]{0,1:T(8,128)}, u32[]{:S(2)}) copy-start(f32[448,32]{0,1:T(8,128)} %param.5) | copy-start | bytes 172036
  2.6 23.1 %collective-permute-start = (f32[64,7168]{1,0:T(8,128)S(1)}, f32[64,7168]{1,0:T(8,128)}, u32[]{:S(2)}, u32[]{:S(2)}) collective-permute-start(f32[64,7168]{1,0:T(8,128)S(1)} %add_bitcast_fusion), channel_id=1, source_target_pairs={{0,16},{16,0},{1,17},{17,1},{2,18},{18,2},{3,19},{19,3},{4,20},{20... | collective-permute-start | bytes 5505032 | tf_op jit(solution)/shard_map/ppermute | solution.py:24
  27.3 1.2 copy-start.1
  107.4 14.0 %collective-permute-start.1 = (f32[16,16,512]{2,1,0:T(8,128)S(1)}, f32[16,16,512]{2,1,0:T(8,128)S(1)}, u32[]{:S(2)}, u32[]{:S(2)}) collective-permute-start(f32[16,16,512]{2,1,0:T(8,128)S(1)} %all_to_all.29), channel_id=1, source_target_pairs={{0,16},{16,0},{1,17},{17,1},{2,18},{18,2},{3,19},{19,3},{4,20},{20... | collective-permute-start | bytes 1572872 | tf_op jit(solution)/shard_map/ppermute | solution.py:38

commit v2 on v0

v2 whole, which is shorter than its diff:
```python
import functools

import jax
import jax.numpy as jnp
from jax import lax
from jax.experimental import pallas as pl
from jax.experimental.pallas import tpu as pltpu
from jax.sharding import Mesh, PartitionSpec as P

F32, BF16 = jnp.float32, jnp.bfloat16
HIGH = lax.Precision.HIGHEST
PLANE = ("z0", "shard")
SWAP = [(0, 1), (1, 0)]
VMEM = pl.BlockSpec(memory_space=pltpu.VMEM)
SMEM = pl.BlockSpec(memory_space=pltpu.SMEM)


def call(body, out, operands, specs, scratch=(), out_specs=None, flops=0):
    moved = sum(o.size * o.dtype.itemsize for o in [*operands, *out])
    return pl.pallas_call(
        body,
        out_shape=out,
        in_specs=specs,
        out_specs=out_specs or [VMEM] * len(out),
        scratch_shapes=list(scratch),
        compiler_params=pltpu.CompilerParams(vmem_limit_bytes=24 * 2**20),
        cost_estimate=pl.CostEstimate(flops=flops, bytes_accessed=moved, transcendentals=0),
    )(*operands)


def split(x, parts):
    out = []
    for _ in range(parts):
        part = x.astype(BF16)
        out.append(part)
        x = x - part.astype(F32)
    return out


def dot(a, b, dims, precision=None):
    return lax.dot_general(a, b, (dims, ((), ())), precision=precision, preferred_element_type=F32)


def left_kernel(q_ref, own_ref, other_ref, parts_ref, out_ref, q3_ref):
    shards, half, share = q_ref.shape
    rows, width = own_ref.shape
    for g in range(shards // 2):
        pair = jnp.concatenate([q_ref[2 * g], q_ref[2 * g + 1]], axis=1)
        for i, part in enumerate(split(pair, 3)):
            q3_ref[i * half : (i + 1) * half, 2 * share * g : 2 * share * (g + 1)] = part
    total = jnp.zeros((3 * half, 3 * rows), F32)
    step = width // 4
    for g in range(4):
        cols = slice(g * step, (g + 1) * step)
        for i, part in enumerate(split(own_ref[:, cols] + other_ref[:, cols], 3)):
            parts_ref[i * rows : (i + 1) * rows, cols] = part
        total = total + dot(q3_ref[:, cols], parts_ref[:, cols], ((1,), (1,)))
    block = lambda i, j: total[i * half : (i + 1) * half, j * rows : (j + 1) * rows]
    left = block(2, 0) + block(1, 1) + block(0, 2)
    left = left + (block(1, 0) + block(0, 1))
    left = left + block(0, 0)
    packed = jnp.concatenate([left[: half // 2], left[half // 2 :]], axis=1)
    out_ref[...] = jnp.broadcast_to(packed[None], out_ref.shape)


def right_kernel(replicas, z0_ref, left_ref, parts_ref, out_ref):
    packed = left_ref[0]
    for z in range(1, left_ref.shape[0]):
        packed = packed + left_ref[z]
    packed = packed * (1.0 / replicas)
    rows = packed.shape[1] // 2
    half = 2 * packed.shape[0]
    left = jnp.concatenate([packed[:, :rows], packed[:, rows:]], axis=0)
    big, mid, low = (part.astype(F32) for part in split(left, 3))
    none = jnp.zeros_like(big)
    stacked = jnp.concatenate(
        [
            jnp.concatenate([big, big, big], axis=1),
            jnp.concatenate([mid, mid, none], axis=1),
            jnp.concatenate([low, none, none], axis=1),
        ],
        axis=0,
    ).astype(BF16)
    mine = jnp.where(z0_ref[0] == 0, left[:, : rows // 2], left[:, rows // 2 :])
    width = parts_ref.shape[1]
    step = width // 8
    piece = step // 4
    for g in range(8):
        product = dot(stacked, parts_ref[:, g * step : (g + 1) * step], ((1,), (0,)))
        right = product[2 * half :] + product[half : 2 * half] + product[:half]
        right = right * (1.0 / replicas)
        for k in range(4):
            cut = right[:, k * piece : (k + 1) * piece]
            out_ref[k % 2, 2 * g + k // 2] = jnp.concatenate([cut, mine], axis=1)


def scatter_kernel(got_ref, out_ref, left_ref):
    total = jnp.zeros(got_ref.shape[2:], F32)
    for z in range(2):
        for s in range(got_ref.shape[1]):
            total = total + got_ref[z, s]
    out_ref[...] = jnp.broadcast_to(total[None], out_ref.shape)
    for g in range(got_ref.shape[1] // 2):
        four = [got_ref[k % 2, 2 * g + k // 2][:, 224:] for k in range(4)]
        left_ref[:, 128 * g : 128 * (g + 1)] = jnp.concatenate(four, axis=1)


def factor_kernel(place_ref, own_ref, other_ref, weights_ref, inverse_ref, left_ref, all_ref):
    core, here = place_ref[0], place_ref[1]
    half = own_ref.shape[0]
    rank = 2 * half
    left_ref[...] = jnp.zeros_like(left_ref)
    left_ref[pl.ds(pl.multiple_of(core * half, half), half), :] = own_ref[...]
    left_ref[pl.ds(pl.multiple_of((1 - core) * half, half), half), :] = other_ref[...]
    left = left_ref[:rank]
    work = dot(left, left_ref[...], ((1,), (1,)), HIGH)
    at_row = lax.broadcasted_iota(jnp.int32, work.shape, 0)
    at_lane = lax.broadcasted_iota(jnp.int32, work.shape, 1)
    work = jnp.where(at_lane == at_row + rank, 1.0, work)
    row_id = lax.broadcasted_iota(jnp.int32, (rank, 1), 0)
    for j in range(rank):
        row = work[j : j + 1]
        column = work[:, j : j + 1]
        scale = 1.0 / work[j : j + 1, j : j + 1]
        factor = jnp.where(row_id > j, column * scale, 0.0)
        work = work - factor * row
    pivots = jnp.sum(jnp.where(at_lane == at_row, work, 0.0), axis=1, keepdims=True)
    inverse = (work / jnp.sqrt(pivots))[:, rank : 2 * rank]
    hat = dot(left, inverse, ((0,), (1,)), HIGH)
    all_ref[...] = dot(hat, inverse, ((1,), (0,)), HIGH)
    rows = 64
    mine = all_ref[pl.ds(pl.multiple_of(here * rows, rows), rows), :]
    mine = jnp.where(core == 0, mine, jnp.concatenate([mine[:, half:], mine[:, :half]], axis=1))
    big, low = (part.astype(F32) for part in split(mine, 2))
    weights_ref[...] = jnp.concatenate(
        [
            jnp.concatenate([big, big], axis=1),
            jnp.concatenate([low, jnp.zeros_like(low)], axis=1),
        ],
        axis=0,
    ).astype(BF16)
    swapped = jnp.concatenate([inverse[:, half:], inverse[:, :half]], axis=1)
    inverse_ref[...] = jnp.where(core == 0, inverse, swapped)


def final_kernel(place_ref, own_ref, other_ref, weights_ref, inverse_ref, merged_ref, out_ref, q_ref, hold_ref, sem):
    here = place_ref[1]
    rows, width = merged_ref.shape
    piece = 224
    step = 4 * piece
    copies = []
    for g in range(width // step):
        cols = slice(g * step, (g + 1) * step)
        raw = jnp.concatenate(
            [
                jnp.concatenate([ref[k % 2, 2 * g + k // 2][:, :piece] for k in range(4)], axis=1)
                for ref in (own_ref, other_ref)
            ],
            axis=0,
        )
        product = dot(weights_ref[...], jnp.concatenate(split(raw, 2), axis=0), ((1,), (0,)))
        hold_ref[:, cols] = merged_ref[:, cols] - (product[rows:] + product[:rows])
        copy = pltpu.make_async_copy(hold_ref.at[:, cols], out_ref.at[:, cols], sem.at[g])
        copy.start()
        copies.append(copy)
    raw = jnp.concatenate(
        [
            jnp.concatenate([ref[0, here][:, :piece], ref[1, here][:, :piece]], axis=1)
            for ref in (own_ref, other_ref)
        ],
        axis=0,
    )
    q_ref[...] = dot(inverse_ref[...], raw, ((1,), (0,)), HIGH)
    for copy in copies:
        copy.wait()


def to_all(block, peers, axis):
    return lax.all_to_all(jnp.broadcast_to(block, (peers, *block.shape)), axis, 0, 0)


def per_device(grads, errors, q_prev):
    shape = jax.ShapeDtypeStruct
    rows, width = errors.shape[1:]
    share, rank = q_prev.shape
    half = rank // 2
    core, z0, here = lax.axis_index("core"), lax.axis_index("z0"), lax.axis_index("shard")
    replicas = 32

    merged = grads[0].astype(F32) + errors[0]
    own_q = lax.dynamic_slice_in_dim(q_prev.T, core * half, half, 0)
    all_q = to_all(own_q, 16, "shard")
    other = lax.ppermute(merged, "core", SWAP)

    parts, left = call(
        left_kernel,
        [shape((3 * rows, width), BF16), shape((16, 8, 128), F32)],
        [all_q, merged, other],
        [VMEM] * 3,
        [pltpu.VMEM((3 * half, width), BF16)],
        flops=2 * 48 * 192 * width,
    )
    left = lax.all_to_all(left, ("z8", "z0"), 0, 0)

    (pieces,) = call(
        functools.partial(right_kernel, replicas),
        [shape((2, 16, half, 256), F32)],
        [z0[None], left, parts],
        [SMEM, VMEM, VMEM],
        flops=2 * 48 * 192 * width,
    )
    pieces = lax.all_to_all(pieces.reshape(32, half, 256), PLANE, 0, 0).reshape(pieces.shape)
    right, left_own = call(
        scatter_kernel,
        [shape((8, half, 256), F32), shape((half, 16 * rows), F32)],
        [pieces],
        [VMEM],
    )
    right = lax.all_to_all(right, "z8", 0, 0)

    left_other = lax.ppermute(left_own, "core", SWAP)
    place = jnp.stack([core, here])
    weights, inverse = call(
        factor_kernel,
        [shape((2 * rows, 2 * rank), BF16), shape((rank, rank), F32)],
        [place, left_own, left_other],
        [SMEM, VMEM, VMEM],
        [pltpu.VMEM((128, 16 * rows), F32), pltpu.VMEM((16 * rows, rank), F32)],
        flops=10**7,
    )

    raw = to_all(right.sum(0), 32, PLANE)
    raw_other = lax.ppermute(raw, "core", SWAP)
    out, q_new = call(
        final_kernel,
        [shape((rows, width), F32), shape((rank, share), F32)],
        [place, raw.reshape(2, 16, half, 256), raw_other.reshape(2, 16, half, 256), weights, inverse, merged],
        [SMEM] + [VMEM] * 5,
        [pltpu.VMEM((rows, width), F32), pltpu.SemaphoreType.DMA((8,))],
        [pl.BlockSpec(memory_space=pl.ANY), VMEM],
        flops=2 * 128 * 64 * width,
    )
    return (out[None], q_new.T)


def solution(mesh):
    parts = Mesh(mesh.devices.reshape(8, 2, 2, 16), ("z8", "z0", "core", "shard"))
    dp = ("z8", "z0", "core")
    in_specs = (P(dp, "shard", None), P(dp, "shard", None), P("shard", None))
    out_specs = (P(dp, "shard", None), P("shard", None))
    return jax.shard_map(
        per_device, mesh=parts, in_specs=in_specs, out_specs=out_specs, check_vma=False
    )
```

time: 686 us -> 120 us (0.17)
  waiting for transfers between devices: 472 us -> 12.7 us
  blocking collectives: 178 us -> 56.8 us
  starting transfers between devices: 0.04 us -> 31.3 us
  between operations: 14.1 us -> 0.75 us
  Pallas kernels: 0 us -> 12.6 us
  matrix products: 8.32 us -> 0 us
    psum x1 -> x0, waiting for transfers between devices: 472 us -> none  [per_device(): right_full = lax.psum(own_term, ('dp', 'shard')) / replicas]
    psum x2 -> x0, blocking collectives: 157 us -> none  [the longest x1 98.7 us: per_device(): left = lax.psum(partial_left, 'dp') / replicas]
    all_to_all x0 -> x4, blocking collectives: none -> 56.8 us  [the longest x2 26 us: to_all(): lax.all_to_all(jnp.broadcast_to(block, (peers, *block.shape)), axis, 0, 0)]
    all_gather x1 -> x0, blocking collectives: 21.1 us -> none  [per_device(): lax.all_gather(q_prev, 'shard', axis=0, tiled=True)]
    ppermute x0 -> x3, starting transfers between devices: none -> 18.7 us  [the longest x1 8.79 us: per_device(): other = lax.ppermute(merged, 'core', SWAP)]
    pallas_call x0 -> x5, Pallas kernels: none -> 12.6 us  [call(): pl.pallas_call(body, out_shape=out, in_specs=specs, out_specs=out_specs o...]
    all_to_all x0 -> x1, starting transfers between devices: none -> 12.6 us  [per_device(): left = lax.all_to_all(left, ('z8', 'z0'), 0, 0)]
    all_to_all x0 -> x1, waiting for transfers between devices: none -> 11.6 us  [per_device(): left = lax.all_to_all(left, ('z8', 'z0'), 0, 0)]
  transfers between devices with their start and end apart: 1 -> 4, of which waited for: 1 -> 2; matrix products, arithmetic and copies ran while one was open for 0% -> 0% of each run, Pallas kernels for 0% -> 5%
where the time goes in v2:
time: 120 us
  blocking collectives  56.8 us (47%)
  starting transfers between devices  31.3 us (26%)
  waiting for transfers between devices  12.7 us (11%)
  Pallas kernels  12.6 us (10%)
  local copies, waits for them, and re-layouts  3.43 us (3%)
  other arithmetic  2.01 us (2%)
    all_to_all x2, blocking collectives, to_all(): lax.all_to_all(jnp.broadcast_to(block, (peers, *block.shape)), axis, 0, 0)  26 us
    all_to_all x1, blocking collectives, per_device(): right = lax.all_to_all(right, 'z8', 0, 0)  16.8 us
    all_to_all x1, blocking collectives, per_device(): lax.all_to_all(pieces.reshape(32, half, 256), PLANE, 0, 0)  14 us
    pallas_call x5, Pallas kernels, call(): pl.pallas_call(body, out_shape=out, in_specs=specs, out_specs=out_specs o...  12.6 us
    all_to_all x1, starting transfers between devices, per_device(): left = lax.all_to_all(left, ('z8', 'z0'), 0, 0)  12.6 us
    all_to_all x1, waiting for transfers between devices, per_device(): left = lax.all_to_all(left, ('z8', 'z0'), 0, 0)  11.6 us
    ppermute x1, starting transfers between devices, per_device(): other = lax.ppermute(merged, 'core', SWAP)  8.79 us
    ppermute x1, starting transfers between devices, per_device(): raw_other = lax.ppermute(raw, 'core', SWAP)  8.04 us
  transfers between devices with their start and end apart: 4, of which 2 were waited for; matrix products, arithmetic and copies ran while one was open for 0% of the time, Pallas kernels for 5%

profile of v2, /device:TPU:1, one launch (start us, length us, event | category | flops | bytes accessed | tf_op | source)
XLA Modules:
  0.0 119.7 jit_solution(13397610364207336201)
XLA Ops:
  0.6 0.0 copy-start
  0.6 1.9 %add_bitcast_fusion.own_ref.merged_ref = f32[64,7168]{1,0:T(8,128)S(1)} fusion(f32[1,64,7168]{2,1,0:T(8,128)} %param.4, bf16[1,64,7168]{2,1,0:T(8,128)(2,1)} %param.3), kind=kLoop, calls=%fused_computation | loop fusion | flops 917504 | bytes 4587520 | tf_op jit(solution)/shard_map/add | solution.py:190
  2.6 8.8 %collective-permute-start = (f32[64,7168]{1,0:T(8,128)S(1)}, f32[64,7168]{1,0:T(8,128)}, u32[]{:S(2)}, u32[]{:S(2)}) collective-permute-start(f32[64,7168]{1,0:T(8,128)S(1)} %add_bitcast_fusion.own_ref.merged_ref), channel_id=1, source_target_pairs={{0,16},{16,0},{1,17},{17,1},{2,18},{18,2},{3,19},{19,3},{4,20},{20... | collective-permute-start | bytes 5505032 | tf_op jit(solution)/shard_map/ppermute | solution.py:193
  11.4 0.0 copy-done
  11.4 0.1 broadcast_in_dim.13
  11.5 13.6 %all_to_all.25.q_ref = f32[16,16,448]{2,1,0:T(8,128)S(1)} all-to-all(f32[16,16,448]{2,1,0:T(8,128)S(1)} %broadcast_in_dim.13), channel_id=1, replica_groups=mesh['z8'=8,'z0'=2,'core'=2,'shard'=16] {'shard'}, dimensions={0} | all-to-all | bytes 917504 | tf_op jit(solution)/shard_map/all_to_all | solution.py:179
  25.1 0.0 collective-permute-done.other_ref
  25.1 3.3 %shard_map.50 = (bf16[192,7168]{1,0:T(8,128)(2,1)S(1)}, f32[16,8,128]{2,1,0:T(8,128)}) custom-call(f32[16,16,448]{2,1,0:T(8,128)S(1)} %all_to_all.25.q_ref, f32[64,7168]{1,0:T(8,128)S(1)} %add_bitcast_fusion.own_ref.merged_ref, f32[64,7168]{1,0:T(8,128)} %collective-permute-done.other_ref), custom_call_target="tpu_custom_call" | custom-call | flops 132120576 | bytes 6946816 | tf_op jit(solution)/shard_map/pallas_call | solution.py:20
  28.4 0.0 copy-start.1
  28.4 1.5 %copy-done.1 = bf16[192,7168]{1,0:T(8,128)(2,1)} copy-done((bf16[192,7168]{1,0:T(8,128)(2,1)}, bf16[192,7168]{1,0:T(8,128)(2,1)S(1)}, u32[]{:S(2)}) %copy-start.1) | copy-done | bytes 2752536
  29.9 12.6 %all-to-all-start.1 = ((f32[16,8,128]{2,1,0:T(8,128)}), f32[16,8,128]{2,1,0:T(8,128)S(1)}, u32[]{:S(2)}, u32[]{:S(2)}) async-start(f32[16,8,128]{2,1,0:T(8,128)} %get-tuple-element.10), calls=%async_computation.1 | async-start | bytes 131072 | tf_op jit(solution)/shard_map/all_to_all | solution.py:203
  42.5 11.6 %all-to-all-done.1.left_ref = f32[16,8,128]{2,1,0:T(8,128)S(1)} async-done(((f32[16,8,128]{2,1,0:T(8,128)}), f32[16,8,128]{2,1,0:T(8,128)S(1)}, u32[]{:S(2)}, u32[]{:S(2)}) %all-to-all-start.1) | async-done | bytes 65568 | tf_op jit(solution)/shard_map/all_to_all | solution.py:203
  54.1 0.0 copy-start.2
  54.1 1.8 %copy-done.2 = bf16[192,7168]{1,0:T(8,128)(2,1)S(1)} copy-done((bf16[192,7168]{1,0:T(8,128)(2,1)S(1)}, bf16[192,7168]{1,0:T(8,128)(2,1)}, u32[]{:S(2)}) %copy-start.2) | copy-done | bytes 2752536
  55.8 0.8 shard_map.51
  56.6 14.0 %all_to_all.26 = f32[32,16,256]{2,1,0:T(8,128)S(1)} all-to-all(f32[32,16,256]{2,1,0:T(8,128)S(1)} %bitcast.15), channel_id=1, replica_groups=mesh['z8'=8,'z0'=2,'core'=2,'shard'=16] {'z0','shard'}, dimensions={0} | all-to-all | bytes 1048576 | tf_op jit(solution)/shard_map/all_to_all | solution.py:212
  70.6 0.1 shard_map.52
  70.8 16.8 %all_to_all.27 = f32[8,16,256]{2,1,0:T(8,128)S(1)} all-to-all(f32[8,16,256]{2,1,0:T(8,128)S(1)} %get-tuple-element.12), channel_id=1, replica_groups=mesh['z8'=8,'z0'=2,'core'=2,'shard'=16] {'z8'}, dimensions={0} | all-to-all | bytes 262144 | tf_op jit(solution)/shard_map/all_to_all | solution.py:219
  87.6 0.1 broadcast_in_dim.14
  87.6 12.4 %all_to_all.28 = f32[32,16,256]{2,1,0:T(8,128)S(1)} all-to-all(f32[32,16,256]{2,1,0:T(8,128)S(1)} %broadcast_in_dim.14), channel_id=1, replica_groups=mesh['z8'=8,'z0'=2,'core'=2,'shard'=16] {'z0','shard'}, dimensions={0} | all-to-all | bytes 1048576 | tf_op jit(solution)/shard_map/all_to_all | solution.py:179
  100.0 8.0 %collective-permute-start.1 = (f32[32,16,256]{2,1,0:T(8,128)S(1)}, f32[32,16,256]{2,1,0:T(8,128)S(1)}, u32[]{:S(2)}, u32[]{:S(2)}) collective-permute-start(f32[32,16,256]{2,1,0:T(8,128)S(1)} %all_to_all.28), channel_id=1, source_target_pairs={{0,16},{16,0},{1,17},{17,1},{2,18},{18,2},{3,19},{19,3},{4,20},{20... | collective-permute-start | bytes 1572872 | tf_op jit(solution)/shard_map/ppermute | solution.py:233
  108.0 1.9 %collective-permute-start.2 = (f32[16,1024]{1,0:T(8,128)S(1)}, f32[16,1024]{1,0:T(8,128)S(1)}, u32[]{:S(2)}, u32[]{:S(2)}) collective-permute-start(f32[16,1024]{1,0:T(8,128)S(1)} %get-tuple-element.13.own_ref), channel_id=1, source_target_pairs={{0,16},{16,0},{1,17},{17,1},{2,18},{18,2},{3,19},{19,3},{4,20},{20... | collective-permute-start | bytes 196616 | tf_op jit(solution)/shard_map/ppermute | solution.py:221
  110.0 0.1 pad_add_fusion.place_ref
  110.1 1.1 collective-permute-done.2.other_ref
  111.2 5.7 %shard_map.53 = (bf16[128,64]{1,0:T(8,128)(2,1)S(1)}, f32[32,32]{1,0:T(8,128)S(1)}) custom-call(s32[2]{0:T(128)S(1)} %pad_add_fusion.place_ref, f32[16,1024]{1,0:T(8,128)S(1)} %get-tuple-element.13.own_ref, f32[16,1024]{1,0:T(8,128)S(1)} %collective-permute-done.2.other_ref), custom_call_target="tpu_custom_call" | custom-call | flops 10000000 | bytes 151560 | tf_op jit(solution)/shard_map/pallas_call | solution.py:20
  116.9 0.0 collective-permute-done.1
  116.9 2.8 %shard_map.54 = (f32[64,7168]{1,0:T(8,128)}, f32[32,448]{1,0:T(8,128)}) custom-call(s32[2]{0:T(128)S(1)} %pad_add_fusion.place_ref, f32[2,16,16,256]{3,2,1,0:T(8,128)S(1)} %bitcast.13, f32[2,16,16,256]{3,2,1,0:T(8,128)S(1)} %bitcast.16, bf16[128,64]{1,0:T(8,128)(2,1)S(1)} %get-tuple-element.14.weights_ref, f32[32,32]{1,0:T(8,128)S(1)} %get-tuple-element.15.inverse_ref, ...), custom_call_target="tpu_custom_call" | custom-call | flops 117440512 | bytes 4796424 | tf_op jit(solution)/shard_map/pallas_call | solution.py:20
  (2 shorter events, 0.0 us)
Async XLA Ops:
  0.6 10.7 %copy-start = (f32[448,32]{0,1:T(8,128)S(1)}, f32[448,32]{0,1:T(8,128)}, u32[]{:S(2)}) copy-start(f32[448,32]{0,1:T(8,128)} %param.5) | copy-start | bytes 172036
  2.6 22.5 %collective-permute-start = (f32[64,7168]{1,0:T(8,128)S(1)}, f32[64,7168]{1,0:T(8,128)}, u32[]{:S(2)}, u32[]{:S(2)}) collective-permute-start(f32[64,7168]{1,0:T(8,128)S(1)} %add_bitcast_fusion.own_ref.merged_ref), channel_id=1, source_target_pairs={{0,16},{16,0},{1,17},{17,1},{2,18},{18,2},{3,19},{19,3},{4,20},{20... | collective-permute-start | bytes 5505032 | tf_op jit(solution)/shard_map/ppermute | solution.py:193
  28.4 1.5 %copy-start.1 = (bf16[192,7168]{1,0:T(8,128)(2,1)}, bf16[192,7168]{1,0:T(8,128)(2,1)S(1)}, u32[]{:S(2)}) copy-start(bf16[192,7168]{1,0:T(8,128)(2,1)S(1)} %get-tuple-element.11.parts_ref) | copy-start | bytes 8257540
  29.9 24.2 %all-to-all-start.1 = ((f32[16,8,128]{2,1,0:T(8,128)}), f32[16,8,128]{2,1,0:T(8,128)S(1)}, u32[]{:S(2)}, u32[]{:S(2)}) async-start(f32[16,8,128]{2,1,0:T(8,128)} %get-tuple-element.10), calls=%async_computation.1 | async-start | bytes 131072 | tf_op jit(solution)/shard_map/all_to_all | solution.py:203
  54.1 1.8 %copy-start.2 = (bf16[192,7168]{1,0:T(8,128)(2,1)S(1)}, bf16[192,7168]{1,0:T(8,128)(2,1)}, u32[]{:S(2)}) copy-start(bf16[192,7168]{1,0:T(8,128)(2,1)} %copy-done.1) | copy-start | bytes 8257540
  100.0 16.9 %collective-permute-start.1 = (f32[32,16,256]{2,1,0:T(8,128)S(1)}, f32[32,16,256]{2,1,0:T(8,128)S(1)}, u32[]{:S(2)}, u32[]{:S(2)}) collective-permute-start(f32[32,16,256]{2,1,0:T(8,128)S(1)} %all_to_all.28), channel_id=1, source_target_pairs={{0,16},{16,0},{1,17},{17,1},{2,18},{18,2},{3,19},{19,3},{4,20},{20... | collective-permute-start | bytes 1572872 | tf_op jit(solution)/shard_map/ppermute | solution.py:233
  108.0 3.1 %collective-permute-start.2 = (f32[16,1024]{1,0:T(8,128)S(1)}, f32[16,1024]{1,0:T(8,128)S(1)}, u32[]{:S(2)}, u32[]{:S(2)}) collective-permute-start(f32[16,1024]{1,0:T(8,128)S(1)} %get-tuple-element.13.own_ref), channel_id=1, source_target_pairs={{0,16},{16,0},{1,17},{17,1},{2,18},{18,2},{3,19},{19,3},{4,20},{20... | collective-permute-start | bytes 196616 | tf_op jit(solution)/shard_map/ppermute | solution.py:221

commit v3 on v2

--- a/solution.py
+++ b/solution.py
@@ -12,10 +12,13 @@
 PLANE = ("z0", "shard")
 SWAP = [(0, 1), (1, 0)]
 VMEM = pl.BlockSpec(memory_space=pltpu.VMEM)
+ANY = pl.BlockSpec(memory_space=pl.ANY)
+CUTS = 8
+PIECE = 224
 SMEM = pl.BlockSpec(memory_space=pltpu.SMEM)
 
 
-def call(body, out, operands, specs, scratch=(), out_specs=None, flops=0):
+def call(body, out, operands, specs, scratch=(), out_specs=None, flops=0, limit=24):
     moved = sum(o.size * o.dtype.itemsize for o in [*operands, *out])
     return pl.pallas_call(
         body,
@@ -23,7 +26,7 @@
         in_specs=specs,
         out_specs=out_specs or [VMEM] * len(out),
         scratch_shapes=list(scratch),
-        compiler_params=pltpu.CompilerParams(vmem_limit_bytes=24 * 2**20),
+        compiler_params=pltpu.CompilerParams(vmem_limit_bytes=limit * 2**20),
         cost_estimate=pl.CostEstimate(flops=flops, bytes_accessed=moved, transcendentals=0),
     )(*operands)
 
@@ -41,29 +44,61 @@
     return lax.dot_general(a, b, (dims, ((), ())), precision=precision, preferred_element_type=F32)
 
 
-def left_kernel(q_ref, own_ref, other_ref, parts_ref, out_ref, q3_ref):
+def ask_kernel(core_ref, q_ref, out_ref):
+    half = out_ref.shape[1]
+    mine = q_ref[pl.ds(pl.multiple_of(core_ref[0] * half, half), half), :]
+    out_ref[...] = jnp.broadcast_to(mine[None], out_ref.shape)
+
+
+def line_kernel(q_ref, out_ref):
     shards, half, share = q_ref.shape
-    rows, width = own_ref.shape
     for g in range(shards // 2):
         pair = jnp.concatenate([q_ref[2 * g], q_ref[2 * g + 1]], axis=1)
         for i, part in enumerate(split(pair, 3)):
-            q3_ref[i * half : (i + 1) * half, 2 * share * g : 2 * share * (g + 1)] = part
+            out_ref[i * half : (i + 1) * half, 2 * share * g : 2 * share * (g + 1)] = part
+
+
+def left_kernel(q_ref, own_ref, other_ref, parts_ref, out_ref, own_buf, other_buf, parts_buf, in_sem, out_sem):
+    half = q_ref.shape[0] // 3
+    rows, width = own_ref.shape
+    step = width // CUTS
+    cuts = [slice(g * step, (g + 1) * step) for g in range(CUTS)]
+    loads, stores = [], []
+    for g, cols in enumerate(cuts):
+        pair = [(own_ref, own_buf), (other_ref, other_buf)]
+        loads.append(
+            [pltpu.make_async_copy(r.at[:, cols], b.at[:, cols], in_sem.at[i, g]) for i, (r, b) in enumerate(pair)]
+        )
+        for load in loads[-1]:
+            load.start()
     total = jnp.zeros((3 * half, 3 * rows), F32)
-    step = width // 4
-    for g in range(4):
-        cols = slice(g * step, (g + 1) * step)
-        for i, part in enumerate(split(own_ref[:, cols] + other_ref[:, cols], 3)):
-            parts_ref[i * rows : (i + 1) * rows, cols] = part
-        total = total + dot(q3_ref[:, cols], parts_ref[:, cols], ((1,), (1,)))
+    for g, cols in enumerate(cuts):
+        for load in loads[g]:
+            load.wait()
+        for i, part in enumerate(split(own_buf[:, cols] + other_buf[:, cols], 3)):
+            parts_buf[i * rows : (i + 1) * rows, cols] = part
+        stores.append(pltpu.make_async_copy(parts_buf.at[:, cols], parts_ref.at[:, cols], out_sem.at[g]))
+        stores[-1].start()
+        total = total + dot(q_ref[:, cols], parts_buf[:, cols], ((1,), (1,)))
     block = lambda i, j: total[i * half : (i + 1) * half, j * rows : (j + 1) * rows]
     left = block(2, 0) + block(1, 1) + block(0, 2)
     left = left + (block(1, 0) + block(0, 1))
     left = left + block(0, 0)
     packed = jnp.concatenate([left[: half // 2], left[half // 2 :]], axis=1)
     out_ref[...] = jnp.broadcast_to(packed[None], out_ref.shape)
-
-
-def right_kernel(replicas, z0_ref, left_ref, parts_ref, out_ref):
+    for store in stores:
+        store.wait()
+
+
+def right_kernel(replicas, z0_ref, left_ref, parts_ref, out_ref, parts_buf, sem):
+    width = parts_ref.shape[1]
+    step = width // 8
+    piece = step // 4
+    loads = []
+    for g in range(8):
+        cols = slice(g * step, (g + 1) * step)
+        loads.append(pltpu.make_async_copy(parts_ref.at[:, cols], parts_buf.at[:, cols], sem.at[g]))
+        loads[-1].start()
     packed = left_ref[0]
     for z in range(1, left_ref.shape[0]):
         packed = packed + left_ref[z]
@@ -82,11 +117,9 @@
         axis=0,
     ).astype(BF16)
     mine = jnp.where(z0_ref[0] == 0, left[:, : rows // 2], left[:, rows // 2 :])
-    width = parts_ref.shape[1]
-    step = width // 8
-    piece = step // 4
     for g in range(8):
-        product = dot(stacked, parts_ref[:, g * step : (g + 1) * step], ((1,), (0,)))
+        loads[g].wait()
+        product = dot(stacked, parts_buf[:, g * step : (g + 1) * step], ((1,), (0,)))
         right = product[2 * half :] + product[half : 2 * half] + product[:half]
         right = right * (1.0 / replicas)
         for k in range(4):
@@ -99,10 +132,17 @@
     for z in range(2):
         for s in range(got_ref.shape[1]):
             total = total + got_ref[z, s]
+    out_ref[...] = jnp.broadcast_to(total[None, :, :PIECE], out_ref.shape)
+    for g in range(got_ref.shape[1] // 2):
+        four = [got_ref[k % 2, 2 * g + k // 2][:, PIECE:] for k in range(4)]
+        left_ref[:, 128 * g : 128 * (g + 1)] = jnp.concatenate(four, axis=1)
+
+
+def spread_kernel(got_ref, weights_ref, inverse_ref, out_ref):
+    total = got_ref[0]
+    for z in range(1, got_ref.shape[0]):
+        total = total + got_ref[z]
     out_ref[...] = jnp.broadcast_to(total[None], out_ref.shape)
-    for g in range(got_ref.shape[1] // 2):
-        four = [got_ref[k % 2, 2 * g + k // 2][:, 224:] for k in range(4)]
-        left_ref[:, 128 * g : 128 * (g + 1)] = jnp.concatenate(four, axis=1)
 
 
 def factor_kernel(place_ref, own_ref, other_ref, weights_ref, inverse_ref, left_ref, all_ref):
@@ -130,7 +170,6 @@
     all_ref[...] = dot(hat, inverse, ((1,), (0,)), HIGH)
     rows = 64
     mine = all_ref[pl.ds(pl.multiple_of(here * rows, rows), rows), :]
-    mine = jnp.where(core == 0, mine, jnp.concatenate([mine[:, half:], mine[:, :half]], axis=1))
     big, low = (part.astype(F32) for part in split(mine, 2))
     weights_ref[...] = jnp.concatenate(
         [
@@ -139,34 +178,33 @@
         ],
         axis=0,
     ).astype(BF16)
-    swapped = jnp.concatenate([inverse[:, half:], inverse[:, :half]], axis=1)
-    inverse_ref[...] = jnp.where(core == 0, inverse, swapped)
-
-
-def final_kernel(place_ref, own_ref, other_ref, weights_ref, inverse_ref, merged_ref, out_ref, q_ref, hold_ref, sem):
+    inverse_ref[...] = inverse
+
+
+def final_kernel(place_ref, raw_ref, weights_ref, inverse_ref, grads_ref, errors_ref, out_ref, q_ref, hold_ref, sem):
     here = place_ref[1]
-    rows, width = merged_ref.shape
-    piece = 224
-    step = 4 * piece
+    rows, width = hold_ref.shape
+    step = 4 * PIECE
     copies = []
     for g in range(width // step):
         cols = slice(g * step, (g + 1) * step)
         raw = jnp.concatenate(
             [
-                jnp.concatenate([ref[k % 2, 2 * g + k // 2][:, :piece] for k in range(4)], axis=1)
-                for ref in (own_ref, other_ref)
+                jnp.concatenate([raw_ref[core, k % 2, 2 * g + k // 2] for k in range(4)], axis=1)
+                for core in range(2)
             ],
             axis=0,
         )
         product = dot(weights_ref[...], jnp.concatenate(split(raw, 2), axis=0), ((1,), (0,)))
-        hold_ref[:, cols] = merged_ref[:, cols] - (product[rows:] + product[:rows])
+        merged = grads_ref[0, :, cols].astype(F32) + errors_ref[0, :, cols]
+        hold_ref[:, cols] = merged - (product[rows:] + product[:rows])
         copy = pltpu.make_async_copy(hold_ref.at[:, cols], out_ref.at[:, cols], sem.at[g])
         copy.start()
         copies.append(copy)
     raw = jnp.concatenate(
         [
-            jnp.concatenate([ref[0, here][:, :piece], ref[1, here][:, :piece]], axis=1)
-            for ref in (own_ref, other_ref)
+            jnp.concatenate([raw_ref[core, 0, here], raw_ref[core, 1, here]], axis=1)
+            for core in range(2)
         ],
         axis=0,
     )
@@ -187,18 +225,37 @@
     core, z0, here = lax.axis_index("core"), lax.axis_index("z0"), lax.axis_index("shard")
     replicas = 32
 
+    (own_q,) = call(
+        ask_kernel,
+        [shape((16, half, share), F32)],
+        [core[None], q_prev.T],
+        [SMEM, VMEM],
+    )
+    all_q = lax.all_to_all(own_q, "shard", 0, 0)
     merged = grads[0].astype(F32) + errors[0]
-    own_q = lax.dynamic_slice_in_dim(q_prev.T, core * half, half, 0)
-    all_q = to_all(own_q, 16, "shard")
     other = lax.ppermute(merged, "core", SWAP)
-
+    (all_q,) = call(
+        line_kernel,
+        [shape((3 * half, width), BF16)],
+        [all_q],
+        [VMEM],
+        flops=10**11,
+    )
     parts, left = call(
         left_kernel,
         [shape((3 * rows, width), BF16), shape((16, 8, 128), F32)],
         [all_q, merged, other],
-        [VMEM] * 3,
-        [pltpu.VMEM((3 * half, width), BF16)],
+        [VMEM, ANY, ANY],
+        [
+            pltpu.VMEM((rows, width), F32),
+            pltpu.VMEM((rows, width), F32),
+            pltpu.VMEM((3 * rows, width), BF16),
+            pltpu.SemaphoreType.DMA((2, CUTS)),
+            pltpu.SemaphoreType.DMA((CUTS,)),
+        ],
+        [ANY, VMEM],
         flops=2 * 48 * 192 * width,
+        limit=52,
     )
     left = lax.all_to_all(left, ("z8", "z0"), 0, 0)
 
@@ -206,13 +263,15 @@
         functools.partial(right_kernel, replicas),
         [shape((2, 16, half, 256), F32)],
         [z0[None], left, parts],
-        [SMEM, VMEM, VMEM],
+        [SMEM, VMEM, ANY],
+        [pltpu.VMEM((3 * rows, width), BF16), pltpu.SemaphoreType.DMA((8,))],
         flops=2 * 48 * 192 * width,
+        limit=52,
     )
     pieces = lax.all_to_all(pieces.reshape(32, half, 256), PLANE, 0, 0).reshape(pieces.shape)
     right, left_own = call(
         scatter_kernel,
-        [shape((8, half, 256), F32), shape((half, 16 * rows), F32)],
+        [shape((8, half, PIECE), F32), shape((half, 16 * rows), F32)],
         [pieces],
         [VMEM],
     )
@@ -229,12 +288,15 @@
         flops=10**7,
     )
 
-    raw = to_all(right.sum(0), 32, PLANE)
-    raw_other = lax.ppermute(raw, "core", SWAP)
+    (raw,) = call(
+        spread_kernel, [shape((32, half, PIECE), F32)], [right, weights, inverse], [VMEM] * 3
+    )
+    raw = lax.all_to_all(raw, PLANE, 0, 0)
+    raw = lax.all_gather(raw, "core").reshape(2, 2, 16, half, PIECE)
     out, q_new = call(
         final_kernel,
         [shape((rows, width), F32), shape((rank, share), F32)],
-        [place, raw.reshape(2, 16, half, 256), raw_other.reshape(2, 16, half, 256), weights, inverse, merged],
+        [place, raw, weights, inverse, grads, errors],
         [SMEM] + [VMEM] * 5,
         [pltpu.VMEM((rows, width), F32), pltpu.SemaphoreType.DMA((8,))],
         [pl.BlockSpec(memory_space=pl.ANY), VMEM],

time: 120 us -> 113 us (0.942)
  blocking collectives: 56.8 us -> 35.6 us
  Pallas kernels: 12.6 us -> 18.6 us
  waiting for transfers between devices: 12.7 us -> 18.1 us
  starting transfers between devices: 31.3 us -> 35.7 us
  local copies, waits for them, and re-layouts: 3.43 us -> 0.92 us
    all_to_all x3 -> x1, blocking collectives: 42.8 us -> 12.7 us  [per_device(): raw = lax.all_to_all(raw, PLANE, 0, 0)]
    all_to_all x0 -> x2, starting transfers between devices: none -> 11.5 us  [the longest x1 7.58 us: per_device(): all_q = lax.all_to_all(own_q, 'shard', 0, 0)]
    ppermute x1 -> x0, starting transfers between devices: 8.04 us -> none  [per_device(): raw_other = lax.ppermute(raw, 'core', SWAP)]
    all_gather x0 -> x1, blocking collectives: none -> 7.28 us  [per_device(): raw = lax.all_gather(raw, 'core').reshape(2, 2, 16, half, PIECE)]
    pallas_call x5 -> x8, Pallas kernels: 12.6 us -> 18.6 us  [call(): pl.pallas_call(body, out_shape=out, in_specs=specs, out_specs=out_specs o...]
    ppermute x1, starting transfers between devices: 8.79 us -> 4.76 us  [per_device(): other = lax.ppermute(merged, 'core', SWAP)]
    all_to_all x0 -> x2, waiting for transfers between devices: none -> 3.51 us  [the longest x1 2.11 us: per_device(): right = lax.all_to_all(right, 'z8', 0, 0)]
    ppermute x1, starting transfers between devices: 1.92 us -> 5.37 us  [per_device(): left_other = lax.ppermute(left_own, 'core', SWAP)]
  transfers between devices with their start and end apart: 4 -> 5, of which waited for: 2 -> 5; matrix products, arithmetic and copies ran while one was open for 0% -> 3% of each run, Pallas kernels for 5% -> 5%
where the time goes in v3:
time: 113 us
  starting transfers between devices  35.7 us (32%)
  blocking collectives  35.6 us (32%)
  Pallas kernels  18.6 us (16%)
  waiting for transfers between devices  18.1 us (16%)
  other arithmetic  2.96 us (3%)
    pallas_call x8, Pallas kernels, call(): pl.pallas_call(body, out_shape=out, in_specs=specs, out_specs=out_specs o...  18.6 us
    all_to_all x1, blocking collectives, per_device(): lax.all_to_all(pieces.reshape(32, half, 256), PLANE, 0, 0)  15.6 us
    all_to_all x1, starting transfers between devices, per_device(): left = lax.all_to_all(left, ('z8', 'z0'), 0, 0)  14 us
    all_to_all x1, blocking collectives, per_device(): raw = lax.all_to_all(raw, PLANE, 0, 0)  12.7 us
    all_to_all x1, waiting for transfers between devices, per_device(): left = lax.all_to_all(left, ('z8', 'z0'), 0, 0)  11.7 us
    all_to_all x1, starting transfers between devices, per_device(): all_q = lax.all_to_all(own_q, 'shard', 0, 0)  7.58 us
    all_gather x1, blocking collectives, per_device(): raw = lax.all_gather(raw, 'core').reshape(2, 2, 16, half, PIECE)  7.28 us
    ppermute x1, starting transfers between devices, per_device(): left_other = lax.ppermute(left_own, 'core', SWAP)  5.37 us
  transfers between devices with their start and end apart: 5, of which 5 were waited for; matrix products, arithmetic and copies ran while one was open for 3% of the time, Pallas kernels for 5%

profile of v3, /device:TPU:1, one launch (start us, length us, event | category | flops | bytes accessed | tf_op | source)
XLA Modules:
  0.0 112.6 jit_solution(18003452778215979321)
XLA Ops:
  0.6 0.0 copy-start.1
  0.6 0.0 copy-start.2
  0.7 0.9 copy-done.2
  1.6 0.8 shard_map.50
  2.4 7.6 %all-to-all-start = ((f32[16,16,448]{2,1,0:T(8,128)}), f32[16,16,448]{2,1,0:T(8,128)S(1)}, u32[]{:S(2)}, u32[]{:S(2)}) async-start(f32[16,16,448]{2,1,0:T(8,128)} %shard_map.50), calls=%async_computation | async-start | bytes 1048576 | tf_op jit(solution)/shard_map/all_to_all | solution.py:234
  10.0 0.0 copy-done.1
  10.0 2.9 %add_bitcast_fusion.own_ref = f32[64,7168]{1,0:T(8,128)} fusion(f32[1,64,7168]{2,1,0:T(8,128)} %errors_ref.1, bf16[1,64,7168]{2,1,0:T(8,128)(2,1)S(1)} %copy-done.1), kind=kLoop, calls=%fused_computation | loop fusion | flops 917504 | bytes 4587520 | tf_op jit(solution)/shard_map/add | solution.py:235
  12.9 4.8 %collective-permute-start = (f32[64,7168]{1,0:T(8,128)}, f32[64,7168]{1,0:T(8,128)}, u32[]{:S(2)}, u32[]{:S(2)}) collective-permute-start(f32[64,7168]{1,0:T(8,128)} %add_bitcast_fusion.own_ref), channel_id=1, source_target_pairs={{0,16},{16,0},{1,17},{17,1},{2,18},{18,2},{3,19},{19,3},{4,20},{20... | collective-permute-start | bytes 5505032 | tf_op jit(solution)/shard_map/ppermute | solution.py:236
  17.7 1.4 %all-to-all-done.q_ref = f32[16,16,448]{2,1,0:T(8,128)S(1)} async-done(((f32[16,16,448]{2,1,0:T(8,128)}), f32[16,16,448]{2,1,0:T(8,128)S(1)}, u32[]{:S(2)}, u32[]{:S(2)}) %all-to-all-start) | async-done | bytes 458784 | tf_op jit(solution)/shard_map/all_to_all | solution.py:234
  19.1 0.2 shard_map.51.q_ref
  19.2 2.2 %collective-permute-done.other_ref = f32[64,7168]{1,0:T(8,128)} collective-permute-done((f32[64,7168]{1,0:T(8,128)}, f32[64,7168]{1,0:T(8,128)}, u32[]{:S(2)}, u32[]{:S(2)}) %collective-permute-start) | collective-permute-done | bytes 1835040 | tf_op jit(solution)/shard_map/ppermute | solution.py:236
  21.4 5.3 %shard_map.52 = (bf16[192,7168]{1,0:T(8,128)(2,1)}, f32[16,8,128]{2,1,0:T(8,128)}) custom-call(bf16[48,7168]{1,0:T(8,128)(2,1)S(1)} %shard_map.51.q_ref, f32[64,7168]{1,0:T(8,128)} %add_bitcast_fusion.own_ref, f32[64,7168]{1,0:T(8,128)} %collective-permute-done.other_ref), custom_call_target="tpu_custom_call" | custom-call | flops 132120576 | bytes 7176192 | tf_op jit(solution)/shard_map/pallas_call | solution.py:23
  26.7 14.0 %all-to-all-start.1 = ((f32[16,8,128]{2,1,0:T(8,128)}), f32[16,8,128]{2,1,0:T(8,128)S(1)}, u32[]{:S(2)}, u32[]{:S(2)}) async-start(f32[16,8,128]{2,1,0:T(8,128)} %get-tuple-element.10), calls=%async_computation.1 | async-start | bytes 131072 | tf_op jit(solution)/shard_map/all_to_all | solution.py:260
  40.7 11.7 %all-to-all-done.1.left_ref = f32[16,8,128]{2,1,0:T(8,128)S(1)} async-done(((f32[16,8,128]{2,1,0:T(8,128)}), f32[16,8,128]{2,1,0:T(8,128)S(1)}, u32[]{:S(2)}, u32[]{:S(2)}) %all-to-all-start.1) | async-done | bytes 65568 | tf_op jit(solution)/shard_map/all_to_all | solution.py:260
  52.4 3.2 %shard_map.53 = f32[2,16,16,256]{3,2,1,0:T(8,128)S(1)} custom-call(s32[1]{0:T(128)} %bitcast.2.z0_ref, f32[16,8,128]{2,1,0:T(8,128)S(1)} %all-to-all-done.1.left_ref, bf16[192,7168]{1,0:T(8,128)(2,1)} %get-tuple-element.11.parts_ref), custom_call_target="tpu_custom_call" | custom-call | flops 132120576 | bytes 3342340 | tf_op jit(solution)/shard_map/pallas_call | solution.py:23
  55.6 15.6 %all_to_all.25 = f32[32,16,256]{2,1,0:T(8,128)S(1)} all-to-all(f32[32,16,256]{2,1,0:T(8,128)S(1)} %bitcast.13), channel_id=1, replica_groups=mesh['z8'=8,'z0'=2,'core'=2,'shard'=16] {'z0','shard'}, dimensions={0} | all-to-all | bytes 1048576 | tf_op jit(solution)/shard_map/all_to_all | solution.py:271
  71.2 0.7 shard_map.54
  71.9 0.0 copy-start
  71.9 3.9 %all-to-all-start.3 = ((f32[8,16,224]{2,1,0:T(8,128)}), f32[8,16,224]{2,1,0:T(8,128)S(1)}, u32[]{:S(2)}, u32[]{:S(2)}) async-start(f32[8,16,224]{2,1,0:T(8,128)} %get-tuple-element.12), calls=%async_computation.3 | async-start | bytes 262144 | tf_op jit(solution)/shard_map/all_to_all | solution.py:278
  75.8 5.4 %collective-permute-start.1 = (f32[16,1024]{1,0:T(8,128)S(1)}, f32[16,1024]{1,0:T(8,128)S(1)}, u32[]{:S(2)}, u32[]{:S(2)}) collective-permute-start(f32[16,1024]{1,0:T(8,128)S(1)} %get-tuple-element.13.own_ref), channel_id=1, source_target_pairs={{0,16},{16,0},{1,17},{17,1},{2,18},{18,2},{3,19},{19,3},{4,20},{20... | collective-permute-start | bytes 196616 | tf_op jit(solution)/shard_map/ppermute | solution.py:280
  81.2 0.1 pad_add_fusion.place_ref
  81.3 0.8 collective-permute-done.1.other_ref
  82.1 5.6 %shard_map.55 = (bf16[128,64]{1,0:T(8,128)(2,1)S(1)}, f32[32,32]{1,0:T(8,128)S(1)}) custom-call(s32[2]{0:T(128)S(1)} %pad_add_fusion.place_ref, f32[16,1024]{1,0:T(8,128)S(1)} %get-tuple-element.13.own_ref, f32[16,1024]{1,0:T(8,128)S(1)} %collective-permute-done.1.other_ref), custom_call_target="tpu_custom_call" | custom-call | flops 10000000 | bytes 151560 | tf_op jit(solution)/shard_map/pallas_call | solution.py:23
  87.7 2.1 %all-to-all-done.3.got_ref = f32[8,16,224]{2,1,0:T(8,128)S(1)} async-done(((f32[8,16,224]{2,1,0:T(8,128)}), f32[8,16,224]{2,1,0:T(8,128)S(1)}, u32[]{:S(2)}, u32[]{:S(2)}) %all-to-all-start.3) | async-done | bytes 114720 | tf_op jit(solution)/shard_map/all_to_all | solution.py:278
  89.8 0.1 shard_map.56
  89.9 12.7 %all_to_all.26 = f32[32,16,224]{2,1,0:T(8,128)S(1)} all-to-all(f32[32,16,224]{2,1,0:T(8,128)S(1)} %shard_map.56), channel_id=1, replica_groups=mesh['z8'=8,'z0'=2,'core'=2,'shard'=16] {'z0','shard'}, dimensions={0} | all-to-all | bytes 917504 | tf_op jit(solution)/shard_map/all_to_all | solution.py:294
  102.6 7.3 %all-gather = f32[64,16,224]{2,1,0:T(8,128)S(1)} all-gather(f32[32,16,224]{2,1,0:T(8,128)S(1)} %all_to_all.26), channel_id=2, replica_groups=mesh['z8'=8,'z0'=2,'core'=2,'shard'=16] {'core'}, dimensions={0}, use_global_device_ids=true | all-gather | bytes 1376256 | tf_op jit(solution)/shard_map/all_gather | solution.py:295
  109.9 0.0 copy-done
  109.9 2.7 %shard_map.57 = (f32[64,7168]{1,0:T(8,128)}, f32[32,448]{1,0:T(8,128)}) custom-call(s32[2]{0:T(128)S(1)} %pad_add_fusion.place_ref, f32[2,2,16,16,224]{4,3,2,1,0:T(8,128)S(1)} %bitcast.11, bf16[128,64]{1,0:T(8,128)(2,1)S(1)} %get-tuple-element.14.weights_ref, f32[32,32]{1,0:T(8,128)S(1)} %get-tuple-element.15.inverse_ref, ...), custom_call_target="tpu_custom_call" | custom-call | flops 117440512 | bytes 5582856 | tf_op jit(solution)/shard_map/pallas_call | solution.py:23
Async XLA Ops:
  0.6 9.4 %copy-start.1 = (bf16[1,64,7168]{2,1,0:T(8,128)(2,1)S(1)}, bf16[1,64,7168]{2,1,0:T(8,128)(2,1)}, u32[]{:S(2)}) copy-start(bf16[1,64,7168]{2,1,0:T(8,128)(2,1)} %grads_ref.1) | copy-start | bytes 2752516
  0.6 0.9 copy-start.2
  2.4 16.7 %all-to-all-start = ((f32[16,16,448]{2,1,0:T(8,128)}), f32[16,16,448]{2,1,0:T(8,128)S(1)}, u32[]{:S(2)}, u32[]{:S(2)}) async-start(f32[16,16,448]{2,1,0:T(8,128)} %shard_map.50), calls=%async_computation | async-start | bytes 1048576 | tf_op jit(solution)/shard_map/all_to_all | solution.py:234
  12.9 8.5 %collective-permute-start = (f32[64,7168]{1,0:T(8,128)}, f32[64,7168]{1,0:T(8,128)}, u32[]{:S(2)}, u32[]{:S(2)}) collective-permute-start(f32[64,7168]{1,0:T(8,128)} %add_bitcast_fusion.own_ref), channel_id=1, source_target_pairs={{0,16},{16,0},{1,17},{17,1},{2,18},{18,2},{3,19},{19,3},{4,20},{20... | collective-permute-start | bytes 5505032 | tf_op jit(solution)/shard_map/ppermute | solution.py:236
  26.7 25.7 %all-to-all-start.1 = ((f32[16,8,128]{2,1,0:T(8,128)}), f32[16,8,128]{2,1,0:T(8,128)S(1)}, u32[]{:S(2)}, u32[]{:S(2)}) async-start(f32[16,8,128]{2,1,0:T(8,128)} %get-tuple-element.10), calls=%async_computation.1 | async-start | bytes 131072 | tf_op jit(solution)/shard_map/all_to_all | solution.py:260
  71.9 38.0 %copy-start = (f32[1,64,7168]{2,1,0:T(8,128)S(1)}, f32[1,64,7168]{2,1,0:T(8,128)}, u32[]{:S(2)}) copy-start(f32[1,64,7168]{2,1,0:T(8,128)} %errors_ref.1) | copy-start | bytes 5505028
  71.9 17.9 %all-to-all-start.3 = ((f32[8,16,224]{2,1,0:T(8,128)}), f32[8,16,224]{2,1,0:T(8,128)S(1)}, u32[]{:S(2)}, u32[]{:S(2)}) async-start(f32[8,16,224]{2,1,0:T(8,128)} %get-tuple-element.12), calls=%async_computation.3 | async-start | bytes 262144 | tf_op jit(solution)/shard_map/all_to_all | solution.py:278
  75.8 6.3 %collective-permute-start.1 = (f32[16,1024]{1,0:T(8,128)S(1)}, f32[16,1024]{1,0:T(8,128)S(1)}, u32[]{:S(2)}, u32[]{:S(2)}) collective-permute-start(f32[16,1024]{1,0:T(8,128)S(1)} %get-tuple-element.13.own_ref), channel_id=1, source_target_pairs={{0,16},{16,0},{1,17},{17,1},{2,18},{18,2},{3,19},{19,3},{4,20},{20... | collective-permute-start | bytes 196616 | tf_op jit(solution)/shard_map/ppermute | solution.py:280

commit v4 on v3

v4 whole, which is shorter than its diff:
```python
import functools

import jax
import jax.numpy as jnp
from jax import lax
from jax.experimental import pallas as pl
from jax.experimental.pallas import tpu as pltpu
from jax.sharding import Mesh, PartitionSpec as P

F32, BF16 = jnp.float32, jnp.bfloat16
HIGH = lax.Precision.HIGHEST
PLANE = ("z0", "shard")
SWAP = [(0, 1), (1, 0)]
VMEM = pl.BlockSpec(memory_space=pltpu.VMEM)
ANY = pl.BlockSpec(memory_space=pl.ANY)
CUTS = 8
STRIDE = 4
PIECE = 224
SMEM = pl.BlockSpec(memory_space=pltpu.SMEM)


def call(body, out, operands, specs, scratch=(), out_specs=None, flops=0, limit=24):
    moved = sum(o.size * o.dtype.itemsize for o in [*operands, *out])
    return pl.pallas_call(
        body,
        out_shape=out,
        in_specs=specs,
        out_specs=out_specs or [VMEM] * len(out),
        scratch_shapes=list(scratch),
        compiler_params=pltpu.CompilerParams(vmem_limit_bytes=limit * 2**20),
        cost_estimate=pl.CostEstimate(flops=flops, bytes_accessed=moved, transcendentals=0),
    )(*operands)


def split(x, parts):
    out = []
    for _ in range(parts):
        part = x.astype(BF16)
        out.append(part)
        x = x - part.astype(F32)
    return out


def dot(a, b, dims, precision=None):
    return lax.dot_general(a, b, (dims, ((), ())), precision=precision, preferred_element_type=F32)


def ask_kernel(place_ref, q_ref, out_ref):
    half = out_ref.shape[1]
    mine = q_ref[pl.ds(pl.multiple_of(place_ref[0] * half, half), half), :]
    out_ref[...] = jnp.broadcast_to(mine[None], out_ref.shape)


def line_kernel(q_ref, out_ref):
    shards, half, share = q_ref.shape
    for g in range(shards // 2):
        pair = jnp.concatenate([q_ref[2 * g], q_ref[2 * g + 1]], axis=1)
        for i, part in enumerate(split(pair, 2)):
            out_ref[i * half : (i + 1) * half, 2 * share * g : 2 * share * (g + 1)] = part


def left_kernel(q_ref, own_ref, other_ref, parts_ref, out_ref, other_buf, sem):
    half = q_ref.shape[0] // 2
    rows, width = own_ref.shape
    step = width // CUTS
    cuts = [slice(g * step, (g + 1) * step) for g in range(CUTS)]
    loads = []
    for g, cols in enumerate(cuts):
        loads.append(pltpu.make_async_copy(other_ref.at[:, cols], other_buf.at[:, cols], sem.at[g]))
        loads[-1].start()
    total = jnp.zeros((2 * half, 2 * rows), F32)
    for g, cols in enumerate(cuts):
        loads[g].wait()
        for i, part in enumerate(split(own_ref[:, cols] + other_buf[:, cols], 2)):
            parts_ref[i * rows : (i + 1) * rows, cols] = part
        total = total + dot(q_ref[:, cols], parts_ref[:, cols], ((1,), (1,)))
    left = total[half:, rows:] + total[half:, :rows] + total[:half, rows:]
    left = left + total[:half, :rows]
    packed = jnp.concatenate([left[: half // 2], left[half // 2 :]], axis=1)
    out_ref[...] = jnp.broadcast_to(packed[None], out_ref.shape)


def right_kernel(replicas, place_ref, left_ref, parts_ref, out_ref, mine_ref):
    width = parts_ref.shape[1]
    step = width // 8
    piece = step // 4
    packed = left_ref[0]
    for z in range(1, left_ref.shape[0]):
        packed = packed + left_ref[z]
    packed = packed * (1.0 / replicas)
    rows = packed.shape[1] // 2
    half = 2 * packed.shape[0]
    left = jnp.concatenate([packed[:, :rows], packed[:, rows:]], axis=0)
    mine_ref[...] = left
    big, low = (part.astype(F32) for part in split(left, 2))
    stacked = jnp.concatenate(
        [jnp.concatenate([big, big], axis=1), jnp.concatenate([low, low], axis=1)], axis=0
    ).astype(BF16)
    mine = jnp.where(place_ref[2] == 0, left[:, : rows // 2], left[:, rows // 2 :])
    for g in range(8):
        product = dot(stacked, parts_ref[:, g * step : (g + 1) * step], ((1,), (0,)))
        right = (product[half:] + product[:half]) * (1.0 / replicas)
        for k in range(4):
            cut = right[:, k * piece : (k + 1) * piece]
            out_ref[k % 2, 2 * g + k // 2] = jnp.concatenate([cut, mine], axis=1)


def scatter_kernel(got_ref, out_ref, left_ref):
    total = jnp.zeros(got_ref.shape[2:], F32)
    for z in range(2):
        for s in range(got_ref.shape[1]):
            total = total + got_ref[z, s]
    out_ref[...] = jnp.broadcast_to(total[None, :, :PIECE], out_ref.shape)
    for g in range(got_ref.shape[1] // 2):
        four = [got_ref[k % 2, 2 * g + k // 2][:, PIECE:] for k in range(4)]
        left_ref[:, 128 * g : 128 * (g + 1)] = jnp.concatenate(four, axis=1)


def spread_kernel(got_ref, weights_ref, inverse_ref, out_ref):
    total = got_ref[0]
    for z in range(1, got_ref.shape[0]):
        total = total + got_ref[z]
    out_ref[...] = jnp.broadcast_to(total[None], out_ref.shape)


def factor_kernel(place_ref, own_ref, other_ref, mine_ref, weights_ref, inverse_ref, left_ref, both_ref):
    core, here = place_ref[0], place_ref[1]
    half, rows = mine_ref.shape
    rank = 2 * half
    first = pl.ds(pl.multiple_of(core * half, half), half)
    second = pl.ds(pl.multiple_of((1 - core) * half, half), half)
    left_ref[first, :] = own_ref[...]
    left_ref[second, :] = other_ref[...]
    pair = other_ref[:, pl.ds(pl.multiple_of(here // 2 * 2 * rows, 2 * rows), 2 * rows)]
    both_ref[first, :] = mine_ref[...]
    both_ref[second, :] = jnp.where(here % 2 == 0, pair[:, :rows], pair[:, rows:])
    parts = jnp.concatenate(split(left_ref[...], 3), axis=0)
    products = dot(parts, parts, ((1,), (1,)))
    block = lambda i, j: products[i * rank : (i + 1) * rank, j * rank : (j + 1) * rank]
    gram = block(2, 0) + block(1, 1) + block(0, 2)
    gram = gram + (block(1, 0) + block(0, 1))
    gram = gram + block(0, 0)
    at_row = lax.broadcasted_iota(jnp.int32, (rank, 4 * rank), 0)
    at_lane = lax.broadcasted_iota(jnp.int32, (rank, 4 * rank), 1)
    work = jnp.concatenate([gram, jnp.zeros((rank, rank), F32), both_ref[...]], axis=1)
    work = jnp.where(at_lane == at_row + rank, 1.0, work)
    for start in range(0, rank, STRIDE):
        columns = [jnp.broadcast_to(work[:, j : j + 1], work.shape) for j in range(start, start + STRIDE)]
        for t in range(STRIDE):
            j = start + t
            factor = jnp.where(at_row > j, columns[t] * (1.0 / columns[t][j : j + 1]), 0.0)
            for u in range(t + 1, STRIDE):
                columns[u] = columns[u] - factor * columns[u][j : j + 1]
            work = work - factor * work[j : j + 1]
    pivots = jnp.sum(jnp.where(at_lane == at_row, work, 0.0), axis=1, keepdims=True)
    work = work / jnp.sqrt(pivots)
    inverse = work[:, rank : 2 * rank]
    mine = dot(work[:, 2 * rank :], inverse, ((0,), (0,)), HIGH)
    big, low = (part.astype(F32) for part in split(mine, 2))
    weights_ref[...] = jnp.concatenate(
        [jnp.concatenate([big, big], axis=1), jnp.concatenate([low, low], axis=1)], axis=0
    ).astype(BF16)
    inverse_ref[...] = inverse


def final_kernel(place_ref, raw_ref, weights_ref, inverse_ref, grads_ref, errors_ref, out_ref, q_ref, hold_ref, sem):
    here = place_ref[1]
    rows, width = hold_ref.shape
    step = 4 * PIECE
    copies = []
    for g in range(width // step):
        cols = slice(g * step, (g + 1) * step)
        raw = jnp.concatenate(
            [
                jnp.concatenate([raw_ref[core, k % 2, 2 * g + k // 2] for k in range(4)], axis=1)
                for core in range(2)
            ],
            axis=0,
        )
        product = dot(weights_ref[...], jnp.concatenate(split(raw, 2), axis=0), ((1,), (0,)))
        merged = grads_ref[0, :, cols].astype(F32) + errors_ref[0, :, cols]
        hold_ref[:, cols] = merged - (product[rows:] + product[:rows])
        copy = pltpu.make_async_copy(hold_ref.at[:, cols], out_ref.at[:, cols], sem.at[g])
        copy.start()
        copies.append(copy)
    raw = jnp.concatenate(
        [
            jnp.concatenate([raw_ref[core, 0, here], raw_ref[core, 1, here]], axis=1)
            for core in range(2)
        ],
        axis=0,
    )
    q_ref[...] = dot(inverse_ref[...], raw, ((1,), (0,)), HIGH)
    for copy in copies:
        copy.wait()


def to_all(block, peers, axis):
    return lax.all_to_all(jnp.broadcast_to(block, (peers, *block.shape)), axis, 0, 0)


def per_device(grads, errors, q_prev):
    shape = jax.ShapeDtypeStruct
    rows, width = errors.shape[1:]
    share, rank = q_prev.shape
    half = rank // 2
    place = jnp.stack([lax.axis_index(axis) for axis in ("core", "shard", "z0")])
    replicas = 32

    (own_q,) = call(
        ask_kernel,
        [shape((16, half, share), F32)],
        [place, q_prev.T],
        [SMEM, VMEM],
    )
    all_q = lax.all_to_all(own_q, "shard", 0, 0)
    merged = grads[0].astype(F32) + errors[0]
    other = lax.ppermute(merged, "core", SWAP)
    (all_q,) = call(
        line_kernel,
        [shape((2 * half, width), BF16)],
        [all_q],
        [VMEM],
        flops=10**11,
    )
    parts, left = call(
        left_kernel,
        [shape((2 * rows, width), BF16), shape((16, 8, 128), F32)],
        [all_q, merged, other],
        [VMEM, VMEM, ANY],
        [pltpu.VMEM((rows, width), F32), pltpu.SemaphoreType.DMA((CUTS,))],
        flops=2 * 32 * 128 * width,
    )
    left = lax.all_to_all(left, ("z8", "z0"), 0, 0)

    pieces, mine = call(
        functools.partial(right_kernel, replicas),
        [shape((2, 16, half, 256), F32), shape((half, rows), F32)],
        [place, left, parts],
        [SMEM, VMEM, VMEM],
        flops=2 * 32 * 128 * width,
    )
    pieces = lax.all_to_all(pieces.reshape(32, half, 256), PLANE, 0, 0).reshape(pieces.shape)
    right, left_own = call(
        scatter_kernel,
        [shape((8, half, PIECE), F32), shape((half, 16 * rows), F32)],
        [pieces],
        [VMEM],
    )
    right = lax.all_to_all(right, "z8", 0, 0)

    left_other = lax.ppermute(left_own, "core", SWAP)
    weights, inverse = call(
        factor_kernel,
        [shape((2 * rows, 2 * rank), BF16), shape((rank, rank), F32)],
        [place, left_own, left_other, mine],
        [SMEM] + [VMEM] * 3,
        [pltpu.VMEM((rank, 16 * rows), F32), pltpu.VMEM((rank, rows), F32)],
        flops=10**7,
    )

    (raw,) = call(
        spread_kernel, [shape((32, half, PIECE), F32)], [right, weights, inverse], [VMEM] * 3
    )
    raw = lax.all_to_all(raw, PLANE, 0, 0)
    raw = lax.all_gather(raw, "core").reshape(2, 2, 16, half, PIECE)
    out, q_new = call(
        final_kernel,
        [shape((rows, width), F32), shape((rank, share), F32)],
        [place, raw, weights, inverse, grads, errors],
        [SMEM] + [VMEM] * 5,
        [pltpu.VMEM((rows, width), F32), pltpu.SemaphoreType.DMA((8,))],
        [pl.BlockSpec(memory_space=pl.ANY), VMEM],
        flops=2 * 128 * 64 * width,
    )
    return (out[None], q_new.T)


def solution(mesh):
    parts = Mesh(mesh.devices.reshape(8, 2, 2, 16), ("z8", "z0", "core", "shard"))
    dp = ("z8", "z0", "core")
    in_specs = (P(dp, "shard", None), P(dp, "shard", None), P("shard", None))
    out_specs = (P(dp, "shard", None), P("shard", None))
    return jax.shard_map(
        per_device, mesh=parts, in_specs=in_specs, out_specs=out_specs, check_vma=False
    )
```

time: 113 us -> 107 us (0.947)
  blocking collectives: 35.6 us -> 61.4 us
  starting transfers between devices: 35.7 us -> 21.4 us
  waiting for transfers between devices: 18.1 us -> 9.02 us
  Pallas kernels: 18.6 us -> 11.7 us
  other arithmetic: 2.96 us -> 1.73 us
    all_to_all x0 -> x1, blocking collectives: none -> 26.9 us  [per_device(): left = lax.all_to_all(left, ('z8', 'z0'), 0, 0)]
    all_to_all x1 -> x0, starting transfers between devices: 14 us -> none  [per_device(): left = lax.all_to_all(left, ('z8', 'z0'), 0, 0)]
    all_to_all x1 -> x0, waiting for transfers between devices: 11.7 us -> none  [per_device(): left = lax.all_to_all(left, ('z8', 'z0'), 0, 0)]
    pallas_call x8, Pallas kernels: 18.6 us -> 11.7 us  [call(): pl.pallas_call(body, out_shape=out, in_specs=specs, out_specs=out_specs o...]
    all_to_all x1, waiting for transfers between devices: 2.11 us -> 4.76 us  [per_device(): right = lax.all_to_all(right, 'z8', 0, 0)]
    all_to_all x1, blocking collectives: 15.6 us -> 14.1 us  [per_device(): lax.all_to_all(pieces.reshape(32, half, 256), PLANE, 0, 0)]
    ppermute x1, waiting for transfers between devices: 2.15 us -> 0.77 us  [per_device(): other = lax.ppermute(merged, 'core', SWAP)]
    add x1, other arithmetic: 2.88 us -> 1.66 us  [per_device(): merged = grads[0].astype(F32) + errors[0]]
  transfers between devices with their start and end apart: 5 -> 4, of which waited for: 5 -> 4; matrix products, arithmetic and copies ran while one was open for 3% -> 2% of each run, Pallas kernels for 5% -> 3%
where the time goes in v4:
time: 107 us
  blocking collectives  61.4 us (57%)
  starting transfers between devices  21.4 us (20%)
  Pallas kernels  11.7 us (11%)
  waiting for transfers between devices  9.02 us (8%)
  other arithmetic  1.73 us (2%)
    all_to_all x1, blocking collectives, per_device(): left = lax.all_to_all(left, ('z8', 'z0'), 0, 0)  26.9 us
    all_to_all x1, blocking collectives, per_device(): lax.all_to_all(pieces.reshape(32, half, 256), PLANE, 0, 0)  14.1 us
    all_to_all x1, blocking collectives, per_device(): raw = lax.all_to_all(raw, PLANE, 0, 0)  12.5 us
    pallas_call x8, Pallas kernels, call(): pl.pallas_call(body, out_shape=out, in_specs=specs, out_specs=out_specs o...  11.7 us
    all_gather x1, blocking collectives, per_device(): raw = lax.all_gather(raw, 'core').reshape(2, 2, 16, half, PIECE)  7.98 us
    all_to_all x1, starting transfers between devices, per_device(): all_q = lax.all_to_all(own_q, 'shard', 0, 0)  7.58 us
    ppermute x1, starting transfers between devices, per_device(): left_other = lax.ppermute(left_own, 'core', SWAP)  5.38 us
    ppermute x1, starting transfers between devices, per_device(): other = lax.ppermute(merged, 'core', SWAP)  4.78 us
  transfers between devices with their start and end apart: 4, of which 4 were waited for; matrix products, arithmetic and copies ran while one was open for 2% of the time, Pallas kernels for 3%

profile of v4, /device:TPU:1, one launch (start us, length us, event | category | flops | bytes accessed | tf_op | source)
XLA Modules:
  0.0 106.9 jit_solution(6934958157826851810)
XLA Ops:
  0.6 0.0 copy-start.1
  0.6 0.1 pad_add_fusion.place_ref
  0.7 0.0 copy-start.2
  0.7 0.9 copy-done.2
  1.6 1.4 %shard_map.50 = f32[16,16,448]{2,1,0:T(8,128)} custom-call(s32[3]{0:T(128)S(1)} %pad_add_fusion.place_ref, f32[32,448]{1,0:T(8,128)S(1)} %bitcast.14), custom_call_target="tpu_custom_call" | custom-call | bytes 516108 | tf_op jit(solution)/shard_map/pallas_call | solution.py:24
  3.0 7.6 %all-to-all-start = ((f32[16,16,448]{2,1,0:T(8,128)}), f32[16,16,448]{2,1,0:T(8,128)S(1)}, u32[]{:S(2)}, u32[]{:S(2)}) async-start(f32[16,16,448]{2,1,0:T(8,128)} %shard_map.50), calls=%async_computation | async-start | bytes 1048576 | tf_op jit(solution)/shard_map/all_to_all | solution.py:216
  10.6 0.0 copy-done.1
  10.6 1.7 %add_bitcast_fusion.own_ref = f32[64,7168]{1,0:T(8,128)S(1)} fusion(f32[1,64,7168]{2,1,0:T(8,128)} %errors_ref.1, bf16[1,64,7168]{2,1,0:T(8,128)(2,1)S(1)} %copy-done.1), kind=kLoop, calls=%fused_computation | loop fusion | flops 917504 | bytes 4587520 | tf_op jit(solution)/shard_map/add | solution.py:217
  12.3 4.8 %collective-permute-start = (f32[64,7168]{1,0:T(8,128)S(1)}, f32[64,7168]{1,0:T(8,128)}, u32[]{:S(2)}, u32[]{:S(2)}) collective-permute-start(f32[64,7168]{1,0:T(8,128)S(1)} %add_bitcast_fusion.own_ref), channel_id=1, source_target_pairs={{0,16},{16,0},{1,17},{17,1},{2,18},{18,2},{3,19},{19,3},{4,20},{20... | collective-permute-start | bytes 5505032 | tf_op jit(solution)/shard_map/ppermute | solution.py:218
  17.1 2.6 %all-to-all-done.q_ref = f32[16,16,448]{2,1,0:T(8,128)S(1)} async-done(((f32[16,16,448]{2,1,0:T(8,128)}), f32[16,16,448]{2,1,0:T(8,128)S(1)}, u32[]{:S(2)}, u32[]{:S(2)}) %all-to-all-start) | async-done | bytes 458784 | tf_op jit(solution)/shard_map/all_to_all | solution.py:216
  19.7 0.1 shard_map.51.q_ref
  19.8 0.8 collective-permute-done.other_ref
  20.6 3.0 %shard_map.52 = (bf16[128,7168]{1,0:T(8,128)(2,1)S(1)}, f32[16,8,128]{2,1,0:T(8,128)S(1)}) custom-call(bf16[32,7168]{1,0:T(8,128)(2,1)S(1)} %shard_map.51.q_ref, f32[64,7168]{1,0:T(8,128)S(1)} %add_bitcast_fusion.own_ref, f32[64,7168]{1,0:T(8,128)} %collective-permute-done.other_ref), custom_call_target="tpu_custom_call" | custom-call | flops 58720256 | bytes 6029312 | tf_op jit(solution)/shard_map/pallas_call | solution.py:24
  23.6 26.9 %all_to_all.25.left_ref = f32[16,8,128]{2,1,0:T(8,128)S(1)} all-to-all(f32[16,8,128]{2,1,0:T(8,128)S(1)} %get-tuple-element.12), channel_id=1, replica_groups=mesh['z8'=8,'z0'=2,'core'=2,'shard'=16] {'z8','z0'}, dimensions={0} | all-to-all | bytes 131072 | tf_op jit(solution)/shard_map/all_to_all | solution.py:234
  50.4 1.2 %shard_map.53 = (f32[2,16,16,256]{3,2,1,0:T(8,128)S(1)}, f32[16,64]{1,0:T(8,128)S(1)}) custom-call(s32[3]{0:T(128)S(1)} %pad_add_fusion.place_ref, f32[16,8,128]{2,1,0:T(8,128)S(1)} %all_to_all.25.left_ref, bf16[128,7168]{1,0:T(8,128)(2,1)S(1)} %get-tuple-element.13.parts_ref), custom_call_target="tpu_custom_call" | custom-call | flops 58720256 | bytes 2428940 | tf_op jit(solution)/shard_map/pallas_call | solution.py:24
  51.6 14.1 %all_to_all.26 = f32[32,16,256]{2,1,0:T(8,128)S(1)} all-to-all(f32[32,16,256]{2,1,0:T(8,128)S(1)} %bitcast.13), channel_id=1, replica_groups=mesh['z8'=8,'z0'=2,'core'=2,'shard'=16] {'z0','shard'}, dimensions={0} | all-to-all | bytes 1048576 | tf_op jit(solution)/shard_map/all_to_all | solution.py:243
  65.7 0.7 shard_map.54
  66.4 0.0 copy-start
  66.4 3.6 %all-to-all-start.3 = ((f32[8,16,224]{2,1,0:T(8,128)}), f32[8,16,224]{2,1,0:T(8,128)S(1)}, u32[]{:S(2)}, u32[]{:S(2)}) async-start(f32[8,16,224]{2,1,0:T(8,128)} %get-tuple-element.15), calls=%async_computation.3 | async-start | bytes 262144 | tf_op jit(solution)/shard_map/all_to_all | solution.py:250
  70.0 5.4 %collective-permute-start.1 = (f32[16,1024]{1,0:T(8,128)S(1)}, f32[16,1024]{1,0:T(8,128)S(1)}, u32[]{:S(2)}, u32[]{:S(2)}) collective-permute-start(f32[16,1024]{1,0:T(8,128)S(1)} %get-tuple-element.16.own_ref), channel_id=1, source_target_pairs={{0,16},{16,0},{1,17},{17,1},{2,18},{18,2},{3,19},{19,3},{4,20},{20... | collective-permute-start | bytes 196616 | tf_op jit(solution)/shard_map/ppermute | solution.py:252
  75.4 0.9 collective-permute-done.1.other_ref
  76.3 2.6 %shard_map.55 = (bf16[128,64]{1,0:T(8,128)(2,1)S(1)}, f32[32,32]{1,0:T(8,128)S(1)}) custom-call(s32[3]{0:T(128)S(1)} %pad_add_fusion.place_ref, f32[16,1024]{1,0:T(8,128)S(1)} %get-tuple-element.16.own_ref, f32[16,1024]{1,0:T(8,128)S(1)} %collective-permute-done.1.other_ref, f32[16,64]{1,0:T(8,128)S(1)} %get-tuple-element.17.mine_ref), custom_call_target="tpu_custom_call" | custom-call | flops 10000000 | bytes 155660 | tf_op jit(solution)/shard_map/pallas_call | solution.py:24
  78.9 4.8 %all-to-all-done.3.got_ref = f32[8,16,224]{2,1,0:T(8,128)S(1)} async-done(((f32[8,16,224]{2,1,0:T(8,128)}), f32[8,16,224]{2,1,0:T(8,128)S(1)}, u32[]{:S(2)}, u32[]{:S(2)}) %all-to-all-start.3) | async-done | bytes 114720 | tf_op jit(solution)/shard_map/all_to_all | solution.py:250
  83.6 0.1 shard_map.56
  83.7 12.5 %all_to_all.27 = f32[32,16,224]{2,1,0:T(8,128)S(1)} all-to-all(f32[32,16,224]{2,1,0:T(8,128)S(1)} %shard_map.56), channel_id=1, replica_groups=mesh['z8'=8,'z0'=2,'core'=2,'shard'=16] {'z0','shard'}, dimensions={0} | all-to-all | bytes 917504 | tf_op jit(solution)/shard_map/all_to_all | solution.py:265
  96.1 8.0 %all-gather = f32[64,16,224]{2,1,0:T(8,128)S(1)} all-gather(f32[32,16,224]{2,1,0:T(8,128)S(1)} %all_to_all.27), channel_id=2, replica_groups=mesh['z8'=8,'z0'=2,'core'=2,'shard'=16] {'core'}, dimensions={0}, use_global_device_ids=true | all-gather | bytes 1376256 | tf_op jit(solution)/shard_map/all_gather | solution.py:266
  104.1 0.0 copy-done
  104.1 2.7 %shard_map.57 = (f32[64,7168]{1,0:T(8,128)}, f32[32,448]{1,0:T(8,128)}) custom-call(s32[3]{0:T(128)S(1)} %pad_add_fusion.place_ref, f32[2,2,16,16,224]{4,3,2,1,0:T(8,128)S(1)} %bitcast.11, bf16[128,64]{1,0:T(8,128)(2,1)S(1)} %get-tuple-element.18.weights_ref, f32[32,32]{1,0:T(8,128)S(1)} %get-tuple-element.19.inverse_ref, ...), custom_call_target="tpu_custom_call" | custom-call | flops 117440512 | bytes 5582860 | tf_op jit(solution)/shard_map/pallas_call | solution.py:24
Async XLA Ops:
  0.6 10.0 %copy-start.1 = (bf16[1,64,7168]{2,1,0:T(8,128)(2,1)S(1)}, bf16[1,64,7168]{2,1,0:T(8,128)(2,1)}, u32[]{:S(2)}) copy-start(bf16[1,64,7168]{2,1,0:T(8,128)(2,1)} %grads_ref.1) | copy-start | bytes 2752516
  0.7 0.9 copy-start.2
  3.0 16.7 %all-to-all-start = ((f32[16,16,448]{2,1,0:T(8,128)}), f32[16,16,448]{2,1,0:T(8,128)S(1)}, u32[]{:S(2)}, u32[]{:S(2)}) async-start(f32[16,16,448]{2,1,0:T(8,128)} %shard_map.50), calls=%async_computation | async-start | bytes 1048576 | tf_op jit(solution)/shard_map/all_to_all | solution.py:216
  12.3 8.3 %collective-permute-start = (f32[64,7168]{1,0:T(8,128)S(1)}, f32[64,7168]{1,0:T(8,128)}, u32[]{:S(2)}, u32[]{:S(2)}) collective-permute-start(f32[64,7168]{1,0:T(8,128)S(1)} %add_bitcast_fusion.own_ref), channel_id=1, source_target_pairs={{0,16},{16,0},{1,17},{17,1},{2,18},{18,2},{3,19},{19,3},{4,20},{20... | collective-permute-start | bytes 5505032 | tf_op jit(solution)/shard_map/ppermute | solution.py:218
  66.4 37.7 %copy-start = (f32[1,64,7168]{2,1,0:T(8,128)S(1)}, f32[1,64,7168]{2,1,0:T(8,128)}, u32[]{:S(2)}) copy-start(f32[1,64,7168]{2,1,0:T(8,128)} %errors_ref.1) | copy-start | bytes 5505028
  66.4 17.2 %all-to-all-start.3 = ((f32[8,16,224]{2,1,0:T(8,128)}), f32[8,16,224]{2,1,0:T(8,128)S(1)}, u32[]{:S(2)}, u32[]{:S(2)}) async-start(f32[8,16,224]{2,1,0:T(8,128)} %get-tuple-element.15), calls=%async_computation.3 | async-start | bytes 262144 | tf_op jit(solution)/shard_map/all_to_all | solution.py:250
  70.0 6.3 %collective-permute-start.1 = (f32[16,1024]{1,0:T(8,128)S(1)}, f32[16,1024]{1,0:T(8,128)S(1)}, u32[]{:S(2)}, u32[]{:S(2)}) collective-permute-start(f32[16,1024]{1,0:T(8,128)S(1)} %get-tuple-element.16.own_ref), channel_id=1, source_target_pairs={{0,16},{16,0},{1,17},{17,1},{2,18},{18,2},{3,19},{19,3},{4,20},{20... | collective-permute-start | bytes 196616 | tf_op jit(solution)/shard_map/ppermute | solution.py:252

commit v5 on v4

--- a/solution.py
+++ b/solution.py
@@ -13,9 +13,8 @@
 SWAP = [(0, 1), (1, 0)]
 VMEM = pl.BlockSpec(memory_space=pltpu.VMEM)
 ANY = pl.BlockSpec(memory_space=pl.ANY)
-CUTS = 8
+CUTS = 7
 STRIDE = 4
-PIECE = 224
 SMEM = pl.BlockSpec(memory_space=pltpu.SMEM)
 
 
@@ -46,17 +45,26 @@
 
 
 def ask_kernel(place_ref, q_ref, out_ref):
-    half = out_ref.shape[1]
+    half = q_ref.shape[0] // 2
     mine = q_ref[pl.ds(pl.multiple_of(place_ref[0] * half, half), half), :]
-    out_ref[...] = jnp.broadcast_to(mine[None], out_ref.shape)
+    packed = jnp.concatenate([mine[: half // 2], mine[half // 2 :]], axis=1)
+    out_ref[...] = jnp.broadcast_to(packed[None], out_ref.shape)
 
 
 def line_kernel(q_ref, out_ref):
-    shards, half, share = q_ref.shape
+    shards, low, span = q_ref.shape
+    share = span // 2
     for g in range(shards // 2):
-        pair = jnp.concatenate([q_ref[2 * g], q_ref[2 * g + 1]], axis=1)
+        a, b = q_ref[2 * g], q_ref[2 * g + 1]
+        pair = jnp.concatenate(
+            [
+                jnp.concatenate([a[:, :share], b[:, :share]], axis=1),
+                jnp.concatenate([a[:, share:], b[:, share:]], axis=1),
+            ],
+            axis=0,
+        )
         for i, part in enumerate(split(pair, 2)):
-            out_ref[i * half : (i + 1) * half, 2 * share * g : 2 * share * (g + 1)] = part
+            out_ref[2 * low * i : 2 * low * (i + 1), span * g : span * (g + 1)] = part
 
 
 def left_kernel(q_ref, own_ref, other_ref, parts_ref, out_ref, other_buf, sem):
@@ -83,7 +91,7 @@
 def right_kernel(replicas, place_ref, left_ref, parts_ref, out_ref, mine_ref):
     width = parts_ref.shape[1]
     step = width // 8
-    piece = step // 4
+    share = step // 2
     packed = left_ref[0]
     for z in range(1, left_ref.shape[0]):
         packed = packed + left_ref[z]
@@ -96,24 +104,30 @@
     stacked = jnp.concatenate(
         [jnp.concatenate([big, big], axis=1), jnp.concatenate([low, low], axis=1)], axis=0
     ).astype(BF16)
-    mine = jnp.where(place_ref[2] == 0, left[:, : rows // 2], left[:, rows // 2 :])
+    mine = jnp.where(place_ref[2] == 0, left[: half // 2], left[half // 2 :])
+    mine = jnp.concatenate([mine, mine], axis=0)
     for g in range(8):
         product = dot(stacked, parts_ref[:, g * step : (g + 1) * step], ((1,), (0,)))
         right = (product[half:] + product[:half]) * (1.0 / replicas)
-        for k in range(4):
-            cut = right[:, k * piece : (k + 1) * piece]
-            out_ref[k % 2, 2 * g + k // 2] = jnp.concatenate([cut, mine], axis=1)
+        for k in range(2):
+            cut = jnp.concatenate([right[:, k * share : (k + 1) * share], mine], axis=1)
+            out_ref[0, 2 * g + k] = cut[: half // 2]
+            out_ref[1, 2 * g + k] = cut[half // 2 :]
 
 
 def scatter_kernel(got_ref, out_ref, left_ref):
-    total = jnp.zeros(got_ref.shape[2:], F32)
+    total = got_ref[0, 0]
+    for s in range(1, got_ref.shape[1]):
+        total = total + got_ref[0, s]
+    for s in range(got_ref.shape[1]):
+        total = total + got_ref[1, s]
+    share = out_ref.shape[2]
+    out_ref[...] = jnp.broadcast_to(total[None, :, :share], out_ref.shape)
+    low, rows = got_ref.shape[2], got_ref.shape[3] - share
     for z in range(2):
-        for s in range(got_ref.shape[1]):
-            total = total + got_ref[z, s]
-    out_ref[...] = jnp.broadcast_to(total[None, :, :PIECE], out_ref.shape)
-    for g in range(got_ref.shape[1] // 2):
-        four = [got_ref[k % 2, 2 * g + k // 2][:, PIECE:] for k in range(4)]
-        left_ref[:, 128 * g : 128 * (g + 1)] = jnp.concatenate(four, axis=1)
+        for g in range(got_ref.shape[1] // 2):
+            pair = [got_ref[z, 2 * g + k][:, share:] for k in range(2)]
+            left_ref[low * z : low * (z + 1), 2 * rows * g : 2 * rows * (g + 1)] = jnp.concatenate(pair, axis=1)
 
 
 def spread_kernel(got_ref, weights_ref, inverse_ref, out_ref):
@@ -163,40 +177,31 @@
     inverse_ref[...] = inverse
 
 
-def final_kernel(place_ref, raw_ref, weights_ref, inverse_ref, grads_ref, errors_ref, out_ref, q_ref, hold_ref, sem):
+def final_kernel(place_ref, raw_ref, weights_ref, inverse_ref, merged_ref, out_ref, q_ref, hold_ref, sem):
     here = place_ref[1]
     rows, width = hold_ref.shape
-    step = 4 * PIECE
+    share = raw_ref.shape[-1]
+    step = 2 * share
     copies = []
     for g in range(width // step):
         cols = slice(g * step, (g + 1) * step)
         raw = jnp.concatenate(
             [
-                jnp.concatenate([raw_ref[core, k % 2, 2 * g + k // 2] for k in range(4)], axis=1)
+                jnp.concatenate([raw_ref[core, z, 2 * g], raw_ref[core, z, 2 * g + 1]], axis=1)
                 for core in range(2)
+                for z in range(2)
             ],
             axis=0,
         )
         product = dot(weights_ref[...], jnp.concatenate(split(raw, 2), axis=0), ((1,), (0,)))
-        merged = grads_ref[0, :, cols].astype(F32) + errors_ref[0, :, cols]
-        hold_ref[:, cols] = merged - (product[rows:] + product[:rows])
+        hold_ref[:, cols] = merged_ref[:, cols] - (product[rows:] + product[:rows])
         copy = pltpu.make_async_copy(hold_ref.at[:, cols], out_ref.at[:, cols], sem.at[g])
         copy.start()
         copies.append(copy)
-    raw = jnp.concatenate(
-        [
-            jnp.concatenate([raw_ref[core, 0, here], raw_ref[core, 1, here]], axis=1)
-            for core in range(2)
-        ],
-        axis=0,
-    )
+    raw = jnp.concatenate([raw_ref[core, z, here] for core in range(2) for z in range(2)], axis=0)
     q_ref[...] = dot(inverse_ref[...], raw, ((1,), (0,)), HIGH)
     for copy in copies:
         copy.wait()
-
-
-def to_all(block, peers, axis):
-    return lax.all_to_all(jnp.broadcast_to(block, (peers, *block.shape)), axis, 0, 0)
 
 
 def per_device(grads, errors, q_prev):
@@ -209,7 +214,7 @@
 
     (own_q,) = call(
         ask_kernel,
-        [shape((16, half, share), F32)],
+        [shape((16, half // 2, 2 * share), F32)],
         [place, q_prev.T],
         [SMEM, VMEM],
     )
@@ -235,15 +240,15 @@
 
     pieces, mine = call(
         functools.partial(right_kernel, replicas),
-        [shape((2, 16, half, 256), F32), shape((half, rows), F32)],
+        [shape((2, 16, half // 2, 512), F32), shape((half, rows), F32)],
         [place, left, parts],
         [SMEM, VMEM, VMEM],
         flops=2 * 32 * 128 * width,
     )
-    pieces = lax.all_to_all(pieces.reshape(32, half, 256), PLANE, 0, 0).reshape(pieces.shape)
+    pieces = lax.all_to_all(pieces.reshape(32, half // 2, 512), PLANE, 0, 0).reshape(pieces.shape)
     right, left_own = call(
         scatter_kernel,
-        [shape((8, half, PIECE), F32), shape((half, 16 * rows), F32)],
+        [shape((8, half // 2, share), F32), shape((half, 16 * rows), F32)],
         [pieces],
         [VMEM],
     )
@@ -260,15 +265,15 @@
     )
 
     (raw,) = call(
-        spread_kernel, [shape((32, half, PIECE), F32)], [right, weights, inverse], [VMEM] * 3
+        spread_kernel, [shape((32, half // 2, share), F32)], [right, weights, inverse], [VMEM] * 3
     )
     raw = lax.all_to_all(raw, PLANE, 0, 0)
-    raw = lax.all_gather(raw, "core").reshape(2, 2, 16, half, PIECE)
+    raw = lax.all_gather(raw, "core").reshape(2, 2, 16, half // 2, share)
     out, q_new = call(
         final_kernel,
         [shape((rows, width), F32), shape((rank, share), F32)],
-        [place, raw, weights, inverse, grads, errors],
-        [SMEM] + [VMEM] * 5,
+        [place, raw, weights, inverse, merged],
+        [SMEM] + [VMEM] * 4,
         [pltpu.VMEM((rows, width), F32), pltpu.SemaphoreType.DMA((8,))],
         [pl.BlockSpec(memory_space=pl.ANY), VMEM],
         flops=2 * 128 * 64 * width,

time: 107 us -> 107 us (level)
  no operation moved by 1% of the time
where the time goes in v5:
time: 107 us
  blocking collectives  61.1 us (57%)
  starting transfers between devices  21.5 us (20%)
  Pallas kernels  11.1 us (10%)
  waiting for transfers between devices  9.43 us (9%)
  other arithmetic  1.79 us (2%)
    all_to_all x1, blocking collectives, per_device(): left = lax.all_to_all(left, ('z8', 'z0'), 0, 0)  26 us
    all_to_all x1, blocking collectives, per_device(): lax.all_to_all(pieces.reshape(32, half // 2, 512), PLANE, 0, 0)  15.1 us
    all_to_all x1, blocking collectives, per_device(): raw = lax.all_to_all(raw, PLANE, 0, 0)  12.7 us
    pallas_call x8, Pallas kernels, call(): pl.pallas_call(body, out_shape=out, in_specs=specs, out_specs=out_specs o...  11.1 us
    all_to_all x1, starting transfers between devices, per_device(): all_q = lax.all_to_all(own_q, 'shard', 0, 0)  7.58 us
    all_gather x1, blocking collectives, per_device(): raw = lax.all_gather(raw, 'core').reshape(2, 2, 16, half // 2, share)  7.28 us
    ppermute x1, starting transfers between devices, per_device(): left_other = lax.ppermute(left_own, 'core', SWAP)  5.36 us
    all_to_all x1, waiting for transfers between devices, per_device(): right = lax.all_to_all(right, 'z8', 0, 0)  5.18 us
  transfers between devices with their start and end apart: 4, of which 4 were waited for; matrix products, arithmetic and copies ran while one was open for 2% of the time, Pallas kernels for 3%

profile of v5, /device:TPU:1, one launch (start us, length us, event | category | flops | bytes accessed | tf_op | source)
XLA Modules:
  0.0 106.5 jit_solution(3131667763543719049)
XLA Ops:
  0.6 0.1 pad_add_fusion.place_ref
  0.7 0.0 copy-start
  0.7 0.8 copy-done
  1.6 0.0 copy-start.1
  1.6 1.4 %shard_map.50 = f32[16,8,896]{2,1,0:T(8,128)} custom-call(s32[3]{0:T(128)S(1)} %pad_add_fusion.place_ref, f32[32,448]{1,0:T(8,128)S(1)} %bitcast.14), custom_call_target="tpu_custom_call" | custom-call | bytes 516108 | tf_op jit(solution)/shard_map/pallas_call | solution.py:23
  3.0 7.6 %all-to-all-start = ((f32[16,8,896]{2,1,0:T(8,128)}), f32[16,8,896]{2,1,0:T(8,128)S(1)}, u32[]{:S(2)}, u32[]{:S(2)}) async-start(f32[16,8,896]{2,1,0:T(8,128)} %shard_map.50), calls=%async_computation | async-start | bytes 917504 | tf_op jit(solution)/shard_map/all_to_all | solution.py:221
  10.5 0.0 copy-done.1
  10.6 1.7 %add_bitcast_fusion.own_ref.merged_ref = f32[64,7168]{1,0:T(8,128)S(1)} fusion(f32[1,64,7168]{2,1,0:T(8,128)} %param.4, bf16[1,64,7168]{2,1,0:T(8,128)(2,1)S(1)} %copy-done.1), kind=kLoop, calls=%fused_computation | loop fusion | flops 917504 | bytes 4587520 | tf_op jit(solution)/shard_map/add | solution.py:222
  12.3 4.8 %collective-permute-start = (f32[64,7168]{1,0:T(8,128)S(1)}, f32[64,7168]{1,0:T(8,128)}, u32[]{:S(2)}, u32[]{:S(2)}) collective-permute-start(f32[64,7168]{1,0:T(8,128)S(1)} %add_bitcast_fusion.own_ref.merged_ref), channel_id=1, source_target_pairs={{0,16},{16,0},{1,17},{17,1},{2,18},{18,2},{3,19},{19,3},{4,20},{20... | collective-permute-start | bytes 5505032 | tf_op jit(solution)/shard_map/ppermute | solution.py:223
  17.0 2.1 %all-to-all-done.q_ref = f32[16,8,896]{2,1,0:T(8,128)S(1)} async-done(((f32[16,8,896]{2,1,0:T(8,128)}), f32[16,8,896]{2,1,0:T(8,128)S(1)}, u32[]{:S(2)}, u32[]{:S(2)}) %all-to-all-start) | async-done | bytes 458784 | tf_op jit(solution)/shard_map/all_to_all | solution.py:221
  19.2 0.1 shard_map.51.q_ref
  19.3 1.2 %collective-permute-done.other_ref = f32[64,7168]{1,0:T(8,128)} collective-permute-done((f32[64,7168]{1,0:T(8,128)S(1)}, f32[64,7168]{1,0:T(8,128)}, u32[]{:S(2)}, u32[]{:S(2)}) %collective-permute-start) | collective-permute-done | bytes 1835040 | tf_op jit(solution)/shard_map/ppermute | solution.py:223
  20.6 2.4 %shard_map.52 = (bf16[128,7168]{1,0:T(8,128)(2,1)S(1)}, f32[16,8,128]{2,1,0:T(8,128)S(1)}) custom-call(bf16[32,7168]{1,0:T(8,128)(2,1)S(1)} %shard_map.51.q_ref, f32[64,7168]{1,0:T(8,128)S(1)} %add_bitcast_fusion.own_ref.merged_ref, f32[64,7168]{1,0:T(8,128)} %collective-permute-done.other_ref), custom_call_target="tpu_custom_call" | custom-call | flops 58720256 | bytes 6029312 | tf_op jit(solution)/shard_map/pallas_call | solution.py:23
  23.0 26.0 %all_to_all.25.left_ref = f32[16,8,128]{2,1,0:T(8,128)S(1)} all-to-all(f32[16,8,128]{2,1,0:T(8,128)S(1)} %get-tuple-element.12), channel_id=1, replica_groups=mesh['z8'=8,'z0'=2,'core'=2,'shard'=16] {'z8','z0'}, dimensions={0} | all-to-all | bytes 131072 | tf_op jit(solution)/shard_map/all_to_all | solution.py:239
  49.0 1.1 %shard_map.53 = (f32[2,16,8,512]{3,2,1,0:T(8,128)S(1)}, f32[16,64]{1,0:T(8,128)S(1)}) custom-call(s32[3]{0:T(128)S(1)} %pad_add_fusion.place_ref, f32[16,8,128]{2,1,0:T(8,128)S(1)} %all_to_all.25.left_ref, bf16[128,7168]{1,0:T(8,128)(2,1)S(1)} %get-tuple-element.13.parts_ref), custom_call_target="tpu_custom_call" | custom-call | flops 58720256 | bytes 2428940 | tf_op jit(solution)/shard_map/pallas_call | solution.py:23
  50.1 15.1 %all_to_all.26 = f32[32,8,512]{2,1,0:T(8,128)S(1)} all-to-all(f32[32,8,512]{2,1,0:T(8,128)S(1)} %bitcast.13), channel_id=1, replica_groups=mesh['z8'=8,'z0'=2,'core'=2,'shard'=16] {'z0','shard'}, dimensions={0} | all-to-all | bytes 1048576 | tf_op jit(solution)/shard_map/all_to_all | solution.py:248
  65.3 0.7 shard_map.54
  66.0 3.8 %all-to-all-start.3 = ((f32[8,8,448]{2,1,0:T(8,128)}), f32[8,8,448]{2,1,0:T(8,128)S(1)}, u32[]{:S(2)}, u32[]{:S(2)}) async-start(f32[8,8,448]{2,1,0:T(8,128)} %get-tuple-element.15), calls=%async_computation.3 | async-start | bytes 262144 | tf_op jit(solution)/shard_map/all_to_all | solution.py:255
  69.8 5.4 %collective-permute-start.1 = (f32[16,1024]{1,0:T(8,128)S(1)}, f32[16,1024]{1,0:T(8,128)S(1)}, u32[]{:S(2)}, u32[]{:S(2)}) collective-permute-start(f32[16,1024]{1,0:T(8,128)S(1)} %get-tuple-element.16.own_ref), channel_id=1, source_target_pairs={{0,16},{16,0},{1,17},{17,1},{2,18},{18,2},{3,19},{19,3},{4,20},{20... | collective-permute-start | bytes 196616 | tf_op jit(solution)/shard_map/ppermute | solution.py:257
  75.1 0.9 collective-permute-done.1.other_ref
  76.0 2.6 %shard_map.55 = (bf16[128,64]{1,0:T(8,128)(2,1)S(1)}, f32[32,32]{1,0:T(8,128)S(1)}) custom-call(s32[3]{0:T(128)S(1)} %pad_add_fusion.place_ref, f32[16,1024]{1,0:T(8,128)S(1)} %get-tuple-element.16.own_ref, f32[16,1024]{1,0:T(8,128)S(1)} %collective-permute-done.1.other_ref, f32[16,64]{1,0:T(8,128)S(1)} %get-tuple-element.17.mine_ref), custom_call_target="tpu_custom_call" | custom-call | flops 10000000 | bytes 155660 | tf_op jit(solution)/shard_map/pallas_call | solution.py:23
  78.6 5.2 %all-to-all-done.3.got_ref = f32[8,8,448]{2,1,0:T(8,128)S(1)} async-done(((f32[8,8,448]{2,1,0:T(8,128)}), f32[8,8,448]{2,1,0:T(8,128)S(1)}, u32[]{:S(2)}, u32[]{:S(2)}) %all-to-all-start.3) | async-done | bytes 114720 | tf_op jit(solution)/shard_map/all_to_all | solution.py:255
  83.8 0.1 shard_map.56
  83.8 12.7 %all_to_all.27 = f32[32,8,448]{2,1,0:T(8,128)S(1)} all-to-all(f32[32,8,448]{2,1,0:T(8,128)S(1)} %shard_map.56), channel_id=1, replica_groups=mesh['z8'=8,'z0'=2,'core'=2,'shard'=16] {'z0','shard'}, dimensions={0} | all-to-all | bytes 917504 | tf_op jit(solution)/shard_map/all_to_all | solution.py:270
  96.5 7.3 %all-gather = f32[64,8,448]{2,1,0:T(8,128)S(1)} all-gather(f32[32,8,448]{2,1,0:T(8,128)S(1)} %all_to_all.27), channel_id=2, replica_groups=mesh['z8'=8,'z0'=2,'core'=2,'shard'=16] {'core'}, dimensions={0}, use_global_device_ids=true | all-gather | bytes 1376256 | tf_op jit(solution)/shard_map/all_gather | solution.py:271
  103.8 2.7 %shard_map.57 = (f32[64,7168]{1,0:T(8,128)}, f32[32,448]{1,0:T(8,128)}) custom-call(s32[3]{0:T(128)S(1)} %pad_add_fusion.place_ref, f32[2,2,16,8,448]{4,3,2,1,0:T(8,128)S(1)} %bitcast.11, bf16[128,64]{1,0:T(8,128)(2,1)S(1)} %get-tuple-element.18.weights_ref, f32[32,32]{1,0:T(8,128)S(1)} %get-tuple-element.19.inverse_ref, ...), custom_call_target="tpu_custom_call" | custom-call | flops 117440512 | bytes 4665356 | tf_op jit(solution)/shard_map/pallas_call | solution.py:23
Async XLA Ops:
  0.7 0.8 copy-start
  1.6 9.0 %copy-start.1 = (bf16[1,64,7168]{2,1,0:T(8,128)(2,1)S(1)}, bf16[1,64,7168]{2,1,0:T(8,128)(2,1)}, u32[]{:S(2)}) copy-start(bf16[1,64,7168]{2,1,0:T(8,128)(2,1)} %param.3) | copy-start | bytes 2752516
  3.0 16.2 %all-to-all-start = ((f32[16,8,896]{2,1,0:T(8,128)}), f32[16,8,896]{2,1,0:T(8,128)S(1)}, u32[]{:S(2)}, u32[]{:S(2)}) async-start(f32[16,8,896]{2,1,0:T(8,128)} %shard_map.50), calls=%async_computation | async-start | bytes 917504 | tf_op jit(solution)/shard_map/all_to_all | solution.py:221
  12.3 8.3 %collective-permute-start = (f32[64,7168]{1,0:T(8,128)S(1)}, f32[64,7168]{1,0:T(8,128)}, u32[]{:S(2)}, u32[]{:S(2)}) collective-permute-start(f32[64,7168]{1,0:T(8,128)S(1)} %add_bitcast_fusion.own_ref.merged_ref), channel_id=1, source_target_pairs={{0,16},{16,0},{1,17},{17,1},{2,18},{18,2},{3,19},{19,3},{4,20},{20... | collective-permute-start | bytes 5505032 | tf_op jit(solution)/shard_map/ppermute | solution.py:223
  66.0 17.8 %all-to-all-start.3 = ((f32[8,8,448]{2,1,0:T(8,128)}), f32[8,8,448]{2,1,0:T(8,128)S(1)}, u32[]{:S(2)}, u32[]{:S(2)}) async-start(f32[8,8,448]{2,1,0:T(8,128)} %get-tuple-element.15), calls=%async_computation.3 | async-start | bytes 262144 | tf_op jit(solution)/shard_map/all_to_all | solution.py:255
  69.8 6.3 %collective-permute-start.1 = (f32[16,1024]{1,0:T(8,128)S(1)}, f32[16,1024]{1,0:T(8,128)S(1)}, u32[]{:S(2)}, u32[]{:S(2)}) collective-permute-start(f32[16,1024]{1,0:T(8,128)S(1)} %get-tuple-element.16.own_ref), channel_id=1, source_target_pairs={{0,16},{16,0},{1,17},{17,1},{2,18},{18,2},{3,19},{19,3},{4,20},{20... | collective-permute-start | bytes 196616 | tf_op jit(solution)/shard_map/ppermute | solution.py:257

commit v6 on v5

--- a/solution.py
+++ b/solution.py
@@ -91,7 +91,7 @@
 def right_kernel(replicas, place_ref, left_ref, parts_ref, out_ref, mine_ref):
     width = parts_ref.shape[1]
     step = width // 8
-    share = step // 2
+    quarter = left_ref.shape[1] // 2
     packed = left_ref[0]
     for z in range(1, left_ref.shape[0]):
         packed = packed + left_ref[z]
@@ -105,29 +105,36 @@
         [jnp.concatenate([big, big], axis=1), jnp.concatenate([low, low], axis=1)], axis=0
     ).astype(BF16)
     mine = jnp.where(place_ref[2] == 0, left[: half // 2], left[half // 2 :])
-    mine = jnp.concatenate([mine, mine], axis=0)
+    mine = jnp.concatenate([mine[:quarter], mine[quarter:]], axis=1)
     for g in range(8):
         product = dot(stacked, parts_ref[:, g * step : (g + 1) * step], ((1,), (0,)))
         right = (product[half:] + product[:half]) * (1.0 / replicas)
-        for k in range(2):
-            cut = jnp.concatenate([right[:, k * share : (k + 1) * share], mine], axis=1)
-            out_ref[0, 2 * g + k] = cut[: half // 2]
-            out_ref[1, 2 * g + k] = cut[half // 2 :]
+        for z in range(2):
+            for k in range(2):
+                row = quarter * (2 * z + k)
+                out_ref[z, 2 * g + k] = jnp.concatenate([right[row : row + quarter], mine], axis=1)
 
 
 def scatter_kernel(got_ref, out_ref, left_ref):
-    total = got_ref[0, 0]
+    quarter, span = out_ref.shape[1:]
+    rows = (got_ref.shape[3] - span) // 2
+    total = got_ref[0, 0, :, :span]
     for s in range(1, got_ref.shape[1]):
-        total = total + got_ref[0, s]
+        total = total + got_ref[0, s, :, :span]
     for s in range(got_ref.shape[1]):
-        total = total + got_ref[1, s]
-    share = out_ref.shape[2]
-    out_ref[...] = jnp.broadcast_to(total[None, :, :share], out_ref.shape)
-    low, rows = got_ref.shape[2], got_ref.shape[3] - share
+        total = total + got_ref[1, s, :, :span]
+    out_ref[...] = jnp.broadcast_to(total[None], out_ref.shape)
     for z in range(2):
         for g in range(got_ref.shape[1] // 2):
-            pair = [got_ref[z, 2 * g + k][:, share:] for k in range(2)]
-            left_ref[low * z : low * (z + 1), 2 * rows * g : 2 * rows * (g + 1)] = jnp.concatenate(pair, axis=1)
+            a, b = got_ref[z, 2 * g, :, span:], got_ref[z, 2 * g + 1, :, span:]
+            eight = jnp.concatenate(
+                [
+                    jnp.concatenate([a[:, :rows], b[:, :rows]], axis=1),
+                    jnp.concatenate([a[:, rows:], b[:, rows:]], axis=1),
+                ],
+                axis=0,
+            )
+            left_ref[2 * quarter * z : 2 * quarter * (z + 1), 2 * rows * g : 2 * rows * (g + 1)] = eight
 
 
 def spread_kernel(got_ref, weights_ref, inverse_ref, out_ref):
@@ -180,25 +187,20 @@
 def final_kernel(place_ref, raw_ref, weights_ref, inverse_ref, merged_ref, out_ref, q_ref, hold_ref, sem):
     here = place_ref[1]
     rows, width = hold_ref.shape
-    share = raw_ref.shape[-1]
-    step = 2 * share
+    step = raw_ref.shape[-1]
+    gather = lambda g: jnp.concatenate(
+        [raw_ref[core, z, 2 * g + k] for core in range(2) for z in range(2) for k in range(2)], axis=0
+    )
     copies = []
     for g in range(width // step):
         cols = slice(g * step, (g + 1) * step)
-        raw = jnp.concatenate(
-            [
-                jnp.concatenate([raw_ref[core, z, 2 * g], raw_ref[core, z, 2 * g + 1]], axis=1)
-                for core in range(2)
-                for z in range(2)
-            ],
-            axis=0,
-        )
-        product = dot(weights_ref[...], jnp.concatenate(split(raw, 2), axis=0), ((1,), (0,)))
+        product = dot(weights_ref[...], jnp.concatenate(split(gather(g), 2), axis=0), ((1,), (0,)))
         hold_ref[:, cols] = merged_ref[:, cols] - (product[rows:] + product[:rows])
         copy = pltpu.make_async_copy(hold_ref.at[:, cols], out_ref.at[:, cols], sem.at[g])
         copy.start()
         copies.append(copy)
-    raw = jnp.concatenate([raw_ref[core, z, here] for core in range(2) for z in range(2)], axis=0)
+    raw = gather(here // 2)
+    raw = jnp.where(here % 2 == 0, raw[:, : step // 2], raw[:, step // 2 :])
     q_ref[...] = dot(inverse_ref[...], raw, ((1,), (0,)), HIGH)
     for copy in copies:
         copy.wait()
@@ -240,15 +242,15 @@
 
     pieces, mine = call(
         functools.partial(right_kernel, replicas),
-        [shape((2, 16, half // 2, 512), F32), shape((half, rows), F32)],
+        [shape((2, 16, half // 4, 1024), F32), shape((half, rows), F32)],
         [place, left, parts],
         [SMEM, VMEM, VMEM],
         flops=2 * 32 * 128 * width,
     )
-    pieces = lax.all_to_all(pieces.reshape(32, half // 2, 512), PLANE, 0, 0).reshape(pieces.shape)
+    pieces = lax.all_to_all(pieces.reshape(32, half // 4, 1024), PLANE, 0, 0).reshape(pieces.shape)
     right, left_own = call(
         scatter_kernel,
-        [shape((8, half // 2, share), F32), shape((half, 16 * rows), F32)],
+        [shape((8, half // 4, 2 * share), F32), shape((half, 16 * rows), F32)],
         [pieces],
         [VMEM],
     )
@@ -265,10 +267,10 @@
     )
 
     (raw,) = call(
-        spread_kernel, [shape((32, half // 2, share), F32)], [right, weights, inverse], [VMEM] * 3
+        spread_kernel, [shape((32, half // 4, 2 * share), F32)], [right, weights, inverse], [VMEM] * 3
     )
     raw = lax.all_to_all(raw, PLANE, 0, 0)
-    raw = lax.all_gather(raw, "core").reshape(2, 2, 16, half // 2, share)
+    raw = lax.all_gather(raw, "core").reshape(2, 2, 16, half // 4, 2 * share)
     out, q_new = call(
         final_kernel,
         [shape((rows, width), F32), shape((rank, share), F32)],

time: 107 us -> 107 us (level)
  no operation moved by 1% of the time
where the time goes in v6:
time: 107 us; the launch traced here: 106 us
  blocking collectives  61.1 us (57%)
  starting transfers between devices  21.5 us (20%)
  Pallas kernels  11 us (10%)
  waiting for transfers between devices  9.08 us (8%)
  other arithmetic  1.79 us (2%)
    all_to_all x1, blocking collectives, per_device(): left = lax.all_to_all(left, ('z8', 'z0'), 0, 0)  26 us
    all_to_all x1, blocking collectives, per_device(): lax.all_to_all(pieces.reshape(32, half // 4, 1024), PLANE, 0, 0)  15.1 us
    all_to_all x1, blocking collectives, per_device(): raw = lax.all_to_all(raw, PLANE, 0, 0)  12.6 us
    pallas_call x8, Pallas kernels, call(): pl.pallas_call(body, out_shape=out, in_specs=specs, out_specs=out_specs o...  11 us
    all_to_all x1, starting transfers between devices, per_device(): all_q = lax.all_to_all(own_q, 'shard', 0, 0)  7.58 us
    all_gather x1, blocking collectives, per_device(): raw = lax.all_gather(raw, 'core').reshape(2, 2, 16, half // 4, 2 * share)  7.36 us
    ppermute x1, starting transfers between devices, per_device(): left_other = lax.ppermute(left_own, 'core', SWAP)  5.36 us
    all_to_all x1, waiting for transfers between devices, per_device(): right = lax.all_to_all(right, 'z8', 0, 0)  4.82 us
  transfers between devices with their start and end apart: 4, of which 4 were waited for; matrix products, arithmetic and copies ran while one was open for 2% of the time, Pallas kernels for 3%

profile of v6, /device:TPU:1, one launch (start us, length us, event | category | flops | bytes accessed | tf_op | source)
XLA Modules:
  0.0 106.0 jit_solution(16397047577653807425)
XLA Ops:
  0.6 0.1 pad_add_fusion.place_ref
  0.7 0.0 copy-start
  0.7 0.8 copy-done
  1.6 0.0 copy-start.1
  1.6 1.4 %shard_map.50 = f32[16,8,896]{2,1,0:T(8,128)} custom-call(s32[3]{0:T(128)S(1)} %pad_add_fusion.place_ref, f32[32,448]{1,0:T(8,128)S(1)} %bitcast.14), custom_call_target="tpu_custom_call" | custom-call | bytes 516108 | tf_op jit(solution)/shard_map/pallas_call | solution.py:23
  3.0 7.6 %all-to-all-start = ((f32[16,8,896]{2,1,0:T(8,128)}), f32[16,8,896]{2,1,0:T(8,128)S(1)}, u32[]{:S(2)}, u32[]{:S(2)}) async-start(f32[16,8,896]{2,1,0:T(8,128)} %shard_map.50), calls=%async_computation | async-start | bytes 917504 | tf_op jit(solution)/shard_map/all_to_all | solution.py:223
  10.5 0.0 copy-done.1
  10.6 1.7 %add_bitcast_fusion.own_ref.merged_ref = f32[64,7168]{1,0:T(8,128)S(1)} fusion(f32[1,64,7168]{2,1,0:T(8,128)} %param.4, bf16[1,64,7168]{2,1,0:T(8,128)(2,1)S(1)} %copy-done.1), kind=kLoop, calls=%fused_computation | loop fusion | flops 917504 | bytes 4587520 | tf_op jit(solution)/shard_map/add | solution.py:224
  12.3 4.8 %collective-permute-start = (f32[64,7168]{1,0:T(8,128)S(1)}, f32[64,7168]{1,0:T(8,128)}, u32[]{:S(2)}, u32[]{:S(2)}) collective-permute-start(f32[64,7168]{1,0:T(8,128)S(1)} %add_bitcast_fusion.own_ref.merged_ref), channel_id=1, source_target_pairs={{0,16},{16,0},{1,17},{17,1},{2,18},{18,2},{3,19},{19,3},{4,20},{20... | collective-permute-start | bytes 5505032 | tf_op jit(solution)/shard_map/ppermute | solution.py:225
  17.0 2.1 %all-to-all-done.q_ref = f32[16,8,896]{2,1,0:T(8,128)S(1)} async-done(((f32[16,8,896]{2,1,0:T(8,128)}), f32[16,8,896]{2,1,0:T(8,128)S(1)}, u32[]{:S(2)}, u32[]{:S(2)}) %all-to-all-start) | async-done | bytes 458784 | tf_op jit(solution)/shard_map/all_to_all | solution.py:223
  19.2 0.1 shard_map.51.q_ref
  19.3 1.2 %collective-permute-done.other_ref = f32[64,7168]{1,0:T(8,128)} collective-permute-done((f32[64,7168]{1,0:T(8,128)S(1)}, f32[64,7168]{1,0:T(8,128)}, u32[]{:S(2)}, u32[]{:S(2)}) %collective-permute-start) | collective-permute-done | bytes 1835040 | tf_op jit(solution)/shard_map/ppermute | solution.py:225
  20.6 2.4 %shard_map.52 = (bf16[128,7168]{1,0:T(8,128)(2,1)S(1)}, f32[16,8,128]{2,1,0:T(8,128)S(1)}) custom-call(bf16[32,7168]{1,0:T(8,128)(2,1)S(1)} %shard_map.51.q_ref, f32[64,7168]{1,0:T(8,128)S(1)} %add_bitcast_fusion.own_ref.merged_ref, f32[64,7168]{1,0:T(8,128)} %collective-permute-done.other_ref), custom_call_target="tpu_custom_call" | custom-call | flops 58720256 | bytes 6029312 | tf_op jit(solution)/shard_map/pallas_call | solution.py:23
  23.0 26.0 %all_to_all.25.left_ref = f32[16,8,128]{2,1,0:T(8,128)S(1)} all-to-all(f32[16,8,128]{2,1,0:T(8,128)S(1)} %get-tuple-element.12), channel_id=1, replica_groups=mesh['z8'=8,'z0'=2,'core'=2,'shard'=16] {'z8','z0'}, dimensions={0} | all-to-all | bytes 131072 | tf_op jit(solution)/shard_map/all_to_all | solution.py:241
  49.0 1.1 %shard_map.53 = (f32[2,16,4,1024]{3,2,1,0:T(4,128)S(1)}, f32[16,64]{1,0:T(8,128)S(1)}) custom-call(s32[3]{0:T(128)S(1)} %pad_add_fusion.place_ref, f32[16,8,128]{2,1,0:T(8,128)S(1)} %all_to_all.25.left_ref, bf16[128,7168]{1,0:T(8,128)(2,1)S(1)} %get-tuple-element.13.parts_ref), custom_call_target="tpu_custom_call" | custom-call | flops 58720256 | bytes 2428940 | tf_op jit(solution)/shard_map/pallas_call | solution.py:23
  50.1 15.1 %all_to_all.26 = f32[32,4,1024]{2,1,0:T(4,128)S(1)} all-to-all(f32[32,4,1024]{2,1,0:T(4,128)S(1)} %bitcast.13), channel_id=1, replica_groups=mesh['z8'=8,'z0'=2,'core'=2,'shard'=16] {'z0','shard'}, dimensions={0} | all-to-all | bytes 1048576 | tf_op jit(solution)/shard_map/all_to_all | solution.py:250
  65.2 0.7 shard_map.54
  65.9 3.8 %all-to-all-start.3 = ((f32[8,4,896]{2,1,0:T(4,128)}), f32[8,4,896]{2,1,0:T(4,128)S(1)}, u32[]{:S(2)}, u32[]{:S(2)}) async-start(f32[8,4,896]{2,1,0:T(4,128)} %get-tuple-element.15), calls=%async_computation.3 | async-start | bytes 229376 | tf_op jit(solution)/shard_map/all_to_all | solution.py:257
  69.7 5.4 %collective-permute-start.1 = (f32[16,1024]{1,0:T(8,128)S(1)}, f32[16,1024]{1,0:T(8,128)S(1)}, u32[]{:S(2)}, u32[]{:S(2)}) collective-permute-start(f32[16,1024]{1,0:T(8,128)S(1)} %get-tuple-element.16.own_ref), channel_id=1, source_target_pairs={{0,16},{16,0},{1,17},{17,1},{2,18},{18,2},{3,19},{19,3},{4,20},{20... | collective-permute-start | bytes 196616 | tf_op jit(solution)/shard_map/ppermute | solution.py:259
  75.1 0.9 collective-permute-done.1.other_ref
  76.0 2.6 %shard_map.55 = (bf16[128,64]{1,0:T(8,128)(2,1)S(1)}, f32[32,32]{1,0:T(8,128)S(1)}) custom-call(s32[3]{0:T(128)S(1)} %pad_add_fusion.place_ref, f32[16,1024]{1,0:T(8,128)S(1)} %get-tuple-element.16.own_ref, f32[16,1024]{1,0:T(8,128)S(1)} %collective-permute-done.1.other_ref, f32[16,64]{1,0:T(8,128)S(1)} %get-tuple-element.17.mine_ref), custom_call_target="tpu_custom_call" | custom-call | flops 10000000 | bytes 155660 | tf_op jit(solution)/shard_map/pallas_call | solution.py:23
  78.5 4.8 %all-to-all-done.3.got_ref = f32[8,4,896]{2,1,0:T(4,128)S(1)} async-done(((f32[8,4,896]{2,1,0:T(4,128)}), f32[8,4,896]{2,1,0:T(4,128)S(1)}, u32[]{:S(2)}, u32[]{:S(2)}) %all-to-all-start.3) | async-done | bytes 114720 | tf_op jit(solution)/shard_map/all_to_all | solution.py:257
  83.4 12.6 %all_to_all.27 = f32[32,4,896]{2,1,0:T(4,128)S(1)} all-to-all(f32[32,4,896]{2,1,0:T(4,128)S(1)} %shard_map.56), channel_id=1, replica_groups=mesh['z8'=8,'z0'=2,'core'=2,'shard'=16] {'z0','shard'}, dimensions={0} | all-to-all | bytes 917504 | tf_op jit(solution)/shard_map/all_to_all | solution.py:272
  96.0 7.4 %all-gather = f32[64,4,896]{2,1,0:T(4,128)S(1)} all-gather(f32[32,4,896]{2,1,0:T(4,128)S(1)} %all_to_all.27), channel_id=2, replica_groups=mesh['z8'=8,'z0'=2,'core'=2,'shard'=16] {'core'}, dimensions={0}, use_global_device_ids=true | all-gather | bytes 1376256 | tf_op jit(solution)/shard_map/all_gather | solution.py:273
  103.3 2.7 %shard_map.57 = (f32[64,7168]{1,0:T(8,128)}, f32[32,448]{1,0:T(8,128)}) custom-call(s32[3]{0:T(128)S(1)} %pad_add_fusion.place_ref, f32[2,2,16,4,896]{4,3,2,1,0:T(4,128)S(1)} %bitcast.11, bf16[128,64]{1,0:T(8,128)(2,1)S(1)} %get-tuple-element.18.weights_ref, f32[32,32]{1,0:T(8,128)S(1)} %get-tuple-element.19.inverse_ref, ...), custom_call_target="tpu_custom_call" | custom-call | flops 117440512 | bytes 4665356 | tf_op jit(solution)/shard_map/pallas_call | solution.py:23
  (1 shorter events, 0.0 us)
Async XLA Ops:
  0.7 0.8 copy-start
  1.6 9.0 %copy-start.1 = (bf16[1,64,7168]{2,1,0:T(8,128)(2,1)S(1)}, bf16[1,64,7168]{2,1,0:T(8,128)(2,1)}, u32[]{:S(2)}) copy-start(bf16[1,64,7168]{2,1,0:T(8,128)(2,1)} %param.3) | copy-start | bytes 2752516
  3.0 16.2 %all-to-all-start = ((f32[16,8,896]{2,1,0:T(8,128)}), f32[16,8,896]{2,1,0:T(8,128)S(1)}, u32[]{:S(2)}, u32[]{:S(2)}) async-start(f32[16,8,896]{2,1,0:T(8,128)} %shard_map.50), calls=%async_computation | async-start | bytes 917504 | tf_op jit(solution)/shard_map/all_to_all | solution.py:223
  12.3 8.3 %collective-permute-start = (f32[64,7168]{1,0:T(8,128)S(1)}, f32[64,7168]{1,0:T(8,128)}, u32[]{:S(2)}, u32[]{:S(2)}) collective-permute-start(f32[64,7168]{1,0:T(8,128)S(1)} %add_bitcast_fusion.own_ref.merged_ref), channel_id=1, source_target_pairs={{0,16},{16,0},{1,17},{17,1},{2,18},{18,2},{3,19},{19,3},{4,20},{20... | collective-permute-start | bytes 5505032 | tf_op jit(solution)/shard_map/ppermute | solution.py:225
  65.9 17.4 %all-to-all-start.3 = ((f32[8,4,896]{2,1,0:T(4,128)}), f32[8,4,896]{2,1,0:T(4,128)S(1)}, u32[]{:S(2)}, u32[]{:S(2)}) async-start(f32[8,4,896]{2,1,0:T(4,128)} %get-tuple-element.15), calls=%async_computation.3 | async-start | bytes 229376 | tf_op jit(solution)/shard_map/all_to_all | solution.py:257
  69.7 6.3 %collective-permute-start.1 = (f32[16,1024]{1,0:T(8,128)S(1)}, f32[16,1024]{1,0:T(8,128)S(1)}, u32[]{:S(2)}, u32[]{:S(2)}) collective-permute-start(f32[16,1024]{1,0:T(8,128)S(1)} %get-tuple-element.16.own_ref), channel_id=1, source_target_pairs={{0,16},{16,0},{1,17},{17,1},{2,18},{18,2},{3,19},{19,3},{4,20},{20... | collective-permute-start | bytes 196616 | tf_op jit(solution)/shard_map/ppermute | solution.py:259

commit v7 on v6

--- a/solution.py
+++ b/solution.py
@@ -16,6 +16,20 @@
 CUTS = 7
 STRIDE = 4
 SMEM = pl.BlockSpec(memory_space=pltpu.SMEM)
+
+
+ASKED = 10
+FIRST = 10
+START = 11
+TURN = 5
+
+
+def place_of(peer, first=FIRST):
+    return first if peer == 0 else 0 if peer == first else peer
+
+
+def exchange(blocks, axis, order):
+    return lax.all_to_all(blocks, axis, 0, 0, axis_index_groups=[list(order)])
 
 
 def call(body, out, operands, specs, scratch=(), out_specs=None, flops=0, limit=24):
@@ -55,7 +69,7 @@
     shards, low, span = q_ref.shape
     share = span // 2
     for g in range(shards // 2):
-        a, b = q_ref[2 * g], q_ref[2 * g + 1]
+        a, b = q_ref[place_of(2 * g, ASKED)], q_ref[place_of(2 * g + 1, ASKED)]
         pair = jnp.concatenate(
             [
                 jnp.concatenate([a[:, :share], b[:, :share]], axis=1),
@@ -112,21 +126,20 @@
         for z in range(2):
             for k in range(2):
                 row = quarter * (2 * z + k)
-                out_ref[z, 2 * g + k] = jnp.concatenate([right[row : row + quarter], mine], axis=1)
+                out_ref[place_of(16 * z + 2 * g + k)] = jnp.concatenate([right[row : row + quarter], mine], axis=1)
 
 
 def scatter_kernel(got_ref, out_ref, left_ref):
     quarter, span = out_ref.shape[1:]
-    rows = (got_ref.shape[3] - span) // 2
-    total = got_ref[0, 0, :, :span]
-    for s in range(1, got_ref.shape[1]):
-        total = total + got_ref[0, s, :, :span]
-    for s in range(got_ref.shape[1]):
-        total = total + got_ref[1, s, :, :span]
+    peers = got_ref.shape[0]
+    rows = (got_ref.shape[2] - span) // 2
+    total = got_ref[0, :, :span]
+    for peer in range(1, peers):
+        total = total + got_ref[peer, :, :span]
     out_ref[...] = jnp.broadcast_to(total[None], out_ref.shape)
     for z in range(2):
-        for g in range(got_ref.shape[1] // 2):
-            a, b = got_ref[z, 2 * g, :, span:], got_ref[z, 2 * g + 1, :, span:]
+        for g in range(peers // 4):
+            a, b = (got_ref[place_of(peers // 2 * z + 2 * g + k), :, span:] for k in range(2))
             eight = jnp.concatenate(
                 [
                     jnp.concatenate([a[:, :rows], b[:, :rows]], axis=1),
@@ -188,18 +201,17 @@
     here = place_ref[1]
     rows, width = hold_ref.shape
     step = raw_ref.shape[-1]
-    gather = lambda g: jnp.concatenate(
-        [raw_ref[core, z, 2 * g + k] for core in range(2) for z in range(2) for k in range(2)], axis=0
-    )
+    gather = lambda peers: jnp.concatenate([raw_ref[core, peer] for core in range(2) for peer in peers], axis=0)
     copies = []
     for g in range(width // step):
         cols = slice(g * step, (g + 1) * step)
-        product = dot(weights_ref[...], jnp.concatenate(split(gather(g), 2), axis=0), ((1,), (0,)))
+        product = dot(weights_ref[...], jnp.concatenate(split(gather([place_of(16 * z + 2 * g + k) for z in range(2) for k in range(2)]), 2), axis=0), ((1,), (0,)))
         hold_ref[:, cols] = merged_ref[:, cols] - (product[rows:] + product[:rows])
         copy = pltpu.make_async_copy(hold_ref.at[:, cols], out_ref.at[:, cols], sem.at[g])
         copy.start()
         copies.append(copy)
-    raw = gather(here // 2)
+    peers = [here // 2 * 2 + 16 * z + k for z in range(2) for k in range(2)]
+    raw = gather([jnp.where(peer == 0, FIRST, jnp.where(peer == FIRST, 0, peer)) for peer in peers])
     raw = jnp.where(here % 2 == 0, raw[:, : step // 2], raw[:, step // 2 :])
     q_ref[...] = dot(inverse_ref[...], raw, ((1,), (0,)), HIGH)
     for copy in copies:
@@ -220,7 +232,7 @@
         [place, q_prev.T],
         [SMEM, VMEM],
     )
-    all_q = lax.all_to_all(own_q, "shard", 0, 0)
+    all_q = exchange(own_q, "shard", (place_of(s, ASKED) for s in range(16)))
     merged = grads[0].astype(F32) + errors[0]
     other = lax.ppermute(merged, "core", SWAP)
     (all_q,) = call(
@@ -238,23 +250,23 @@
         [pltpu.VMEM((rows, width), F32), pltpu.SemaphoreType.DMA((CUTS,))],
         flops=2 * 32 * 128 * width,
     )
-    left = lax.all_to_all(left, ("z8", "z0"), 0, 0)
+    left = exchange(left, ("z8", "z0"), ((z + START) % 16 for z in range(16)))
 
     pieces, mine = call(
         functools.partial(right_kernel, replicas),
-        [shape((2, 16, half // 4, 1024), F32), shape((half, rows), F32)],
+        [shape((32, half // 4, 1024), F32), shape((half, rows), F32)],
         [place, left, parts],
         [SMEM, VMEM, VMEM],
         flops=2 * 32 * 128 * width,
     )
-    pieces = lax.all_to_all(pieces.reshape(32, half // 4, 1024), PLANE, 0, 0).reshape(pieces.shape)
+    pieces = exchange(pieces, PLANE, map(place_of, range(32)))
     right, left_own = call(
         scatter_kernel,
         [shape((8, half // 4, 2 * share), F32), shape((half, 16 * rows), F32)],
         [pieces],
         [VMEM],
     )
-    right = lax.all_to_all(right, "z8", 0, 0)
+    right = exchange(right, "z8", ((z + TURN) % 8 for z in range(8)))
 
     left_other = lax.ppermute(left_own, "core", SWAP)
     weights, inverse = call(
@@ -269,8 +281,8 @@
     (raw,) = call(
         spread_kernel, [shape((32, half // 4, 2 * share), F32)], [right, weights, inverse], [VMEM] * 3
     )
-    raw = lax.all_to_all(raw, PLANE, 0, 0)
-    raw = lax.all_gather(raw, "core").reshape(2, 2, 16, half // 4, 2 * share)
+    raw = exchange(raw, PLANE, map(place_of, range(32)))
+    raw = lax.all_gather(raw, "core")
     out, q_new = call(
         final_kernel,
         [shape((rows, width), F32), shape((rank, share), F32)],

time: 107 us -> 98.7 us (0.922)
  blocking collectives: 61.1 us -> 48.4 us
  starting transfers between devices: 21.5 us -> 31.1 us
  waiting for transfers between devices: 9.08 us -> 4.25 us
    all_to_all x3, blocking collectives: 53.7 us -> 44.3 us  [exchange(): return lax.all_to_all(blocks, axis, 0, 0, axis_index_groups=[list(order)])]
    all_to_all x2, starting transfers between devices: 11.4 us -> 20 us  [exchange(): return lax.all_to_all(blocks, axis, 0, 0, axis_index_groups=[list(order)])]
    all_to_all x2, waiting for transfers between devices: 6.95 us -> 0.01 us  [exchange(): return lax.all_to_all(blocks, axis, 0, 0, axis_index_groups=[list(order)])]
    all_gather x1, blocking collectives: 7.36 us -> 4.07 us  [per_device(): raw = lax.all_gather(raw, 'core')]
    ppermute x1, waiting for transfers between devices: 1.25 us -> 3.37 us  [per_device(): other = lax.ppermute(merged, 'core', SWAP)]
    ppermute x1, starting transfers between devices: 4.77 us -> 6.4 us  [per_device(): other = lax.ppermute(merged, 'core', SWAP)]
  transfers between devices with their start and end apart: 4 -> 4, of which waited for: 4 -> 2; matrix products, arithmetic and copies ran while one was open for 2% -> 2% of each run, Pallas kernels for 3% -> 3%
where the time goes in v7:
time: 98.7 us; the launch traced here: 98.2 us
  blocking collectives  48.4 us (49%)
  starting transfers between devices  31.1 us (32%)
  Pallas kernels  11.1 us (11%)
  waiting for transfers between devices  4.25 us (4%)
  other arithmetic  1.79 us (2%)
    all_to_all x3, blocking collectives, exchange(): return lax.all_to_all(blocks, axis, 0, 0, axis_index_groups=[list(order)])  44.3 us
    all_to_all x2, starting transfers between devices, exchange(): return lax.all_to_all(blocks, axis, 0, 0, axis_index_groups=[list(order)])  20 us
    pallas_call x8, Pallas kernels, call(): pl.pallas_call(body, out_shape=out, in_specs=specs, out_specs=out_specs o...  11.1 us
    ppermute x1, starting transfers between devices, per_device(): other = lax.ppermute(merged, 'core', SWAP)  6.4 us
    ppermute x1, starting transfers between devices, per_device(): left_other = lax.ppermute(left_own, 'core', SWAP)  4.72 us
    all_gather x1, blocking collectives, per_device(): raw = lax.all_gather(raw, 'core')  4.07 us
    ppermute x1, waiting for transfers between devices, per_device(): other = lax.ppermute(merged, 'core', SWAP)  3.37 us
  transfers between devices with their start and end apart: 4, of which 2 were waited for; matrix products, arithmetic and copies ran while one was open for 2% of the time, Pallas kernels for 3%

profile of v7, /device:TPU:1, one launch (start us, length us, event | category | flops | bytes accessed | tf_op | source)
XLA Modules:
  0.0 98.2 jit_solution(15223665641629724084)
XLA Ops:
  0.6 0.1 pad_add_fusion.place_ref
  0.7 0.0 copy-start
  0.7 0.8 copy-done
  1.6 0.0 copy-start.1
  1.6 1.4 %shard_map.50 = f32[16,8,896]{2,1,0:T(8,128)} custom-call(s32[3]{0:T(128)S(1)} %pad_add_fusion.place_ref, f32[32,448]{1,0:T(8,128)S(1)} %bitcast.10), custom_call_target="tpu_custom_call" | custom-call | bytes 516108 | tf_op jit(solution)/shard_map/pallas_call | solution.py:37
  3.0 9.6 %all-to-all-start = ((f32[16,8,896]{2,1,0:T(8,128)}), f32[16,8,896]{2,1,0:T(8,128)S(1)}, u32[]{:S(2)}, u32[]{:S(2)}) async-start(f32[16,8,896]{2,1,0:T(8,128)} %shard_map.50), calls=%async_computation | async-start | bytes 917504 | tf_op jit(solution)/shard_map/all_to_all | solution.py:32
  12.6 0.0 copy-done.1
  12.6 1.7 %add_bitcast_fusion.own_ref.merged_ref = f32[64,7168]{1,0:T(8,128)S(1)} fusion(f32[1,64,7168]{2,1,0:T(8,128)} %param.4, bf16[1,64,7168]{2,1,0:T(8,128)(2,1)S(1)} %copy-done.1), kind=kLoop, calls=%fused_computation | loop fusion | flops 917504 | bytes 4587520 | tf_op jit(solution)/shard_map/add | solution.py:236
  14.3 6.4 %collective-permute-start = (f32[64,7168]{1,0:T(8,128)S(1)}, f32[64,7168]{1,0:T(8,128)}, u32[]{:S(2)}, u32[]{:S(2)}) collective-permute-start(f32[64,7168]{1,0:T(8,128)S(1)} %add_bitcast_fusion.own_ref.merged_ref), channel_id=1, source_target_pairs={{0,16},{16,0},{1,17},{17,1},{2,18},{18,2},{3,19},{19,3},{4,20},{20... | collective-permute-start | bytes 5505032 | tf_op jit(solution)/shard_map/ppermute | solution.py:237
  20.7 0.0 all-to-all-done.q_ref
  20.7 0.1 shard_map.51.q_ref
  20.8 3.4 %collective-permute-done.other_ref = f32[64,7168]{1,0:T(8,128)} collective-permute-done((f32[64,7168]{1,0:T(8,128)S(1)}, f32[64,7168]{1,0:T(8,128)}, u32[]{:S(2)}, u32[]{:S(2)}) %collective-permute-start) | collective-permute-done | bytes 1835040 | tf_op jit(solution)/shard_map/ppermute | solution.py:237
  24.2 2.5 %shard_map.52 = (bf16[128,7168]{1,0:T(8,128)(2,1)S(1)}, f32[16,8,128]{2,1,0:T(8,128)S(1)}) custom-call(bf16[32,7168]{1,0:T(8,128)(2,1)S(1)} %shard_map.51.q_ref, f32[64,7168]{1,0:T(8,128)S(1)} %add_bitcast_fusion.own_ref.merged_ref, f32[64,7168]{1,0:T(8,128)} %collective-permute-done.other_ref), custom_call_target="tpu_custom_call" | custom-call | flops 58720256 | bytes 6029312 | tf_op jit(solution)/shard_map/pallas_call | solution.py:37
  26.7 17.8 %all_to_all.25.left_ref = f32[16,8,128]{2,1,0:T(8,128)S(1)} all-to-all(f32[16,8,128]{2,1,0:T(8,128)S(1)} %get-tuple-element.12), channel_id=1, replica_groups={{352,384,416,448,480,0,32,64,96,128,160,192,224,256,288,320},{353,385,4..., dimensions={0} | all-to-all | bytes 131072 | tf_op jit(solution)/shard_map/all_to_all | solution.py:32
  44.5 1.1 %shard_map.53 = (f32[32,4,1024]{2,1,0:T(4,128)S(1)}, f32[16,64]{1,0:T(8,128)S(1)}) custom-call(s32[3]{0:T(128)S(1)} %pad_add_fusion.place_ref, f32[16,8,128]{2,1,0:T(8,128)S(1)} %all_to_all.25.left_ref, bf16[128,7168]{1,0:T(8,128)(2,1)S(1)} %get-tuple-element.13.parts_ref), custom_call_target="tpu_custom_call" | custom-call | flops 58720256 | bytes 2428940 | tf_op jit(solution)/shard_map/pallas_call | solution.py:37
  45.6 12.8 %all_to_all.26.got_ref = f32[32,4,1024]{2,1,0:T(4,128)S(1)} all-to-all(f32[32,4,1024]{2,1,0:T(4,128)S(1)} %get-tuple-element.14), channel_id=1, replica_groups={{10,1,2,3,4,5,6,7,8,9,0,11,12,13,14,15,32,33,34,35,36,37,38,39,40,41,42..., dimensions={0} | all-to-all | bytes 1048576 | tf_op jit(solution)/shard_map/all_to_all | solution.py:32
  58.4 0.7 shard_map.54
  59.1 10.4 %all-to-all-start.3 = ((f32[8,4,896]{2,1,0:T(4,128)}), f32[8,4,896]{2,1,0:T(4,128)S(1)}, u32[]{:S(2)}, u32[]{:S(2)}) async-start(f32[8,4,896]{2,1,0:T(4,128)} %get-tuple-element.15), calls=%async_computation.3 | async-start | bytes 229376 | tf_op jit(solution)/shard_map/all_to_all | solution.py:32
  69.5 4.7 %collective-permute-start.1 = (f32[16,1024]{1,0:T(8,128)S(1)}, f32[16,1024]{1,0:T(8,128)S(1)}, u32[]{:S(2)}, u32[]{:S(2)}) collective-permute-start(f32[16,1024]{1,0:T(8,128)S(1)} %get-tuple-element.16.own_ref), channel_id=1, source_target_pairs={{0,16},{16,0},{1,17},{17,1},{2,18},{18,2},{3,19},{19,3},{4,20},{20... | collective-permute-start | bytes 196616 | tf_op jit(solution)/shard_map/ppermute | solution.py:271
  74.2 0.9 collective-permute-done.1.other_ref
  75.1 2.6 %shard_map.55 = (bf16[128,64]{1,0:T(8,128)(2,1)S(1)}, f32[32,32]{1,0:T(8,128)S(1)}) custom-call(s32[3]{0:T(128)S(1)} %pad_add_fusion.place_ref, f32[16,1024]{1,0:T(8,128)S(1)} %get-tuple-element.16.own_ref, f32[16,1024]{1,0:T(8,128)S(1)} %collective-permute-done.1.other_ref, f32[16,64]{1,0:T(8,128)S(1)} %get-tuple-element.17.mine_ref), custom_call_target="tpu_custom_call" | custom-call | flops 10000000 | bytes 155660 | tf_op jit(solution)/shard_map/pallas_call | solution.py:37
  77.7 0.0 all-to-all-done.3.got_ref
  77.7 13.7 %all_to_all.27 = f32[32,4,896]{2,1,0:T(4,128)S(1)} all-to-all(f32[32,4,896]{2,1,0:T(4,128)S(1)} %shard_map.56), channel_id=1, replica_groups={{10,1,2,3,4,5,6,7,8,9,0,11,12,13,14,15,32,33,34,35,36,37,38,39,40,41,42..., dimensions={0} | all-to-all | bytes 917504 | tf_op jit(solution)/shard_map/all_to_all | solution.py:32
  91.4 4.1 %all-gather = f32[64,4,896]{2,1,0:T(4,128)S(1)} all-gather(f32[32,4,896]{2,1,0:T(4,128)S(1)} %all_to_all.27), channel_id=2, replica_groups=mesh['z8'=8,'z0'=2,'core'=2,'shard'=16] {'core'}, dimensions={0}, use_global_device_ids=true | all-gather | bytes 1376256 | tf_op jit(solution)/shard_map/all_gather | solution.py:285
  95.5 2.7 %shard_map.57 = (f32[64,7168]{1,0:T(8,128)}, f32[32,448]{1,0:T(8,128)}) custom-call(s32[3]{0:T(128)S(1)} %pad_add_fusion.place_ref, f32[2,32,4,896]{3,2,1,0:T(4,128)S(1)} %bitcast.9, bf16[128,64]{1,0:T(8,128)(2,1)S(1)} %get-tuple-element.18.weights_ref, f32[32,32]{1,0:T(8,128)S(1)} %get-tuple-element.19.inverse_ref, ...), custom_call_target="tpu_custom_call" | custom-call | flops 117440512 | bytes 4665356 | tf_op jit(solution)/shard_map/pallas_call | solution.py:37
  (1 shorter events, 0.0 us)
Async XLA Ops:
  0.7 0.8 copy-start
  1.6 11.0 %copy-start.1 = (bf16[1,64,7168]{2,1,0:T(8,128)(2,1)S(1)}, bf16[1,64,7168]{2,1,0:T(8,128)(2,1)}, u32[]{:S(2)}) copy-start(bf16[1,64,7168]{2,1,0:T(8,128)(2,1)} %param.3) | copy-start | bytes 2752516
  3.0 17.7 %all-to-all-start = ((f32[16,8,896]{2,1,0:T(8,128)}), f32[16,8,896]{2,1,0:T(8,128)S(1)}, u32[]{:S(2)}, u32[]{:S(2)}) async-start(f32[16,8,896]{2,1,0:T(8,128)} %shard_map.50), calls=%async_computation | async-start | bytes 917504 | tf_op jit(solution)/shard_map/all_to_all | solution.py:32
  14.3 9.9 %collective-permute-start = (f32[64,7168]{1,0:T(8,128)S(1)}, f32[64,7168]{1,0:T(8,128)}, u32[]{:S(2)}, u32[]{:S(2)}) collective-permute-start(f32[64,7168]{1,0:T(8,128)S(1)} %add_bitcast_fusion.own_ref.merged_ref), channel_id=1, source_target_pairs={{0,16},{16,0},{1,17},{17,1},{2,18},{18,2},{3,19},{19,3},{4,20},{20... | collective-permute-start | bytes 5505032 | tf_op jit(solution)/shard_map/ppermute | solution.py:237
  59.1 18.5 %all-to-all-start.3 = ((f32[8,4,896]{2,1,0:T(4,128)}), f32[8,4,896]{2,1,0:T(4,128)S(1)}, u32[]{:S(2)}, u32[]{:S(2)}) async-start(f32[8,4,896]{2,1,0:T(4,128)} %get-tuple-element.15), calls=%async_computation.3 | async-start | bytes 229376 | tf_op jit(solution)/shard_map/all_to_all | solution.py:32
  69.5 5.6 %collective-permute-start.1 = (f32[16,1024]{1,0:T(8,128)S(1)}, f32[16,1024]{1,0:T(8,128)S(1)}, u32[]{:S(2)}, u32[]{:S(2)}) collective-permute-start(f32[16,1024]{1,0:T(8,128)S(1)} %get-tuple-element.16.own_ref), channel_id=1, source_target_pairs={{0,16},{16,0},{1,17},{17,1},{2,18},{18,2},{3,19},{19,3},{4,20},{20... | collective-permute-start | bytes 196616 | tf_op jit(solution)/shard_map/ppermute | solution.py:271

commit v8 on v7

--- a/solution.py
+++ b/solution.py
@@ -15,7 +15,6 @@
 ANY = pl.BlockSpec(memory_space=pl.ANY)
 CUTS = 7
 STRIDE = 4
-SMEM = pl.BlockSpec(memory_space=pltpu.SMEM)
 
 
 ASKED = 10
@@ -58,9 +57,9 @@
     return lax.dot_general(a, b, (dims, ((), ())), precision=precision, preferred_element_type=F32)
 
 
-def ask_kernel(place_ref, q_ref, out_ref):
+def ask_kernel(q_ref, out_ref):
     half = q_ref.shape[0] // 2
-    mine = q_ref[pl.ds(pl.multiple_of(place_ref[0] * half, half), half), :]
+    mine = q_ref[pl.ds(pl.multiple_of(lax.axis_index("core") * half, half), half), :]
     packed = jnp.concatenate([mine[: half // 2], mine[half // 2 :]], axis=1)
     out_ref[...] = jnp.broadcast_to(packed[None], out_ref.shape)
 
@@ -102,7 +101,7 @@
     out_ref[...] = jnp.broadcast_to(packed[None], out_ref.shape)
 
 
-def right_kernel(replicas, place_ref, left_ref, parts_ref, out_ref, mine_ref):
+def right_kernel(replicas, left_ref, parts_ref, out_ref, mine_ref):
     width = parts_ref.shape[1]
     step = width // 8
     quarter = left_ref.shape[1] // 2
@@ -118,7 +117,7 @@
     stacked = jnp.concatenate(
         [jnp.concatenate([big, big], axis=1), jnp.concatenate([low, low], axis=1)], axis=0
     ).astype(BF16)
-    mine = jnp.where(place_ref[2] == 0, left[: half // 2], left[half // 2 :])
+    mine = jnp.where(lax.axis_index("z0") == 0, left[: half // 2], left[half // 2 :])
     mine = jnp.concatenate([mine[:quarter], mine[quarter:]], axis=1)
     for g in range(8):
         product = dot(stacked, parts_ref[:, g * step : (g + 1) * step], ((1,), (0,)))
@@ -157,8 +156,8 @@
     out_ref[...] = jnp.broadcast_to(total[None], out_ref.shape)
 
 
-def factor_kernel(place_ref, own_ref, other_ref, mine_ref, weights_ref, inverse_ref, left_ref, both_ref):
-    core, here = place_ref[0], place_ref[1]
+def factor_kernel(own_ref, other_ref, mine_ref, weights_ref, inverse_ref, left_ref, both_ref):
+    core, here = lax.axis_index("core"), lax.axis_index("shard")
     half, rows = mine_ref.shape
     rank = 2 * half
     first = pl.ds(pl.multiple_of(core * half, half), half)
@@ -191,29 +190,29 @@
     inverse = work[:, rank : 2 * rank]
     mine = dot(work[:, 2 * rank :], inverse, ((0,), (0,)), HIGH)
     big, low = (part.astype(F32) for part in split(mine, 2))
-    weights_ref[...] = jnp.concatenate(
-        [jnp.concatenate([big, big], axis=1), jnp.concatenate([low, low], axis=1)], axis=0
-    ).astype(BF16)
+    weights_ref[...] = jnp.concatenate([big, big, low], axis=1).astype(BF16)
     inverse_ref[...] = inverse
 
 
-def final_kernel(place_ref, raw_ref, weights_ref, inverse_ref, merged_ref, out_ref, q_ref, hold_ref, sem):
-    here = place_ref[1]
-    rows, width = hold_ref.shape
+def final_kernel(raw_ref, weights_ref, inverse_ref, merged_ref, out_ref, q_ref, hold_ref, q_buf, sem):
+    here = lax.axis_index("shard")
+    width = hold_ref.shape[1]
     step = raw_ref.shape[-1]
     gather = lambda peers: jnp.concatenate([raw_ref[core, peer] for core in range(2) for peer in peers], axis=0)
-    copies = []
+    peers = [here // 2 * 2 + 16 * z + k for z in range(2) for k in range(2)]
+    raw = gather([jnp.where(peer == 0, FIRST, jnp.where(peer == FIRST, 0, peer)) for peer in peers])
+    raw = jnp.where(here % 2 == 0, raw[:, : step // 2], raw[:, step // 2 :])
+    q_buf[...] = dot(inverse_ref[...], raw, ((1,), (0,)), HIGH)
+    copies = [pltpu.make_async_copy(q_buf, q_ref, sem.at[width // step])]
+    copies[0].start()
     for g in range(width // step):
         cols = slice(g * step, (g + 1) * step)
-        product = dot(weights_ref[...], jnp.concatenate(split(gather([place_of(16 * z + 2 * g + k) for z in range(2) for k in range(2)]), 2), axis=0), ((1,), (0,)))
-        hold_ref[:, cols] = merged_ref[:, cols] - (product[rows:] + product[:rows])
+        big, low = split(gather([place_of(16 * z + 2 * g + k) for z in range(2) for k in range(2)]), 2)
+        approx = dot(weights_ref[...], jnp.concatenate([big, low, big], axis=0), ((1,), (0,)))
+        hold_ref[:, cols] = merged_ref[:, cols] - approx
         copy = pltpu.make_async_copy(hold_ref.at[:, cols], out_ref.at[:, cols], sem.at[g])
         copy.start()
         copies.append(copy)
-    peers = [here // 2 * 2 + 16 * z + k for z in range(2) for k in range(2)]
-    raw = gather([jnp.where(peer == 0, FIRST, jnp.where(peer == FIRST, 0, peer)) for peer in peers])
-    raw = jnp.where(here % 2 == 0, raw[:, : step // 2], raw[:, step // 2 :])
-    q_ref[...] = dot(inverse_ref[...], raw, ((1,), (0,)), HIGH)
     for copy in copies:
         copy.wait()
 
@@ -223,14 +222,13 @@
     rows, width = errors.shape[1:]
     share, rank = q_prev.shape
     half = rank // 2
-    place = jnp.stack([lax.axis_index(axis) for axis in ("core", "shard", "z0")])
     replicas = 32
 
     (own_q,) = call(
         ask_kernel,
         [shape((16, half // 2, 2 * share), F32)],
-        [place, q_prev.T],
-        [SMEM, VMEM],
+        [q_prev.T],
+        [VMEM],
     )
     all_q = exchange(own_q, "shard", (place_of(s, ASKED) for s in range(16)))
     merged = grads[0].astype(F32) + errors[0]
@@ -255,8 +253,8 @@
     pieces, mine = call(
         functools.partial(right_kernel, replicas),
         [shape((32, half // 4, 1024), F32), shape((half, rows), F32)],
-        [place, left, parts],
-        [SMEM, VMEM, VMEM],
+        [left, parts],
+        [VMEM, VMEM],
         flops=2 * 32 * 128 * width,
     )
     pieces = exchange(pieces, PLANE, map(place_of, range(32)))
@@ -271,9 +269,9 @@
     left_other = lax.ppermute(left_own, "core", SWAP)
     weights, inverse = call(
         factor_kernel,
-        [shape((2 * rows, 2 * rank), BF16), shape((rank, rank), F32)],
-        [place, left_own, left_other, mine],
-        [SMEM] + [VMEM] * 3,
+        [shape((rows, 3 * rank), BF16), shape((rank, rank), F32)],
+        [left_own, left_other, mine],
+        [VMEM] * 3,
         [pltpu.VMEM((rank, 16 * rows), F32), pltpu.VMEM((rank, rows), F32)],
         flops=10**7,
     )
@@ -286,11 +284,11 @@
     out, q_new = call(
         final_kernel,
         [shape((rows, width), F32), shape((rank, share), F32)],
-        [place, raw, weights, inverse, merged],
-        [SMEM] + [VMEM] * 4,
-        [pltpu.VMEM((rows, width), F32), pltpu.SemaphoreType.DMA((8,))],
-        [pl.BlockSpec(memory_space=pl.ANY), VMEM],
-        flops=2 * 128 * 64 * width,
+        [raw, weights, inverse, merged],
+        [VMEM] * 4,
+        [pltpu.VMEM((rows, width), F32), pltpu.VMEM((rank, share), F32), pltpu.SemaphoreType.DMA((9,))],
+        [ANY, ANY],
+        flops=2 * 96 * 64 * width,
     )
     return (out[None], q_new.T)
 

time: 98.7 us -> 95.8 us (0.971)
  Pallas kernels: 11.1 us -> 8.33 us
    pallas_call x8, Pallas kernels: 11.1 us -> 8.33 us  [call(): pl.pallas_call(body, out_shape=out, in_specs=specs, out_specs=out_specs o...]
  transfers between devices with their start and end apart: 4 -> 4, of which waited for: 2 -> 2; matrix products, arithmetic and copies ran while one was open for 2% -> 2% of each run, Pallas kernels for 3% -> 2%
where the time goes in v8:
time: 95.8 us; the launch traced here: 95.3 us
  blocking collectives  48.4 us (51%)
  starting transfers between devices  31.1 us (32%)
  Pallas kernels  8.33 us (9%)
  waiting for transfers between devices  4.25 us (4%)
  other arithmetic  1.66 us (2%)
    all_to_all x3, blocking collectives, exchange(): return lax.all_to_all(blocks, axis, 0, 0, axis_index_groups=[list(order)])  44 us
    all_to_all x2, starting transfers between devices, exchange(): return lax.all_to_all(blocks, axis, 0, 0, axis_index_groups=[list(order)])  20 us
    pallas_call x8, Pallas kernels, call(): pl.pallas_call(body, out_shape=out, in_specs=specs, out_specs=out_specs o...  8.33 us
    ppermute x1, starting transfers between devices, per_device(): other = lax.ppermute(merged, 'core', SWAP)  6.4 us
    ppermute x1, starting transfers between devices, per_device(): left_other = lax.ppermute(left_own, 'core', SWAP)  4.72 us
    all_gather x1, blocking collectives, per_device(): raw = lax.all_gather(raw, 'core')  4.41 us
    ppermute x1, waiting for transfers between devices, per_device(): other = lax.ppermute(merged, 'core', SWAP)  3.37 us
  transfers between devices with their start and end apart: 4, of which 2 were waited for; matrix products, arithmetic and copies ran while one was open for 2% of the time, Pallas kernels for 2%

profile of v8, /device:TPU:1, one launch (start us, length us, event | category | flops | bytes accessed | tf_op | source)
XLA Modules:
  0.0 95.3 jit_solution(3565840622409721854)
XLA Ops:
  0.6 0.0 copy-start
  0.6 0.8 copy-done
  1.5 0.0 copy-start.1
  1.5 0.9 shard_map.50
  2.3 9.6 %all-to-all-start = ((f32[16,8,896]{2,1,0:T(8,128)}), f32[16,8,896]{2,1,0:T(8,128)S(1)}, u32[]{:S(2)}, u32[]{:S(2)}) async-start(f32[16,8,896]{2,1,0:T(8,128)} %shard_map.50), calls=%async_computation | async-start | bytes 917504 | tf_op jit(solution)/shard_map/all_to_all | solution.py:31
  11.9 0.0 copy-done.1
  11.9 1.7 %add_bitcast_fusion.own_ref.merged_ref = f32[64,7168]{1,0:T(8,128)S(1)} fusion(f32[1,64,7168]{2,1,0:T(8,128)} %param.4, bf16[1,64,7168]{2,1,0:T(8,128)(2,1)S(1)} %copy-done.1), kind=kLoop, calls=%fused_computation | loop fusion | flops 917504 | bytes 4587520 | tf_op jit(solution)/shard_map/add | solution.py:234
  13.6 6.4 %collective-permute-start = (f32[64,7168]{1,0:T(8,128)S(1)}, f32[64,7168]{1,0:T(8,128)}, u32[]{:S(2)}, u32[]{:S(2)}) collective-permute-start(f32[64,7168]{1,0:T(8,128)S(1)} %add_bitcast_fusion.own_ref.merged_ref), channel_id=1, source_target_pairs={{0,16},{16,0},{1,17},{17,1},{2,18},{18,2},{3,19},{19,3},{4,20},{20... | collective-permute-start | bytes 5505032 | tf_op jit(solution)/shard_map/ppermute | solution.py:235
  20.0 0.0 all-to-all-done.q_ref
  20.0 0.1 shard_map.51.q_ref
  20.2 3.4 %collective-permute-done.other_ref = f32[64,7168]{1,0:T(8,128)} collective-permute-done((f32[64,7168]{1,0:T(8,128)S(1)}, f32[64,7168]{1,0:T(8,128)}, u32[]{:S(2)}, u32[]{:S(2)}) %collective-permute-start) | collective-permute-done | bytes 1835040 | tf_op jit(solution)/shard_map/ppermute | solution.py:235
  23.5 2.4 %shard_map.52 = (bf16[128,7168]{1,0:T(8,128)(2,1)S(1)}, f32[16,8,128]{2,1,0:T(8,128)S(1)}) custom-call(bf16[32,7168]{1,0:T(8,128)(2,1)S(1)} %shard_map.51.q_ref, f32[64,7168]{1,0:T(8,128)S(1)} %add_bitcast_fusion.own_ref.merged_ref, f32[64,7168]{1,0:T(8,128)} %collective-permute-done.other_ref), custom_call_target="tpu_custom_call" | custom-call | flops 58720256 | bytes 6029312 | tf_op jit(solution)/shard_map/pallas_call | solution.py:36
  26.0 17.8 %all_to_all.25.left_ref = f32[16,8,128]{2,1,0:T(8,128)S(1)} all-to-all(f32[16,8,128]{2,1,0:T(8,128)S(1)} %get-tuple-element.12), channel_id=1, replica_groups={{352,384,416,448,480,0,32,64,96,128,160,192,224,256,288,320},{353,385,4..., dimensions={0} | all-to-all | bytes 131072 | tf_op jit(solution)/shard_map/all_to_all | solution.py:31
  43.7 0.5 shard_map.53
  44.3 12.8 %all_to_all.26.got_ref = f32[32,4,1024]{2,1,0:T(4,128)S(1)} all-to-all(f32[32,4,1024]{2,1,0:T(4,128)S(1)} %get-tuple-element.14), channel_id=1, replica_groups={{10,1,2,3,4,5,6,7,8,9,0,11,12,13,14,15,32,33,34,35,36,37,38,39,40,41,42..., dimensions={0} | all-to-all | bytes 1048576 | tf_op jit(solution)/shard_map/all_to_all | solution.py:31
  57.1 0.7 shard_map.54
  57.8 10.4 %all-to-all-start.3 = ((f32[8,4,896]{2,1,0:T(4,128)}), f32[8,4,896]{2,1,0:T(4,128)S(1)}, u32[]{:S(2)}, u32[]{:S(2)}) async-start(f32[8,4,896]{2,1,0:T(4,128)} %get-tuple-element.15), calls=%async_computation.3 | async-start | bytes 229376 | tf_op jit(solution)/shard_map/all_to_all | solution.py:31
  68.2 4.7 %collective-permute-start.1 = (f32[16,1024]{1,0:T(8,128)S(1)}, f32[16,1024]{1,0:T(8,128)S(1)}, u32[]{:S(2)}, u32[]{:S(2)}) collective-permute-start(f32[16,1024]{1,0:T(8,128)S(1)} %get-tuple-element.16.own_ref), channel_id=1, source_target_pairs={{0,16},{16,0},{1,17},{17,1},{2,18},{18,2},{3,19},{19,3},{4,20},{20... | collective-permute-start | bytes 196616 | tf_op jit(solution)/shard_map/ppermute | solution.py:269
  72.9 0.9 collective-permute-done.1.other_ref
  73.8 2.0 %shard_map.55 = (bf16[64,96]{1,0:T(8,128)(2,1)S(1)}, f32[32,32]{1,0:T(8,128)S(1)}) custom-call(f32[16,1024]{1,0:T(8,128)S(1)} %get-tuple-element.16.own_ref, f32[16,1024]{1,0:T(8,128)S(1)} %collective-permute-done.1.other_ref, f32[16,64]{1,0:T(8,128)S(1)} %get-tuple-element.17.mine_ref), custom_call_target="tpu_custom_call" | custom-call | flops 10000000 | bytes 151552 | tf_op jit(solution)/shard_map/pallas_call | solution.py:36
  75.9 0.0 all-to-all-done.3.got_ref
  75.9 13.4 %all_to_all.27 = f32[32,4,896]{2,1,0:T(4,128)S(1)} all-to-all(f32[32,4,896]{2,1,0:T(4,128)S(1)} %shard_map.56), channel_id=1, replica_groups={{10,1,2,3,4,5,6,7,8,9,0,11,12,13,14,15,32,33,34,35,36,37,38,39,40,41,42..., dimensions={0} | all-to-all | bytes 917504 | tf_op jit(solution)/shard_map/all_to_all | solution.py:31
  89.3 4.4 %all-gather = f32[64,4,896]{2,1,0:T(4,128)S(1)} all-gather(f32[32,4,896]{2,1,0:T(4,128)S(1)} %all_to_all.27), channel_id=2, replica_groups=mesh['z8'=8,'z0'=2,'core'=2,'shard'=16] {'core'}, dimensions={0}, use_global_device_ids=true | all-gather | bytes 1376256 | tf_op jit(solution)/shard_map/all_gather | solution.py:283
  93.7 1.6 %shard_map.57 = (f32[64,7168]{1,0:T(8,128)}, f32[32,448]{1,0:T(8,128)}) custom-call(f32[2,32,4,896]{3,2,1,0:T(4,128)S(1)} %bitcast.6, bf16[64,96]{1,0:T(8,128)(2,1)S(1)} %get-tuple-element.18.weights_ref, f32[32,32]{1,0:T(8,128)S(1)} %get-tuple-element.19.inverse_ref, f32[64,7168]{1,0:T(8,128)S(1)} %add_bitcast_fusion.own_ref.merged_ref), custom_call_target="tpu_custom_call" | custom-call | flops 88080384 | bytes 4661248 | tf_op jit(solution)/shard_map/pallas_call | solution.py:36
  (1 shorter events, 0.0 us)
Async XLA Ops:
  0.6 0.8 copy-start
  1.5 10.5 %copy-start.1 = (bf16[1,64,7168]{2,1,0:T(8,128)(2,1)S(1)}, bf16[1,64,7168]{2,1,0:T(8,128)(2,1)}, u32[]{:S(2)}) copy-start(bf16[1,64,7168]{2,1,0:T(8,128)(2,1)} %param.3) | copy-start | bytes 2752516
  2.3 17.7 %all-to-all-start = ((f32[16,8,896]{2,1,0:T(8,128)}), f32[16,8,896]{2,1,0:T(8,128)S(1)}, u32[]{:S(2)}, u32[]{:S(2)}) async-start(f32[16,8,896]{2,1,0:T(8,128)} %shard_map.50), calls=%async_computation | async-start | bytes 917504 | tf_op jit(solution)/shard_map/all_to_all | solution.py:31
  13.6 9.9 %collective-permute-start = (f32[64,7168]{1,0:T(8,128)S(1)}, f32[64,7168]{1,0:T(8,128)}, u32[]{:S(2)}, u32[]{:S(2)}) collective-permute-start(f32[64,7168]{1,0:T(8,128)S(1)} %add_bitcast_fusion.own_ref.merged_ref), channel_id=1, source_target_pairs={{0,16},{16,0},{1,17},{17,1},{2,18},{18,2},{3,19},{19,3},{4,20},{20... | collective-permute-start | bytes 5505032 | tf_op jit(solution)/shard_map/ppermute | solution.py:235
  57.8 18.0 %all-to-all-start.3 = ((f32[8,4,896]{2,1,0:T(4,128)}), f32[8,4,896]{2,1,0:T(4,128)S(1)}, u32[]{:S(2)}, u32[]{:S(2)}) async-start(f32[8,4,896]{2,1,0:T(4,128)} %get-tuple-element.15), calls=%async_computation.3 | async-start | bytes 229376 | tf_op jit(solution)/shard_map/all_to_all | solution.py:31
  68.2 5.6 %collective-permute-start.1 = (f32[16,1024]{1,0:T(8,128)S(1)}, f32[16,1024]{1,0:T(8,128)S(1)}, u32[]{:S(2)}, u32[]{:S(2)}) collective-permute-start(f32[16,1024]{1,0:T(8,128)S(1)} %get-tuple-element.16.own_ref), channel_id=1, source_target_pairs={{0,16},{16,0},{1,17},{17,1},{2,18},{18,2},{3,19},{19,3},{4,20},{20... | collective-permute-start | bytes 196616 | tf_op jit(solution)/shard_map/ppermute | solution.py:269

commit v9 on v8

--- a/solution.py
+++ b/solution.py
@@ -19,16 +19,20 @@
 
 ASKED = 10
 FIRST = 10
-START = 11
-TURN = 5
+LEFT_Z = [11, 10, 12, 9, 13, 8, 14, 7, 15, 6, 0, 5, 1, 4, 2, 3]
+RIGHT_Z = [10, 12, 14, 0, 2, 4, 6, 8]
 
 
 def place_of(peer, first=FIRST):
-    return first if peer == 0 else 0 if peer == first else peer
-
-
-def exchange(blocks, axis, order):
-    return lax.all_to_all(blocks, axis, 0, 0, axis_index_groups=[list(order)])
+    return 0 if peer == first else peer + (peer < first)
+
+
+def order_of(peers, first=FIRST):
+    return sorted(range(peers), key=lambda peer: place_of(peer, first))
+
+
+def exchange(blocks, axis, *orders):
+    return lax.all_to_all(blocks, axis, 0, 0, axis_index_groups=[list(order) for order in orders])
 
 
 def call(body, out, operands, specs, scratch=(), out_specs=None, flops=0, limit=24):
@@ -200,7 +204,7 @@
     step = raw_ref.shape[-1]
     gather = lambda peers: jnp.concatenate([raw_ref[core, peer] for core in range(2) for peer in peers], axis=0)
     peers = [here // 2 * 2 + 16 * z + k for z in range(2) for k in range(2)]
-    raw = gather([jnp.where(peer == 0, FIRST, jnp.where(peer == FIRST, 0, peer)) for peer in peers])
+    raw = gather([jnp.where(peer == FIRST, 0, peer + (peer < FIRST).astype(jnp.int32)) for peer in peers])
     raw = jnp.where(here % 2 == 0, raw[:, : step // 2], raw[:, step // 2 :])
     q_buf[...] = dot(inverse_ref[...], raw, ((1,), (0,)), HIGH)
     copies = [pltpu.make_async_copy(q_buf, q_ref, sem.at[width // step])]
@@ -230,7 +234,7 @@
         [q_prev.T],
         [VMEM],
     )
-    all_q = exchange(own_q, "shard", (place_of(s, ASKED) for s in range(16)))
+    all_q = exchange(own_q, "shard", order_of(16, ASKED))
     merged = grads[0].astype(F32) + errors[0]
     other = lax.ppermute(merged, "core", SWAP)
     (all_q,) = call(
@@ -248,7 +252,7 @@
         [pltpu.VMEM((rows, width), F32), pltpu.SemaphoreType.DMA((CUTS,))],
         flops=2 * 32 * 128 * width,
     )
-    left = exchange(left, ("z8", "z0"), ((z + START) % 16 for z in range(16)))
+    left = exchange(left, ("z8", "z0"), LEFT_Z)
 
     pieces, mine = call(
         functools.partial(right_kernel, replicas),
@@ -257,14 +261,14 @@
         [VMEM, VMEM],
         flops=2 * 32 * 128 * width,
     )
-    pieces = exchange(pieces, PLANE, map(place_of, range(32)))
+    pieces = exchange(pieces, PLANE, order_of(32))
     right, left_own = call(
         scatter_kernel,
         [shape((8, half // 4, 2 * share), F32), shape((half, 16 * rows), F32)],
         [pieces],
         [VMEM],
     )
-    right = exchange(right, "z8", ((z + TURN) % 8 for z in range(8)))
+    right = exchange(right, "z8", [z // 2 for z in RIGHT_Z])
 
     left_other = lax.ppermute(left_own, "core", SWAP)
     weights, inverse = call(
@@ -279,7 +283,7 @@
     (raw,) = call(
         spread_kernel, [shape((32, half // 4, 2 * share), F32)], [right, weights, inverse], [VMEM] * 3
     )
-    raw = exchange(raw, PLANE, map(place_of, range(32)))
+    raw = exchange(raw, PLANE, order_of(32))
     raw = lax.all_gather(raw, "core")
     out, q_new = call(
         final_kernel,

time: 95.8 us -> 95.7 us (level)
  no operation moved by 1% of the time
where the time goes in v9:
time: 95.7 us; the launch traced here: 95.1 us
  blocking collectives  48.3 us (50%)
  starting transfers between devices  31.1 us (32%)
  Pallas kernels  8.33 us (9%)
  waiting for transfers between devices  4.25 us (4%)
  other arithmetic  1.66 us (2%)
    all_to_all x3, blocking collectives, exchange(): lax.all_to_all(blocks, axis, 0, 0, axis_index_groups=[list(order) for ord...  43.6 us
    all_to_all x2, starting transfers between devices, exchange(): lax.all_to_all(blocks, axis, 0, 0, axis_index_groups=[list(order) for ord...  19.6 us
    pallas_call x8, Pallas kernels, call(): pl.pallas_call(body, out_shape=out, in_specs=specs, out_specs=out_specs o...  8.33 us
    ppermute x1, starting transfers between devices, per_device(): other = lax.ppermute(merged, 'core', SWAP)  6.45 us
    ppermute x1, starting transfers between devices, per_device(): left_other = lax.ppermute(left_own, 'core', SWAP)  4.98 us
    all_gather x1, blocking collectives, per_device(): raw = lax.all_gather(raw, 'core')  4.63 us
    ppermute x1, waiting for transfers between devices, per_device(): other = lax.ppermute(merged, 'core', SWAP)  3.37 us
  transfers between devices with their start and end apart: 4, of which 2 were waited for; matrix products, arithmetic and copies ran while one was open for 2% of the time, Pallas kernels for 2%

profile of v9, /device:TPU:1, one launch (start us, length us, event | category | flops | bytes accessed | tf_op | source)
XLA Modules:
  0.0 95.1 jit_solution(1297528093587123149)
XLA Ops:
  0.6 0.0 copy-start
  0.6 0.8 copy-done
  1.5 0.0 copy-start.1
  1.5 0.9 shard_map.50
  2.3 9.6 %all-to-all-start = ((f32[16,8,896]{2,1,0:T(8,128)}), f32[16,8,896]{2,1,0:T(8,128)S(1)}, u32[]{:S(2)}, u32[]{:S(2)}) async-start(f32[16,8,896]{2,1,0:T(8,128)} %shard_map.50), calls=%async_computation | async-start | bytes 917504 | tf_op jit(solution)/shard_map/all_to_all | solution.py:35
  11.9 0.0 copy-done.1
  11.9 1.7 %add_bitcast_fusion.own_ref.merged_ref = f32[64,7168]{1,0:T(8,128)S(1)} fusion(f32[1,64,7168]{2,1,0:T(8,128)} %param.4, bf16[1,64,7168]{2,1,0:T(8,128)(2,1)S(1)} %copy-done.1), kind=kLoop, calls=%fused_computation | loop fusion | flops 917504 | bytes 4587520 | tf_op jit(solution)/shard_map/add | solution.py:238
  13.5 6.5 %collective-permute-start = (f32[64,7168]{1,0:T(8,128)S(1)}, f32[64,7168]{1,0:T(8,128)}, u32[]{:S(2)}, u32[]{:S(2)}) collective-permute-start(f32[64,7168]{1,0:T(8,128)S(1)} %add_bitcast_fusion.own_ref.merged_ref), channel_id=1, source_target_pairs={{0,16},{16,0},{1,17},{17,1},{2,18},{18,2},{3,19},{19,3},{4,20},{20... | collective-permute-start | bytes 5505032 | tf_op jit(solution)/shard_map/ppermute | solution.py:239
  20.0 0.0 all-to-all-done.q_ref
  20.0 0.1 shard_map.51.q_ref
  20.2 3.4 %collective-permute-done.other_ref = f32[64,7168]{1,0:T(8,128)} collective-permute-done((f32[64,7168]{1,0:T(8,128)S(1)}, f32[64,7168]{1,0:T(8,128)}, u32[]{:S(2)}, u32[]{:S(2)}) %collective-permute-start) | collective-permute-done | bytes 1835040 | tf_op jit(solution)/shard_map/ppermute | solution.py:239
  23.5 2.4 %shard_map.52 = (bf16[128,7168]{1,0:T(8,128)(2,1)S(1)}, f32[16,8,128]{2,1,0:T(8,128)S(1)}) custom-call(bf16[32,7168]{1,0:T(8,128)(2,1)S(1)} %shard_map.51.q_ref, f32[64,7168]{1,0:T(8,128)S(1)} %add_bitcast_fusion.own_ref.merged_ref, f32[64,7168]{1,0:T(8,128)} %collective-permute-done.other_ref), custom_call_target="tpu_custom_call" | custom-call | flops 58720256 | bytes 6029312 | tf_op jit(solution)/shard_map/pallas_call | solution.py:40
  25.9 17.9 %all_to_all.25.left_ref = f32[16,8,128]{2,1,0:T(8,128)S(1)} all-to-all(f32[16,8,128]{2,1,0:T(8,128)S(1)} %get-tuple-element.12), channel_id=1, replica_groups={{352,320,384,288,416,256,448,224,480,192,0,160,32,128,64,96},{353,321,3..., dimensions={0} | all-to-all | bytes 131072 | tf_op jit(solution)/shard_map/all_to_all | solution.py:35
  43.9 0.5 shard_map.53
  44.4 12.6 %all_to_all.26.got_ref = f32[32,4,1024]{2,1,0:T(4,128)S(1)} all-to-all(f32[32,4,1024]{2,1,0:T(4,128)S(1)} %get-tuple-element.14), channel_id=1, replica_groups={{10,0,1,2,3,4,5,6,7,8,9,11,12,13,14,15,32,33,34,35,36,37,38,39,40,41,42..., dimensions={0} | all-to-all | bytes 1048576 | tf_op jit(solution)/shard_map/all_to_all | solution.py:35
  57.0 0.7 shard_map.54
  57.7 10.1 %all-to-all-start.3 = ((f32[8,4,896]{2,1,0:T(4,128)}), f32[8,4,896]{2,1,0:T(4,128)S(1)}, u32[]{:S(2)}, u32[]{:S(2)}) async-start(f32[8,4,896]{2,1,0:T(4,128)} %get-tuple-element.15), calls=%async_computation.3 | async-start | bytes 229376 | tf_op jit(solution)/shard_map/all_to_all | solution.py:35
  67.8 5.0 %collective-permute-start.1 = (f32[16,1024]{1,0:T(8,128)S(1)}, f32[16,1024]{1,0:T(8,128)S(1)}, u32[]{:S(2)}, u32[]{:S(2)}) collective-permute-start(f32[16,1024]{1,0:T(8,128)S(1)} %get-tuple-element.16.own_ref), channel_id=1, source_target_pairs={{0,16},{16,0},{1,17},{17,1},{2,18},{18,2},{3,19},{19,3},{4,20},{20... | collective-permute-start | bytes 196616 | tf_op jit(solution)/shard_map/ppermute | solution.py:273
  72.8 0.9 collective-permute-done.1.other_ref
  73.6 2.0 %shard_map.55 = (bf16[64,96]{1,0:T(8,128)(2,1)S(1)}, f32[32,32]{1,0:T(8,128)S(1)}) custom-call(f32[16,1024]{1,0:T(8,128)S(1)} %get-tuple-element.16.own_ref, f32[16,1024]{1,0:T(8,128)S(1)} %collective-permute-done.1.other_ref, f32[16,64]{1,0:T(8,128)S(1)} %get-tuple-element.17.mine_ref), custom_call_target="tpu_custom_call" | custom-call | flops 10000000 | bytes 151552 | tf_op jit(solution)/shard_map/pallas_call | solution.py:40
  75.7 0.0 all-to-all-done.3.got_ref
  75.7 13.2 %all_to_all.27 = f32[32,4,896]{2,1,0:T(4,128)S(1)} all-to-all(f32[32,4,896]{2,1,0:T(4,128)S(1)} %shard_map.56), channel_id=1, replica_groups={{10,0,1,2,3,4,5,6,7,8,9,11,12,13,14,15,32,33,34,35,36,37,38,39,40,41,42..., dimensions={0} | all-to-all | bytes 917504 | tf_op jit(solution)/shard_map/all_to_all | solution.py:35
  88.9 4.6 %all-gather = f32[64,4,896]{2,1,0:T(4,128)S(1)} all-gather(f32[32,4,896]{2,1,0:T(4,128)S(1)} %all_to_all.27), channel_id=2, replica_groups=mesh['z8'=8,'z0'=2,'core'=2,'shard'=16] {'core'}, dimensions={0}, use_global_device_ids=true | all-gather | bytes 1376256 | tf_op jit(solution)/shard_map/all_gather | solution.py:287
  93.5 1.6 %shard_map.57 = (f32[64,7168]{1,0:T(8,128)}, f32[32,448]{1,0:T(8,128)}) custom-call(f32[2,32,4,896]{3,2,1,0:T(4,128)S(1)} %bitcast.6, bf16[64,96]{1,0:T(8,128)(2,1)S(1)} %get-tuple-element.18.weights_ref, f32[32,32]{1,0:T(8,128)S(1)} %get-tuple-element.19.inverse_ref, f32[64,7168]{1,0:T(8,128)S(1)} %add_bitcast_fusion.own_ref.merged_ref), custom_call_target="tpu_custom_call" | custom-call | flops 88080384 | bytes 4661248 | tf_op jit(solution)/shard_map/pallas_call | solution.py:40
  (1 shorter events, 0.0 us)
Async XLA Ops:
  0.6 0.8 copy-start
  1.5 10.4 %copy-start.1 = (bf16[1,64,7168]{2,1,0:T(8,128)(2,1)S(1)}, bf16[1,64,7168]{2,1,0:T(8,128)(2,1)}, u32[]{:S(2)}) copy-start(bf16[1,64,7168]{2,1,0:T(8,128)(2,1)} %param.3) | copy-start | bytes 2752516
  2.3 17.7 %all-to-all-start = ((f32[16,8,896]{2,1,0:T(8,128)}), f32[16,8,896]{2,1,0:T(8,128)S(1)}, u32[]{:S(2)}, u32[]{:S(2)}) async-start(f32[16,8,896]{2,1,0:T(8,128)} %shard_map.50), calls=%async_computation | async-start | bytes 917504 | tf_op jit(solution)/shard_map/all_to_all | solution.py:35
  13.5 10.0 %collective-permute-start = (f32[64,7168]{1,0:T(8,128)S(1)}, f32[64,7168]{1,0:T(8,128)}, u32[]{:S(2)}, u32[]{:S(2)}) collective-permute-start(f32[64,7168]{1,0:T(8,128)S(1)} %add_bitcast_fusion.own_ref.merged_ref), channel_id=1, source_target_pairs={{0,16},{16,0},{1,17},{17,1},{2,18},{18,2},{3,19},{19,3},{4,20},{20... | collective-permute-start | bytes 5505032 | tf_op jit(solution)/shard_map/ppermute | solution.py:239
  57.7 18.0 %all-to-all-start.3 = ((f32[8,4,896]{2,1,0:T(4,128)}), f32[8,4,896]{2,1,0:T(4,128)S(1)}, u32[]{:S(2)}, u32[]{:S(2)}) async-start(f32[8,4,896]{2,1,0:T(4,128)} %get-tuple-element.15), calls=%async_computation.3 | async-start | bytes 229376 | tf_op jit(solution)/shard_map/all_to_all | solution.py:35
  67.8 5.9 %collective-permute-start.1 = (f32[16,1024]{1,0:T(8,128)S(1)}, f32[16,1024]{1,0:T(8,128)S(1)}, u32[]{:S(2)}, u32[]{:S(2)}) collective-permute-start(f32[16,1024]{1,0:T(8,128)S(1)} %get-tuple-element.16.own_ref), channel_id=1, source_target_pairs={{0,16},{16,0},{1,17},{17,1},{2,18},{18,2},{3,19},{19,3},{4,20},{20... | collective-permute-start | bytes 196616 | tf_op jit(solution)/shard_map/ppermute | solution.py:273
